TPU v7x, 128 devices: a whole 4x4x4 slice. The times are simulated.
128 devices in a mesh: row: 16 (over z, x_lo, core), col: 8 (over y, x_hi).
Axes of the slice: x: 4 (x_hi: 2, x_lo: 2; x = x_hi * 2 + x_lo), y: 4, z: 4, core: 2. Of those that a mesh axis runs over, the one named last changes fastest.
Arguments:
- trials: float32 [2, 512, 1024], P(None, 'col', 'row'), may hold values from -6 to 6
- valence_orb: float32 [512, 8192], P('col', 'row'), may hold values from -0.25 to 0.25
- conduction_orb: float32 [1024, 8192], P('row', 'col'), may hold values from -0.1875 to 0.1875
- screened: float32 [8192, 8192], P('row', 'col'), may hold values from -0.5 to 0.5
Outputs:
- applied: float32 [2, 512, 1024], P(None, 'col', 'row')
All inputs are finite; a program needn't handle non-finite values.
Results may differ from a plain program's by a relative error of at most 0.0003.
Values sent between devices are 32-bit elements; how exact they have to be, the bound alone decides.
No kernel may reach another device: no remote copies, remote signals or barrier semaphores. Data moves between devices by JAX's collectives and lax.ppermute only.
A program may use at most 64 MiB of HBM per device.

v0:
```python
import jax
import jax.numpy as jnp
from jax import lax
from jax.sharding import PartitionSpec as P


def body(trials, valence_orb, conduction_orb, screened):
    highest = lax.Precision.HIGHEST
    valence_all = lax.all_gather(valence_orb, "col", axis=0, tiled=True)
    trials_all = lax.all_gather(trials, "col", axis=1, tiled=True)
    partial_value = jnp.einsum(
        "tvc,cn->tvn",
        trials_all,
        conduction_orb,
        precision=highest,
        preferred_element_type=jnp.float32,
    )
    summed = lax.psum(partial_value, "row")
    encoded = jnp.einsum(
        "vm,tvn->tmn", valence_all, summed, precision=highest, preferred_element_type=jnp.float32
    )
    screened_pairs = screened[None, :, :] * encoded
    point_sums = lax.psum_scatter(
        jnp.einsum(
            "vm,tmn->ntv",
            valence_all,
            screened_pairs,
            precision=highest,
            preferred_element_type=jnp.float32,
        ),
        "row",
        scatter_dimension=0,
        tiled=True,
    )
    conduction_here = lax.all_to_all(conduction_orb, "row", split_axis=1, concat_axis=0, tiled=True)
    result = jnp.einsum(
        "ntv,cn->tvc",
        point_sums,
        conduction_here,
        precision=highest,
        preferred_element_type=jnp.float32,
    )
    reduced = lax.psum_scatter(result, "row", scatter_dimension=2, tiled=True)
    return lax.psum_scatter(reduced, "col", scatter_dimension=1, tiled=True)


def solution(mesh):
    placed = (P(None, "col", "row"), P("col", "row"), P("row", "col"), P("row", "col"))
    return jax.shard_map(
        body, mesh=mesh, in_specs=placed, out_specs=P(None, "col", "row"), check_vma=False
    )
```

profile of v0, /device:TPU:1, one launch (start us, length us, event | category | flops | bytes accessed | tf_op | source)
XLA Modules:
  0.0 435.9 jit_solution(14079766958786000136)
XLA Ops:
  7.4 0.0 all-gather.2.cloned.1.call-start
  7.4 0.7 all-gather.2.cloned.1.call-update
  8.1 0.0 all-reduce.2.cloned.1.call-start
  8.1 32.1 %all_gather.6 = f32[2,512,64]{2,1,0:T(8,128)S(1)} all-gather(f32[2,64,64]{2,1,0:T(8,128)} %param.4), channel_id=1, replica_groups=mesh['row'=16,'col'=8] {'col'}, dimensions={1}, use_global_device_ids=true | all-gather | bytes 294912 | tf_op jit(solution)/shard_map/all_gather | solution.py:10
  40.2 5.8 %fusion.6 = f32[2,512,1024]{2,1,0:T(8,128)} fusion(f32[2,512,64]{2,1,0:T(8,128)S(1)} %all_gather.6, f32[64,1024]{1,0:T(8,128)} %param.6), kind=kOutput, calls=%fused_computation.7 | convolution fusion | flops 805306368 | bytes 4718592 | tf_op jit(solution)/shard_map/tvc,cn->tvn/dot_general | solution.py:11
  46.1 0.0 all-reduce.2.cloned.1.call-update
  46.1 0.0 copy-start
  46.1 0.0 reduce-scatter.6.cloned.1.call-start
  46.1 12.7 %all-gather.2.cloned.1.call-done = f32[512,512]{1,0:T(8,128)} async-done(((f32[64,512]{1,0:T(8,128)}), f32[512,512]{1,0:T(8,128)}) %all-gather.2.cloned.1.call-update) | async-done | bytes 1048592 | tf_op jit(solution)/shard_map/all_gather | solution.py:9
  58.8 0.0 copy-start.1
  58.8 129.4 %all-reduce.2.cloned.1.call-done = f32[2,512,1024]{2,1,0:T(8,128)} async-done(((f32[2,512,1024]{2,1,0:T(8,128)}), f32[2,512,1024]{2,1,0:T(8,128)}) %all-reduce.2.cloned.1.call-update) | async-done | bytes 4194320 | tf_op jit(solution)/shard_map/psum | solution.py:18
  188.2 9.2 %fusion.4 = f32[2,1024,512]{1,2,0:T(8,128)S(1)} fusion(f32[2,512,1024]{2,1,0:T(8,128)} %all-reduce.2.cloned.1.call-done, f32[512,512]{1,0:T(8,128)} %all-gather.2.cloned.1.call-done), kind=kOutput, calls=%fused_computation.5 | convolution fusion | flops 6442450944 | bytes 9437184 | tf_op jit(solution)/shard_map/vm,tvn->tmn/dot_general | solution.py:19
  197.4 0.0 copy-done
  197.4 0.0 copy-done.1
  197.4 14.8 %fusion.1 = f32[1024,2,512]{2,0,1:T(8,128)} fusion(f32[2,1024,512]{1,2,0:T(8,128)S(1)} %fusion.4, f32[512,1024]{1,0:T(8,128)S(1)} %copy-done, f32[512,512]{1,0:T(8,128)S(1)} %copy-done.1), kind=kOutput, calls=%fused_computation.2 | convolution fusion | flops 6443499520 | bytes 11534336 | tf_op jit(solution)/shard_map/vm,tmn->ntv/dot_general | solution.py:24
  212.2 0.0 copy-start.2
  212.2 0.0 reduce-scatter.6.cloned.1.call-update
  212.2 0.0 reduce-scatter.8.cloned.1.call-start
  212.3 0.9 copy-done.2
  213.1 0.2 copy.7
  213.3 0.3 reshape.10
  213.7 13.4 %all_to_all.19 = f32[16,1,4096]{2,1,0:T(1,128)S(1)} all-to-all(f32[16,1,4096]{2,1,0:T(1,128)S(1)} %reshape.10), channel_id=1, replica_groups=mesh['row'=16,'col'=8] {'row'}, dimensions={0} | all-to-all | bytes 524288 | tf_op jit(solution)/shard_map/all_to_all | solution.py:35
  227.0 0.5 broadcast.1
  227.5 1.3 reduce
  228.8 0.2 reshape.11
  229.1 0.3 copy.8
  229.4 0.2 reshape.6
  229.6 51.8 %reduce-scatter.6.cloned.1.call-done = f32[64,2,512]{2,0,1:T(8,128)} async-done(((f32[1024,2,512]{2,0,1:T(8,128)}), f32[64,2,512]{2,0,1:T(8,128)}) %reduce-scatter.6.cloned.1.call-update) | async-done | bytes 262160 | tf_op jit(solution)/shard_map/reduce_scatter | solution.py:23
  281.4 5.9 %fusion.8 = f32[2,512,1024]{1,2,0:T(8,128)} fusion(f32[64,2,512]{2,0,1:T(8,128)} %reduce-scatter.6.cloned.1.call-done, f32[1024,64,1]{0,1,2:T(8,128)S(1)} %reshape.6), kind=kOutput, calls=%fused_computation.10 | convolution fusion | flops 805306368 | bytes 4718592 | tf_op jit(solution)/shard_map/ntv,cn->tvc/dot_general | solution.py:36
  287.3 0.0 reduce-scatter.8.cloned.1.call-update
  287.3 0.0 reduce-scatter.10.cloned.1.call-start
  287.4 68.2 %reduce-scatter.8.cloned.1.call-done = f32[2,512,64]{1,2,0:T(8,128)} async-done(((f32[2,512,1024]{1,2,0:T(8,128)}), f32[2,512,64]{1,2,0:T(8,128)}) %reduce-scatter.8.cloned.1.call-update) | async-done | bytes 262160 | tf_op jit(solution)/shard_map/reduce_scatter | solution.py:43
  355.5 1.2 copy.10
  356.7 1.0 reshape.8
  357.7 0.0 reduce-scatter.10.cloned.1.call-update
  357.7 69.1 %reduce-scatter.10.cloned.1.call-done = f32[64,128]{1,0:T(8,128)} async-done(((f32[512,128]{1,0:T(8,128)}), f32[64,128]{1,0:T(8,128)}) %reduce-scatter.10.cloned.1.call-update) | async-done | bytes 32784
  426.8 0.9 reshape.9
  427.7 0.6 copy.9
  (1 shorter events, 0.0 us)
Async XLA Ops:
  7.4 51.5 %all-gather.2.cloned.1.call-start = ((), (), s32[]{:S(2)}) async-start(), calls=%async_computation.5 | async-start | bytes 1179648 | tf_op jit(solution)/shard_map/all_gather | solution.py:9
  8.1 180.1 %all-reduce.2.cloned.1.call-start = ((), (), s32[]{:S(2)}) async-start(), calls=%async_computation.4 | async-start | bytes 8388608 | tf_op jit(solution)/shard_map/psum | solution.py:18
  46.1 151.3 %copy-start = (f32[512,1024]{1,0:T(8,128)S(1)}, f32[512,1024]{1,0:T(8,128)}, u32[]{:S(2)}) copy-start(f32[512,1024]{1,0:T(8,128)} %param.7) | copy-start | bytes 6291460
  46.1 235.3 %reduce-scatter.6.cloned.1.call-start = ((), (), s32[]{:S(2)}) async-start(), calls=%async_computation.6 | async-start | bytes 4456448 | tf_op jit(solution)/shard_map/reduce_scatter | solution.py:23
  58.8 138.6 %copy-start.1 = (f32[512,512]{1,0:T(8,128)S(1)}, f32[512,512]{1,0:T(8,128)}, u32[]{:S(2)}) copy-start(f32[512,512]{1,0:T(8,128)} %all-gather.2.cloned.1.call-done) | copy-start | bytes 3145732
  212.2 0.9 copy-start.2
  212.2 143.3 %reduce-scatter.8.cloned.1.call-start = ((), (), s32[]{:S(2)}) async-start(), calls=%async_computation.7 | async-start | bytes 4456448 | tf_op jit(solution)/shard_map/reduce_scatter | solution.py:43
  287.3 139.5 %reduce-scatter.10.cloned.1.call-start = ((), (), s32[]{:S(2)}) async-start(), calls=%async_computation.8 | async-start | bytes 294912
Sparse Core Ops, SparseCore 0:
  10.5 48.2 all-gather.1
  357.9 68.9 reduce-scatter.9
Sparse Core Ops, SparseCore 1:
  46.2 142.0 all-reduce.1
  212.3 69.0 reduce-scatter.5
  287.4 68.1 reduce-scatter.7
where the time goes:
time: 437 us; the launch traced here: 436 us
  waiting for transfers between devices  332 us (76%)
  blocking collectives  45.4 us (10%)
  matrix products  35.7 us (8%)
  between operations  15.1 us (3%)
  local copies, waits for them, and re-layouts  6.33 us (1%)
    psum x1, waiting for transfers between devices, body(): summed = lax.psum(partial_value, 'row')  129 us
    unnamed x6, waiting for transfers between devices  69.8 us
    reduce_scatter x1, waiting for transfers between devices, body(): reduced = lax.psum_scatter(result, 'row', scatter_dimension=2, tiled=True)  68.2 us
    reduce_scatter x1, waiting for transfers between devices, body(): lax.psum_scatter(jnp.einsum('vm,tmn->ntv', valence_all, screened_pairs, p...  51.8 us
    all_gather x1, blocking collectives, body(): trials_all = lax.all_gather(trials, 'col', axis=1, tiled=True)  32.1 us
    dot_general x1, matrix products, body(): jnp.einsum('vm,tmn->ntv', valence_all, screened_pairs, precision=highest,...  14.8 us
    all_to_all x1, blocking collectives, body(): lax.all_to_all(conduction_orb, 'row', split_axis=1, concat_axis=0, tiled=...  13.4 us
    all_gather x1, waiting for transfers between devices, body(): valence_all = lax.all_gather(valence_orb, 'col', axis=0, tiled=True)  12.7 us
  transfers between devices with their start and end apart: 5, of which 5 were waited for; matrix products, arithmetic and copies ran while one was open for 2% of the time, Pallas kernels for 0%

commit v1 on v0

v1 whole, which is shorter than its diff:
```python
import jax
import jax.numpy as jnp
from jax import lax
from jax.sharding import Mesh, PartitionSpec as P

AXES = ("z", "xl", "core", "y", "xh")
HIGH = lax.Precision.HIGH


def index(z, x, core, y):
    return (((z * 2 + x % 2) * 2 + core) * 4 + y) * 2 + x // 2


def flip(value, per_core):
    pairs = []
    for z in range(4):
        for x in range(4):
            for core in range(2):
                for y in range(4):
                    if per_core == "core":
                        target = index(z, x, 1 - core, y)
                    else:
                        dz, dx, dy = per_core[core]
                        target = index(z ^ dz, x ^ dx, core, y ^ dy)
                    pairs.append((index(z, x, core, y), target))
    return lax.ppermute(value, AXES, pairs)


Z1, Z3, X1, X2, Y1, Y3 = (1, 0, 0), (3, 0, 0), (0, 1, 0), (0, 2, 0), (0, 0, 1), (0, 0, 3)
ZA, ZB, YA, YB, XL, XH = (Z1, Z3), (Z3, Z1), (Y1, Y3), (Y3, Y1), (X1, X1), (X2, X2)


def grow(value, step, axis):
    return jnp.concatenate([value, flip(value, step)], axis=axis)


def swap_bits(value):
    shape = value.shape
    return value.reshape((2, 2, 2, shape[0] // 8) + shape[1:]).swapaxes(0, 1).reshape(shape)


def halve(value, step, axis):
    size = value.shape[axis] // 2
    kept = lax.slice_in_dim(value, 0, size, axis=axis)
    sent = lax.slice_in_dim(value, size, 2 * size, axis=axis)
    return kept + flip(sent, step)


def dot(spec, a, b):
    return jnp.einsum(spec, a, b, precision=HIGH, preferred_element_type=jnp.float32)


def body(trials, valence, conduction, screened):
    core = lax.axis_index("core")
    mine = lax.dynamic_index_in_dim(trials, core, 0, keepdims=False)
    theirs = lax.dynamic_index_in_dim(trials, 1 - core, 0, keepdims=False)
    trial = jnp.concatenate([mine, flip(theirs, "core")], axis=1)

    c = conduction
    for step in (XL, ZA, ZB):
        c = grow(c, step, 0)
    c_other = swap_bits(flip(c, "core"))
    c_all = jnp.stack([c.reshape(8, 64, -1), c_other.reshape(8, 64, -1)], axis=1).reshape(1024, -1)

    for step in (XL, ZA, ZB):
        trial = grow(trial, step, 1)
    for step in (XH, YA, YB):
        trial = grow(trial, step, 0)

    v = valence
    for step in (XH, YA, YB):
        v = grow(v, step, 0)
    v_other = swap_bits(v)

    half_mine = dot("vc,cn->vn", trial, c_all)
    half_theirs = flip(half_mine, "core")
    pairs_mine = screened * dot("vm,vn->mn", v, half_mine)
    pairs_theirs = screened * dot("vm,vn->mn", v_other, half_theirs)
    sums_theirs = dot("vm,mn->vn", v_other, pairs_theirs)
    sums_mine = dot("vm,mn->vn", v, pairs_mine) + flip(sums_theirs, "core")
    r = dot("vn,cn->vc", sums_mine, c_all)
    for step, axis in ((YB, 0), (ZB, 1), (YA, 0), (ZA, 1), (XH, 0), (XL, 1)):
        r = halve(r, step, axis)
    kept = r[:, :64]
    got = flip(r[:, 64:], "core")
    first = core == 0
    return jnp.stack([jnp.where(first, kept, got), jnp.where(first, got, kept)])


def solution(mesh):
    split = Mesh(mesh.devices.reshape(4, 2, 2, 4, 2), AXES)
    row, col = ("z", "xl", "core"), ("y", "xh")
    placed = (P(None, col, row), P(col, row), P(row, col), P(row, col))
    return jax.shard_map(
        body, mesh=split, in_specs=placed, out_specs=P(None, col, row), check_vma=False
    )
```

time: 437 us -> 172 us (0.39)
  waiting for transfers between devices: 332 us -> 94.8 us
  starting transfers between devices: 0.18 us -> 52.3 us
  blocking collectives: 45.4 us -> 0 us
  matrix products: 35.7 us -> 14.8 us
  between operations: 15.1 us -> 0.33 us
    psum x1 -> x0, waiting for transfers between devices: 129 us -> none  [body(): summed = lax.psum(partial_value, 'row')]
    reduce_scatter x2 -> x0, waiting for transfers between devices: 120 us -> none  [the longest x1 68.2 us: body(): reduced = lax.psum_scatter(result, 'row', scatter_dimension=2, tiled=True)]
    ppermute x0 -> x23, waiting for transfers between devices: none -> 94.8 us  [flip(): return lax.ppermute(value, AXES, pairs)]
    unnamed x6 -> x0, waiting for transfers between devices: 69.8 us -> none
    ppermute x0 -> x23, starting transfers between devices: none -> 52.3 us  [flip(): return lax.ppermute(value, AXES, pairs)]
    all_gather x1 -> x0, blocking collectives: 32.1 us -> none  [body(): trials_all = lax.all_gather(trials, 'col', axis=1, tiled=True)]
    dot_general x4 -> x6, matrix products: 35.7 us -> 14.8 us  [dot(): jnp.einsum(spec, a, b, precision=HIGH, preferred_element_type=jnp.float32)]
    all_to_all x1 -> x0, blocking collectives: 13.4 us -> none  [body(): lax.all_to_all(conduction_orb, 'row', split_axis=1, concat_axis=0, tiled=...]
  transfers between devices with their start and end apart: 5 -> 23, of which waited for: 5 -> 19; matrix products, arithmetic and copies ran while one was open for 2% -> 5% of each run, Pallas kernels for 0% -> 0%
where the time goes in v1:
time: 172 us; the launch traced here: 171 us
  waiting for transfers between devices  94.8 us (55%)
  starting transfers between devices  52.3 us (30%)
  matrix products  14.8 us (9%)
  other arithmetic  5 us (3%)
  local copies, waits for them, and re-layouts  4.16 us (2%)
    ppermute x23, waiting for transfers between devices, flip(): return lax.ppermute(value, AXES, pairs)  94.8 us
    ppermute x23, starting transfers between devices, flip(): return lax.ppermute(value, AXES, pairs)  52.3 us
    dot_general x6, matrix products, dot(): jnp.einsum(spec, a, b, precision=HIGH, preferred_element_type=jnp.float32)  14.8 us
  transfers between devices with their start and end apart: 23, of which 19 were waited for; matrix products, arithmetic and copies ran while one was open for 5% of the time, Pallas kernels for 0%

profile of v1, /device:TPU:1, one launch (start us, length us, event | category | flops | bytes accessed | tf_op | source)
XLA Modules:
  0.0 171.3 jit_solution(17818816238397271713)
XLA Ops:
  0.0 2.0 %collective-permute-start.10 = (f32[64,1024]{1,0:T(8,128)}, f32[64,1024]{1,0:T(8,128)S(1)}, u32[]{:S(2)}, u32[]{:S(2)}) collective-permute-start(f32[64,1024]{1,0:T(8,128)} %param.6), channel_id=1, source_target_pairs={{0,16},{2,18},{4,20},{6,22},{8,24},{10,26},{12,28},{14,30},{16,0},... | collective-permute-start | bytes 786440 | tf_op jit(solution)/shard_map/ppermute | solution.py:26
  2.0 5.9 %collective-permute-done.10 = f32[64,1024]{1,0:T(8,128)S(1)} collective-permute-done((f32[64,1024]{1,0:T(8,128)}, f32[64,1024]{1,0:T(8,128)S(1)}, u32[]{:S(2)}, u32[]{:S(2)}) %collective-permute-start.10) | collective-permute-done | bytes 262176 | tf_op jit(solution)/shard_map/ppermute | solution.py:26
  7.9 1.0 pad_maximum_fusion.5
  8.9 4.1 %collective-permute-start.11 = (f32[128,1024]{1,0:T(8,128)S(1)}, f32[128,1024]{1,0:T(8,128)S(1)}, u32[]{:S(2)}, u32[]{:S(2)}) collective-permute-start(f32[128,1024]{1,0:T(8,128)S(1)} %pad_maximum_fusion.5), channel_id=1, source_target_pairs={{0,32},{2,34},{4,36},{6,38},{8,104},{10,106},{12,108},{14,110},{16... | collective-permute-start | bytes 1572872 | tf_op jit(solution)/shard_map/ppermute | solution.py:26
  13.1 6.6 %collective-permute-done.11 = f32[128,1024]{1,0:T(8,128)S(1)} collective-permute-done((f32[128,1024]{1,0:T(8,128)S(1)}, f32[128,1024]{1,0:T(8,128)S(1)}, u32[]{:S(2)}, u32[]{:S(2)}) %collective-permute-start.11) | collective-permute-done | bytes 524320 | tf_op jit(solution)/shard_map/ppermute | solution.py:26
  19.6 2.0 %pad_maximum_fusion.2 = f32[256,1024]{1,0:T(8,128)} fusion(f32[128,1024]{1,0:T(8,128)S(1)} %collective-permute-done.11, f32[64,1024]{1,0:T(8,128)S(1)} %collective-permute-done.10, f32[64,1024]{1,0:T(8,128)} %param.6), kind=kLoop, calls=%fused_computation.17 | loop fusion | flops 524288 | bytes 2097152 | tf_op jit(solution)/shard_map/concatenate | solution.py:34
  21.7 4.5 %collective-permute-start.3 = (f32[64,64]{1,0:T(8,128)S(1)}, f32[64,64]{1,0:T(8,128)S(1)}, u32[]{:S(2)}, u32[]{:S(2)}) collective-permute-start(f32[64,64]{1,0:T(8,128)S(1)} %get-tuple-element.7), channel_id=1, source_target_pairs={{0,8},{2,10},{4,12},{6,14},{8,0},{10,2},{12,4},{14,6},{16,24},{18,... | collective-permute-start | bytes 49160 | tf_op jit(solution)/shard_map/ppermute | solution.py:26
  26.2 0.9 collective-permute-done.3
  27.1 1.2 collective-permute-start.4
  28.4 1.9 %collective-permute-done.4 = f32[64,128]{1,0:T(8,128)S(1)} collective-permute-done((f32[64,128]{1,0:T(8,128)S(1)}, f32[64,128]{1,0:T(8,128)S(1)}, u32[]{:S(2)}, u32[]{:S(2)}) %collective-permute-start.4) | collective-permute-done | bytes 32800 | tf_op jit(solution)/shard_map/ppermute | solution.py:26
  30.6 6.0 %collective-permute-done.12 = f32[256,1024]{1,0:T(8,128)} collective-permute-done((f32[256,1024]{1,0:T(8,128)}, f32[256,1024]{1,0:T(8,128)}, u32[]{:S(2)}, u32[]{:S(2)}) %collective-permute-start.12) | collective-permute-done | bytes 1048608 | tf_op jit(solution)/shard_map/ppermute | solution.py:26
  36.6 1.3 constant_dynamic-update-slice_fusion.4
  37.9 3.3 %collective-permute-start.13 = (f32[512,1024]{1,0:T(8,128)S(1)}, f32[512,1024]{1,0:T(8,128)}, u32[]{:S(2)}, u32[]{:S(2)}) collective-permute-start(f32[512,1024]{1,0:T(8,128)S(1)} %constant_dynamic-update-slice_fusion.4), channel_id=1, source_target_pairs={{0,8},{2,10},{4,12},{6,14},{8,0},{10,2},{12,4},{14,6},{16,24},{18,... | collective-permute-start | bytes 6291464 | tf_op jit(solution)/shard_map/ppermute | solution.py:26
  41.5 3.8 %collective-permute-done.6 = f32[64,512]{1,0:T(8,128)S(1)} collective-permute-done((f32[64,512]{1,0:T(8,128)S(1)}, f32[64,512]{1,0:T(8,128)S(1)}, u32[]{:S(2)}, u32[]{:S(2)}) %collective-permute-start.6) | collective-permute-done | bytes 131104 | tf_op jit(solution)/shard_map/ppermute | solution.py:26
  45.3 2.8 %collective-permute-start.7 = (f32[64,1024]{1,0:T(8,128)S(1)}, f32[64,1024]{1,0:T(8,128)S(1)}, u32[]{:S(2)}, u32[]{:S(2)}) collective-permute-start(f32[64,1024]{1,0:T(8,128)S(1)} %concatenate.54), channel_id=1, source_target_pairs={{0,1},{2,3},{4,5},{6,7},{8,9},{10,11},{12,13},{14,15},{16,17},{18,... | collective-permute-start | bytes 786440 | tf_op jit(solution)/shard_map/ppermute | solution.py:26
  48.1 4.0 %collective-permute-done.7 = f32[64,1024]{1,0:T(8,128)S(1)} collective-permute-done((f32[64,1024]{1,0:T(8,128)S(1)}, f32[64,1024]{1,0:T(8,128)S(1)}, u32[]{:S(2)}, u32[]{:S(2)}) %collective-permute-start.7) | collective-permute-done | bytes 262176 | tf_op jit(solution)/shard_map/ppermute | solution.py:26
  52.2 2.8 %collective-permute-start.8 = (f32[128,1024]{1,0:T(8,128)S(1)}, f32[128,1024]{1,0:T(8,128)S(1)}, u32[]{:S(2)}, u32[]{:S(2)}) collective-permute-start(f32[128,1024]{1,0:T(8,128)S(1)} %pad_maximum_fusion.4), channel_id=1, source_target_pairs={{0,2},{2,0},{4,6},{6,4},{8,14},{10,12},{12,10},{14,8},{16,18},{18,... | collective-permute-start | bytes 1572872 | tf_op jit(solution)/shard_map/ppermute | solution.py:26
  55.0 6.6 %collective-permute-done.8 = f32[128,1024]{1,0:T(8,128)S(1)} collective-permute-done((f32[128,1024]{1,0:T(8,128)S(1)}, f32[128,1024]{1,0:T(8,128)S(1)}, u32[]{:S(2)}, u32[]{:S(2)}) %collective-permute-start.8) | collective-permute-done | bytes 524320 | tf_op jit(solution)/shard_map/ppermute | solution.py:26
  62.1 1.7 %copy.6 = f32[2,2,2,64,1024]{4,3,2,1,0:T(8,128)S(1)} copy(f32[2,2,2,64,1024]{4,3,2,0,1:T(8,128)} %bitcast.4) | data formatting | bytes 4194304 | tf_op jit(solution)/shard_map/transpose | solution.py:39
  63.8 0.6 pad_maximum_fusion
  64.4 0.6 copy.7
  65.0 10.8 %collective-permute-done.9 = f32[256,1024]{1,0:T(8,128)S(1)} collective-permute-done((f32[256,1024]{1,0:T(8,128)S(1)}, f32[256,1024]{1,0:T(8,128)S(1)}, u32[]{:S(2)}, u32[]{:S(2)}) %collective-permute-start.9) | collective-permute-done | bytes 1048608 | tf_op jit(solution)/shard_map/ppermute | solution.py:26
  75.8 3.5 %fusion = f32[512,1024]{1,0:T(8,128)S(1)} fusion(f32[1024,1024]{1,0:T(8,128)S(1)} %bitcast.26, f32[256,1024]{1,0:T(8,128)S(1)} %collective-permute-done.9, f32[128,1024]{1,0:T(8,128)S(1)} %collective-permute-done.8, f32[64,1024]{1,0:T(8,128)S(1)} %collective-permute-done.7, f32[64,1024]{1,0:T(8,128)S(1)} %concatenate.54), kind=kOutput, calls=%fused_computation.1 | convolution fusion | flops 3222798336 | bytes 8388608 | tf_op jit(solution)/shard_map/vc,cn->vn/dot_general | solution.py:50
  79.4 5.6 %collective-permute-start.14 = (f32[512,1024]{1,0:T(8,128)S(1)}, f32[512,1024]{1,0:T(8,128)S(1)}, u32[]{:S(2)}, u32[]{:S(2)}) collective-permute-start(f32[512,1024]{1,0:T(8,128)S(1)} %fusion), channel_id=1, source_target_pairs={{0,8},{2,10},{4,12},{6,14},{8,0},{10,2},{12,4},{14,6},{16,24},{18,... | collective-permute-start | bytes 6291464 | tf_op jit(solution)/shard_map/ppermute | solution.py:26
  84.9 2.8 %collective-permute-start = (f32[64,512]{1,0:T(8,128)S(1)}, f32[64,512]{1,0:T(8,128)S(1)}, u32[]{:S(2)}, u32[]{:S(2)}) collective-permute-start(f32[64,512]{1,0:T(8,128)S(1)} %copy-done.2), channel_id=1, source_target_pairs={{0,1},{2,3},{4,5},{6,7},{8,9},{10,11},{12,13},{14,15},{16,17},{18,... | collective-permute-start | bytes 393224 | tf_op jit(solution)/shard_map/ppermute | solution.py:26
  87.7 3.8 %collective-permute-done = f32[64,512]{1,0:T(8,128)S(1)} collective-permute-done((f32[64,512]{1,0:T(8,128)S(1)}, f32[64,512]{1,0:T(8,128)S(1)}, u32[]{:S(2)}, u32[]{:S(2)}) %collective-permute-start) | collective-permute-done | bytes 131104 | tf_op jit(solution)/shard_map/ppermute | solution.py:26
  91.5 2.8 %collective-permute-start.1 = (f32[128,512]{1,0:T(8,128)S(1)}, f32[128,512]{1,0:T(8,128)S(1)}, u32[]{:S(2)}, u32[]{:S(2)}) collective-permute-start(f32[128,512]{1,0:T(8,128)S(1)} %pad_maximum_fusion.6), channel_id=1, source_target_pairs={{0,2},{2,0},{4,6},{6,4},{8,14},{10,12},{12,10},{14,8},{16,18},{18,... | collective-permute-start | bytes 786440 | tf_op jit(solution)/shard_map/ppermute | solution.py:26
  94.3 3.8 %collective-permute-done.1 = f32[128,512]{1,0:T(8,128)S(1)} collective-permute-done((f32[128,512]{1,0:T(8,128)S(1)}, f32[128,512]{1,0:T(8,128)S(1)}, u32[]{:S(2)}, u32[]{:S(2)}) %collective-permute-start.1) | collective-permute-done | bytes 262176 | tf_op jit(solution)/shard_map/ppermute | solution.py:26
  98.5 8.2 %collective-permute-done.2 = f32[256,512]{1,0:T(8,128)S(1)} collective-permute-done((f32[256,512]{1,0:T(8,128)S(1)}, f32[256,512]{1,0:T(8,128)S(1)}, u32[]{:S(2)}, u32[]{:S(2)}) %collective-permute-start.2) | collective-permute-done | bytes 524320 | tf_op jit(solution)/shard_map/ppermute | solution.py:26
  106.8 1.9 %fusion.16 = f32[512,1024]{1,0:T(8,128)S(1)} fusion(f32[512,512]{1,0:T(8,128)S(1)} %bitcast.29, f32[512,1024]{1,0:T(8,128)S(1)} %collective-permute-done.14), kind=kOutput, calls=%fused_computation.45 | convolution fusion | flops 1610612736 | bytes 5242880 | tf_op jit(solution)/shard_map/vm,vn->mn/dot_general | solution.py:50
  108.8 1.9 %fusion.10 = f32[512,1024]{1,0:T(8,128)S(1)} fusion(f32[512,512]{1,0:T(8,128)S(1)} %bitcast.30, f32[512,1024]{1,0:T(8,128)S(1)} %copy-done, f32[512,1024]{1,0:T(8,128)S(1)} %fusion.16), kind=kOutput, calls=%fused_computation.11 | convolution fusion | flops 1611137024 | bytes 7340032 | tf_op jit(solution)/shard_map/vm,mn->vn/dot_general | solution.py:50
  110.7 2.9 %collective-permute-start.15 = (f32[512,1024]{1,0:T(8,128)S(1)}, f32[512,1024]{1,0:T(8,128)S(1)}, u32[]{:S(2)}, u32[]{:S(2)}) collective-permute-start(f32[512,1024]{1,0:T(8,128)S(1)} %fusion.10), channel_id=1, source_target_pairs={{0,8},{2,10},{4,12},{6,14},{8,0},{10,2},{12,4},{14,6},{16,24},{18,... | collective-permute-start | bytes 6291464 | tf_op jit(solution)/shard_map/ppermute | solution.py:26
  113.6 1.9 %fusion.15 = f32[512,1024]{1,0:T(8,128)S(1)} fusion(f32[512,512]{1,0:T(8,128)S(1)} %constant_dynamic-update-slice_fusion, f32[512,1024]{1,0:T(8,128)S(1)} %fusion), kind=kOutput, calls=%fused_computation.44 | convolution fusion | flops 1610612736 | bytes 5242880 | tf_op jit(solution)/shard_map/vm,vn->mn/dot_general | solution.py:50
  115.5 1.9 %fusion.12 = f32[512,1024]{1,0:T(8,128)S(1)} fusion(f32[512,512]{1,0:T(8,128)S(1)} %constant_dynamic-update-slice_fusion, f32[512,1024]{1,0:T(8,128)S(1)} %copy-done, f32[512,1024]{1,0:T(8,128)S(1)} %fusion.15), kind=kOutput, calls=%fused_computation.13 | convolution fusion | flops 1611137024 | bytes 7340032 | tf_op jit(solution)/shard_map/vm,mn->vn/dot_general | solution.py:50
  117.5 3.5 %fusion.8 = f32[512,1024]{1,0:T(8,128)S(1)} fusion(f32[1024,1024]{1,0:T(8,128)S(1)} %bitcast.27, f32[512,1024]{1,0:T(8,128)S(1)} %fusion.12, f32[512,1024]{1,0:T(8,128)S(1)} %collective-permute-done.15), kind=kOutput, calls=%fused_computation.9 | convolution fusion | flops 3221749760 | bytes 10485760 | tf_op jit(solution)/shard_map/vn,cn->vc/dot_general | solution.py:50
  121.2 13.9 %collective-permute-done.16 = f32[256,1024]{1,0:T(8,128)S(1)} collective-permute-done((f32[256,1024]{1,0:T(8,128)S(1)}, f32[256,1024]{1,0:T(8,128)S(1)}, u32[]{:S(2)}, u32[]{:S(2)}) %collective-permute-start.16) | collective-permute-done | bytes 1048608 | tf_op jit(solution)/shard_map/ppermute | solution.py:26
  135.6 8.2 %collective-permute-done.17 = f32[256,512]{1,0:T(8,128)S(1)} collective-permute-done((f32[256,512]{1,0:T(8,128)S(1)}, f32[256,512]{1,0:T(8,128)S(1)}, u32[]{:S(2)}, u32[]{:S(2)}) %collective-permute-start.17) | collective-permute-done | bytes 524320 | tf_op jit(solution)/shard_map/ppermute | solution.py:26
  143.9 2.8 %collective-permute-start.18 = (f32[128,512]{1,0:T(8,128)S(1)}, f32[128,512]{1,0:T(8,128)S(1)}, u32[]{:S(2)}, u32[]{:S(2)}) collective-permute-start(f32[128,512]{1,0:T(8,128)S(1)} %slice.61), channel_id=1, source_target_pairs={{0,2},{2,0},{4,6},{6,4},{8,14},{10,12},{12,10},{14,8},{16,18},{18,... | collective-permute-start | bytes 786440 | tf_op jit(solution)/shard_map/ppermute | solution.py:26
  146.7 3.8 %collective-permute-done.18 = f32[128,512]{1,0:T(8,128)S(1)} collective-permute-done((f32[128,512]{1,0:T(8,128)S(1)}, f32[128,512]{1,0:T(8,128)S(1)}, u32[]{:S(2)}, u32[]{:S(2)}) %collective-permute-start.18) | collective-permute-done | bytes 262176 | tf_op jit(solution)/shard_map/ppermute | solution.py:26
  150.5 3.0 %collective-permute-start.19 = (f32[128,256]{1,0:T(8,128)S(1)}, f32[128,256]{1,0:T(8,128)S(1)}, u32[]{:S(2)}, u32[]{:S(2)}) collective-permute-start(f32[128,256]{1,0:T(8,128)S(1)} %slice.63), channel_id=1, source_target_pairs={{0,32},{2,34},{4,36},{6,38},{8,104},{10,106},{12,108},{14,110},{16... | collective-permute-start | bytes 393224 | tf_op jit(solution)/shard_map/ppermute | solution.py:26
  153.5 2.4 %collective-permute-done.19 = f32[128,256]{1,0:T(8,128)S(1)} collective-permute-done((f32[128,256]{1,0:T(8,128)S(1)}, f32[128,256]{1,0:T(8,128)S(1)}, u32[]{:S(2)}, u32[]{:S(2)}) %collective-permute-start.19) | collective-permute-done | bytes 131104 | tf_op jit(solution)/shard_map/ppermute | solution.py:26
  155.9 2.8 %collective-permute-start.20 = (f32[64,256]{1,0:T(8,128)S(1)}, f32[64,256]{1,0:T(8,128)S(1)}, u32[]{:S(2)}, u32[]{:S(2)}) collective-permute-start(f32[64,256]{1,0:T(8,128)S(1)} %slice.65), channel_id=1, source_target_pairs={{0,1},{2,3},{4,5},{6,7},{8,9},{10,11},{12,13},{14,15},{16,17},{18,... | collective-permute-start | bytes 196616 | tf_op jit(solution)/shard_map/ppermute | solution.py:26
  158.7 1.9 %collective-permute-done.20 = f32[64,256]{1,0:T(8,128)S(1)} collective-permute-done((f32[64,256]{1,0:T(8,128)S(1)}, f32[64,256]{1,0:T(8,128)S(1)}, u32[]{:S(2)}, u32[]{:S(2)}) %collective-permute-start.20) | collective-permute-done | bytes 65568 | tf_op jit(solution)/shard_map/ppermute | solution.py:26
  160.6 1.3 collective-permute-start.21
  161.9 1.6 collective-permute-done.21
  163.6 6.3 %collective-permute-start.22 = (f32[64,64]{1,0:T(8,128)S(1)}, f32[64,64]{1,0:T(8,128)S(1)}, u32[]{:S(2)}, u32[]{:S(2)}) collective-permute-start(f32[64,64]{1,0:T(8,128)S(1)} %slice.69), channel_id=1, source_target_pairs={{0,8},{2,10},{4,12},{6,14},{8,0},{10,2},{12,4},{14,6},{16,24},{18,... | collective-permute-start | bytes 49160 | tf_op jit(solution)/shard_map/ppermute | solution.py:26
  169.8 0.9 collective-permute-done.22
  170.7 0.6 pad_maximum_fusion.9
  (50 shorter events, 2.5 us)
Async XLA Ops:
  0.0 28.4 %copy-start.1 = (f32[64,1024]{1,0:T(8,128)S(1)}, f32[64,1024]{1,0:T(8,128)}, u32[]{:S(2)}) copy-start(f32[64,1024]{1,0:T(8,128)} %param.6) | copy-start | bytes 786436
  0.0 21.7 %copy-start.3 = (f32[2,64,64]{2,1,0:T(8,128)S(1)}, f32[2,64,64]{2,1,0:T(8,128)}, u32[]{:S(2)}) copy-start(f32[2,64,64]{2,1,0:T(8,128)} %param.4) | copy-start | bytes 98308
  0.0 7.9 %collective-permute-start.10 = (f32[64,1024]{1,0:T(8,128)}, f32[64,1024]{1,0:T(8,128)S(1)}, u32[]{:S(2)}, u32[]{:S(2)}) collective-permute-start(f32[64,1024]{1,0:T(8,128)} %param.6), channel_id=1, source_target_pairs={{0,16},{2,18},{4,20},{6,22},{8,24},{10,26},{12,28},{14,30},{16,0},... | collective-permute-start | bytes 786440 | tf_op jit(solution)/shard_map/ppermute | solution.py:26
  8.9 10.7 %collective-permute-start.11 = (f32[128,1024]{1,0:T(8,128)S(1)}, f32[128,1024]{1,0:T(8,128)S(1)}, u32[]{:S(2)}, u32[]{:S(2)}) collective-permute-start(f32[128,1024]{1,0:T(8,128)S(1)} %pad_maximum_fusion.5), channel_id=1, source_target_pairs={{0,32},{2,34},{4,36},{6,38},{8,104},{10,106},{12,108},{14,110},{16... | collective-permute-start | bytes 1572872 | tf_op jit(solution)/shard_map/ppermute | solution.py:26
  21.7 15.0 %collective-permute-start.12 = (f32[256,1024]{1,0:T(8,128)}, f32[256,1024]{1,0:T(8,128)}, u32[]{:S(2)}, u32[]{:S(2)}) collective-permute-start(f32[256,1024]{1,0:T(8,128)} %pad_maximum_fusion.2), channel_id=1, source_target_pairs={{0,96},{2,98},{4,100},{6,102},{8,40},{10,42},{12,44},{14,46},{16,1... | collective-permute-start | bytes 3145736 | tf_op jit(solution)/shard_map/ppermute | solution.py:26
  21.7 5.4 %collective-permute-start.3 = (f32[64,64]{1,0:T(8,128)S(1)}, f32[64,64]{1,0:T(8,128)S(1)}, u32[]{:S(2)}, u32[]{:S(2)}) collective-permute-start(f32[64,64]{1,0:T(8,128)S(1)} %get-tuple-element.7), channel_id=1, source_target_pairs={{0,8},{2,10},{4,12},{6,14},{8,0},{10,2},{12,4},{14,6},{16,24},{18,... | collective-permute-start | bytes 49160 | tf_op jit(solution)/shard_map/ppermute | solution.py:26
  27.1 3.2 %collective-permute-start.4 = (f32[64,128]{1,0:T(8,128)S(1)}, f32[64,128]{1,0:T(8,128)S(1)}, u32[]{:S(2)}, u32[]{:S(2)}) collective-permute-start(f32[64,128]{1,0:T(8,128)S(1)} %pad_maximum_fusion.10), channel_id=1, source_target_pairs={{0,16},{2,18},{4,20},{6,22},{8,24},{10,26},{12,28},{14,30},{16,0},... | collective-permute-start | bytes 98312 | tf_op jit(solution)/shard_map/ppermute | solution.py:26
  30.4 10.9 %collective-permute-start.5 = (f32[64,256]{1,0:T(8,128)S(1)}, f32[64,256]{1,0:T(8,128)S(1)}, u32[]{:S(2)}, u32[]{:S(2)}) collective-permute-start(f32[64,256]{1,0:T(8,128)S(1)} %pad_maximum_fusion.8), channel_id=1, source_target_pairs={{0,32},{2,34},{4,36},{6,38},{8,104},{10,106},{12,108},{14,110},{16... | collective-permute-start | bytes 196616 | tf_op jit(solution)/shard_map/ppermute | solution.py:26
  37.9 24.1 %collective-permute-start.13 = (f32[512,1024]{1,0:T(8,128)S(1)}, f32[512,1024]{1,0:T(8,128)}, u32[]{:S(2)}, u32[]{:S(2)}) collective-permute-start(f32[512,1024]{1,0:T(8,128)S(1)} %constant_dynamic-update-slice_fusion.4), channel_id=1, source_target_pairs={{0,8},{2,10},{4,12},{6,14},{8,0},{10,2},{12,4},{14,6},{16,24},{18,... | collective-permute-start | bytes 6291464 | tf_op jit(solution)/shard_map/ppermute | solution.py:26
  41.4 3.9 %collective-permute-start.6 = (f32[64,512]{1,0:T(8,128)S(1)}, f32[64,512]{1,0:T(8,128)S(1)}, u32[]{:S(2)}, u32[]{:S(2)}) collective-permute-start(f32[64,512]{1,0:T(8,128)S(1)} %pad_maximum_fusion.7), channel_id=1, source_target_pairs={{0,96},{2,98},{4,100},{6,102},{8,40},{10,42},{12,44},{14,46},{16,1... | collective-permute-start | bytes 393224 | tf_op jit(solution)/shard_map/ppermute | solution.py:26
  45.3 6.8 %collective-permute-start.7 = (f32[64,1024]{1,0:T(8,128)S(1)}, f32[64,1024]{1,0:T(8,128)S(1)}, u32[]{:S(2)}, u32[]{:S(2)}) collective-permute-start(f32[64,1024]{1,0:T(8,128)S(1)} %concatenate.54), channel_id=1, source_target_pairs={{0,1},{2,3},{4,5},{6,7},{8,9},{10,11},{12,13},{14,15},{16,17},{18,... | collective-permute-start | bytes 786440 | tf_op jit(solution)/shard_map/ppermute | solution.py:26
  52.2 9.4 %collective-permute-start.8 = (f32[128,1024]{1,0:T(8,128)S(1)}, f32[128,1024]{1,0:T(8,128)S(1)}, u32[]{:S(2)}, u32[]{:S(2)}) collective-permute-start(f32[128,1024]{1,0:T(8,128)S(1)} %pad_maximum_fusion.4), channel_id=1, source_target_pairs={{0,2},{2,0},{4,6},{6,4},{8,14},{10,12},{12,10},{14,8},{16,18},{18,... | collective-permute-start | bytes 1572872 | tf_op jit(solution)/shard_map/ppermute | solution.py:26
  61.7 14.1 %collective-permute-start.9 = (f32[256,1024]{1,0:T(8,128)S(1)}, f32[256,1024]{1,0:T(8,128)S(1)}, u32[]{:S(2)}, u32[]{:S(2)}) collective-permute-start(f32[256,1024]{1,0:T(8,128)S(1)} %pad_maximum_fusion.1), channel_id=1, source_target_pairs={{0,6},{2,4},{4,2},{6,0},{8,10},{10,8},{12,14},{14,12},{16,22},{18,... | collective-permute-start | bytes 3145736 | tf_op jit(solution)/shard_map/ppermute | solution.py:26
  75.8 9.1 %copy-start.2 = (f32[64,512]{1,0:T(8,128)S(1)}, f32[64,512]{1,0:T(8,128)}, u32[]{:S(2)}) copy-start(f32[64,512]{1,0:T(8,128)} %param.5) | copy-start | bytes 393220
  79.4 27.5 %collective-permute-start.14 = (f32[512,1024]{1,0:T(8,128)S(1)}, f32[512,1024]{1,0:T(8,128)S(1)}, u32[]{:S(2)}, u32[]{:S(2)}) collective-permute-start(f32[512,1024]{1,0:T(8,128)S(1)} %fusion), channel_id=1, source_target_pairs={{0,8},{2,10},{4,12},{6,14},{8,0},{10,2},{12,4},{14,6},{16,24},{18,... | collective-permute-start | bytes 6291464 | tf_op jit(solution)/shard_map/ppermute | solution.py:26
  84.9 6.6 %collective-permute-start = (f32[64,512]{1,0:T(8,128)S(1)}, f32[64,512]{1,0:T(8,128)S(1)}, u32[]{:S(2)}, u32[]{:S(2)}) collective-permute-start(f32[64,512]{1,0:T(8,128)S(1)} %copy-done.2), channel_id=1, source_target_pairs={{0,1},{2,3},{4,5},{6,7},{8,9},{10,11},{12,13},{14,15},{16,17},{18,... | collective-permute-start | bytes 393224 | tf_op jit(solution)/shard_map/ppermute | solution.py:26
  91.5 6.6 %collective-permute-start.1 = (f32[128,512]{1,0:T(8,128)S(1)}, f32[128,512]{1,0:T(8,128)S(1)}, u32[]{:S(2)}, u32[]{:S(2)}) collective-permute-start(f32[128,512]{1,0:T(8,128)S(1)} %pad_maximum_fusion.6), channel_id=1, source_target_pairs={{0,2},{2,0},{4,6},{6,4},{8,14},{10,12},{12,10},{14,8},{16,18},{18,... | collective-permute-start | bytes 786440 | tf_op jit(solution)/shard_map/ppermute | solution.py:26
  98.1 8.6 %collective-permute-start.2 = (f32[256,512]{1,0:T(8,128)S(1)}, f32[256,512]{1,0:T(8,128)S(1)}, u32[]{:S(2)}, u32[]{:S(2)}) collective-permute-start(f32[256,512]{1,0:T(8,128)S(1)} %pad_maximum_fusion.3), channel_id=1, source_target_pairs={{0,6},{2,4},{4,2},{6,0},{8,10},{10,8},{12,14},{14,12},{16,22},{18,... | collective-permute-start | bytes 1572872 | tf_op jit(solution)/shard_map/ppermute | solution.py:26
  106.8 2.0 %copy-start = (f32[512,1024]{1,0:T(8,128)S(1)}, f32[512,1024]{1,0:T(8,128)}, u32[]{:S(2)}) copy-start(f32[512,1024]{1,0:T(8,128)} %param.7) | copy-start | bytes 6291460
  110.7 6.8 %collective-permute-start.15 = (f32[512,1024]{1,0:T(8,128)S(1)}, f32[512,1024]{1,0:T(8,128)S(1)}, u32[]{:S(2)}, u32[]{:S(2)}) collective-permute-start(f32[512,1024]{1,0:T(8,128)S(1)} %fusion.10), channel_id=1, source_target_pairs={{0,8},{2,10},{4,12},{6,14},{8,0},{10,2},{12,4},{14,6},{16,24},{18,... | collective-permute-start | bytes 6291464 | tf_op jit(solution)/shard_map/ppermute | solution.py:26
  121.1 14.0 %collective-permute-start.16 = (f32[256,1024]{1,0:T(8,128)S(1)}, f32[256,1024]{1,0:T(8,128)S(1)}, u32[]{:S(2)}, u32[]{:S(2)}) collective-permute-start(f32[256,1024]{1,0:T(8,128)S(1)} %slice.57), channel_id=1, source_target_pairs={{0,6},{2,4},{4,2},{6,0},{8,10},{10,8},{12,14},{14,12},{16,22},{18,... | collective-permute-start | bytes 3145736 | tf_op jit(solution)/shard_map/ppermute | solution.py:26
  135.3 8.4 %collective-permute-start.17 = (f32[256,512]{1,0:T(8,128)S(1)}, f32[256,512]{1,0:T(8,128)S(1)}, u32[]{:S(2)}, u32[]{:S(2)}) collective-permute-start(f32[256,512]{1,0:T(8,128)S(1)} %slice.59), channel_id=1, source_target_pairs={{0,96},{2,98},{4,100},{6,102},{8,40},{10,42},{12,44},{14,46},{16,1... | collective-permute-start | bytes 1572872 | tf_op jit(solution)/shard_map/ppermute | solution.py:26
  143.9 6.6 %collective-permute-start.18 = (f32[128,512]{1,0:T(8,128)S(1)}, f32[128,512]{1,0:T(8,128)S(1)}, u32[]{:S(2)}, u32[]{:S(2)}) collective-permute-start(f32[128,512]{1,0:T(8,128)S(1)} %slice.61), channel_id=1, source_target_pairs={{0,2},{2,0},{4,6},{6,4},{8,14},{10,12},{12,10},{14,8},{16,18},{18,... | collective-permute-start | bytes 786440 | tf_op jit(solution)/shard_map/ppermute | solution.py:26
  150.5 5.4 %collective-permute-start.19 = (f32[128,256]{1,0:T(8,128)S(1)}, f32[128,256]{1,0:T(8,128)S(1)}, u32[]{:S(2)}, u32[]{:S(2)}) collective-permute-start(f32[128,256]{1,0:T(8,128)S(1)} %slice.63), channel_id=1, source_target_pairs={{0,32},{2,34},{4,36},{6,38},{8,104},{10,106},{12,108},{14,110},{16... | collective-permute-start | bytes 393224 | tf_op jit(solution)/shard_map/ppermute | solution.py:26
  155.9 4.7 %collective-permute-start.20 = (f32[64,256]{1,0:T(8,128)S(1)}, f32[64,256]{1,0:T(8,128)S(1)}, u32[]{:S(2)}, u32[]{:S(2)}) collective-permute-start(f32[64,256]{1,0:T(8,128)S(1)} %slice.65), channel_id=1, source_target_pairs={{0,1},{2,3},{4,5},{6,7},{8,9},{10,11},{12,13},{14,15},{16,17},{18,... | collective-permute-start | bytes 196616 | tf_op jit(solution)/shard_map/ppermute | solution.py:26
  160.6 2.8 %collective-permute-start.21 = (f32[64,128]{1,0:T(8,128)S(1)}, f32[64,128]{1,0:T(8,128)S(1)}, u32[]{:S(2)}, u32[]{:S(2)}) collective-permute-start(f32[64,128]{1,0:T(8,128)S(1)} %slice.67), channel_id=1, source_target_pairs={{0,16},{2,18},{4,20},{6,22},{8,24},{10,26},{12,28},{14,30},{16,0},... | collective-permute-start | bytes 98312 | tf_op jit(solution)/shard_map/ppermute | solution.py:26
  163.6 7.1 %collective-permute-start.22 = (f32[64,64]{1,0:T(8,128)S(1)}, f32[64,64]{1,0:T(8,128)S(1)}, u32[]{:S(2)}, u32[]{:S(2)}) collective-permute-start(f32[64,64]{1,0:T(8,128)S(1)} %slice.69), channel_id=1, source_target_pairs={{0,8},{2,10},{4,12},{6,14},{8,0},{10,2},{12,4},{14,6},{16,24},{18,... | collective-permute-start | bytes 49160 | tf_op jit(solution)/shard_map/ppermute | solution.py:26

commit v2 on v1

--- a/solution.py
+++ b/solution.py
@@ -34,15 +34,16 @@
     return jnp.concatenate([value, flip(value, step)], axis=axis)
 
 
-def swap_bits(value):
-    shape = value.shape
-    return value.reshape((2, 2, 2, shape[0] // 8) + shape[1:]).swapaxes(0, 1).reshape(shape)
+def halves(value, axis):
+    size = value.shape[axis] // 2
+    return (
+        lax.slice_in_dim(value, 0, size, axis=axis),
+        lax.slice_in_dim(value, size, 2 * size, axis=axis),
+    )
 
 
 def halve(value, step, axis):
-    size = value.shape[axis] // 2
-    kept = lax.slice_in_dim(value, 0, size, axis=axis)
-    sent = lax.slice_in_dim(value, size, 2 * size, axis=axis)
+    kept, sent = halves(value, axis)
     return kept + flip(sent, step)
 
 
@@ -50,37 +51,67 @@
     return jnp.einsum(spec, a, b, precision=HIGH, preferred_element_type=jnp.float32)
 
 
+def in_parts(v):
+    first = v[:, :, :, :32].swapaxes(0, 1).reshape(256, -1)
+    return jnp.concatenate([first, v[:, :, :, 32:].reshape(256, -1)], axis=0)
+
+
 def body(trials, valence, conduction, screened):
     core = lax.axis_index("core")
     mine = lax.dynamic_index_in_dim(trials, core, 0, keepdims=False)
     theirs = lax.dynamic_index_in_dim(trials, 1 - core, 0, keepdims=False)
-    trial = jnp.concatenate([mine, flip(theirs, "core")], axis=1)
 
-    c = conduction
-    for step in (XL, ZA, ZB):
-        c = grow(c, step, 0)
-    c_other = swap_bits(flip(c, "core"))
-    c_all = jnp.stack([c.reshape(8, 64, -1), c_other.reshape(8, 64, -1)], axis=1).reshape(1024, -1)
+    c = grow(conduction, XL, 0)
+    v = grow(valence, YA, 0)
+    t = jnp.concatenate([mine, flip(theirs, "core")], axis=1)
+    t = t.reshape(2, 32, 128)
+    t = grow(t, ZA, 2)
+    t = grow(t, YA, 1)
+    t, c, v = lax.optimization_barrier((t, c, v))
+    c = grow(c, ZA, 0)
+    v = grow(v, XH, 0)
+    t = grow(t, XL, 2)
+    p, q = t[0], t[1]
+    p = grow(p, YB, 0)
+    q = grow(q, ZB, 1)
+    p, q, c, v = lax.optimization_barrier((p, q, c, v))
+    c = grow(c, ZB, 0)
+    v = grow(v, YB, 0)
+    got = flip(jnp.concatenate([p, q[:, :512], q[:, 512:]], axis=0), XH)
+    p = jnp.concatenate([p, got[:128]], axis=0)
+    q = jnp.concatenate([q, jnp.concatenate([got[128:192], got[192:]], axis=1)], axis=0)
+    p, q, c, v = lax.optimization_barrier((p, q, c, v))
+    c_other = flip(c, "core")
+    p = grow(p, ZB, 1)
+    q = grow(q, YB, 0)
+    trial = jnp.concatenate([p, q], axis=0)
 
-    for step in (XL, ZA, ZB):
-        trial = grow(trial, step, 1)
-    for step in (XH, YA, YB):
-        trial = grow(trial, step, 0)
-
-    v = valence
-    for step in (XH, YA, YB):
-        v = grow(v, step, 0)
-    v_other = swap_bits(v)
+    c_own = c.reshape(2, 2, 2, 64, 1024).swapaxes(1, 2)
+    c_other = c_other.reshape(2, 2, 2, 64, 1024).transpose(1, 2, 0, 3, 4)
+    c_all = jnp.stack([c_own, c_other], axis=3).reshape(1024, 1024)
+    v = v.reshape(2, 2, 2, 64, 512)
+    v_mine, v_theirs = in_parts(v), in_parts(v.swapaxes(0, 2))
 
     half_mine = dot("vc,cn->vn", trial, c_all)
     half_theirs = flip(half_mine, "core")
-    pairs_mine = screened * dot("vm,vn->mn", v, half_mine)
-    pairs_theirs = screened * dot("vm,vn->mn", v_other, half_theirs)
-    sums_theirs = dot("vm,mn->vn", v_other, pairs_theirs)
-    sums_mine = dot("vm,mn->vn", v, pairs_mine) + flip(sums_theirs, "core")
+    pairs_mine = screened * dot("vm,vn->mn", v_mine, half_mine)
+    pairs_theirs = screened * dot("vm,vn->mn", v_theirs, half_theirs)
+    sums_theirs = dot("vm,mn->vn", v_theirs, pairs_theirs)
+    sums_mine = dot("vm,mn->vn", v_mine, pairs_mine) + flip(sums_theirs, "core")
+
     r = dot("vn,cn->vc", sums_mine, c_all)
-    for step, axis in ((YB, 0), (ZB, 1), (YA, 0), (ZA, 1), (XH, 0), (XL, 1)):
-        r = halve(r, step, axis)
+    p, q = r[:256], r[256:]
+    p = halve(p, ZB, 1)
+    q = halve(q, YB, 0)
+    p = p.reshape(2, 2, 64, 512)
+    p = (p[:, 0] + flip(p[:, 1], YB)).reshape(128, 512)
+    q = halve(q, ZB, 1)
+    r = jnp.stack([p, q]).reshape(4, 2, 32, 512)
+    r = (r[:, 0] + flip(r[:, 1], YA)).reshape(128, 512)
+    r = r.reshape(128, 2, 2, 128)
+    r = (r[:, :, 0] + flip(r[:, :, 1].reshape(128, 256), ZA).reshape(128, 2, 128)).reshape(2, 64, 256)
+    r = halve(r, XH, 1).reshape(64, 256)
+    r = halve(r, XL, 1)
     kept = r[:, :64]
     got = flip(r[:, 64:], "core")
     first = core == 0

time: 172 us -> 134 us (0.78)
  waiting for transfers between devices: 94.8 us -> 61 us
  starting transfers between devices: 52.3 us -> 50 us
    ppermute x23 -> x27, waiting for transfers between devices: 94.8 us -> 61 us  [flip(): return lax.ppermute(value, AXES, pairs)]
    ppermute x23 -> x27, starting transfers between devices: 52.3 us -> 50 us  [flip(): return lax.ppermute(value, AXES, pairs)]
  transfers between devices with their start and end apart: 23 -> 27, of which waited for: 19 -> 23; matrix products, arithmetic and copies ran while one was open for 5% -> 5% of each run, Pallas kernels for 0% -> 0%
where the time goes in v2:
time: 134 us; the launch traced here: 133 us
  waiting for transfers between devices  61 us (46%)
  starting transfers between devices  50 us (37%)
  matrix products  14.8 us (11%)
  other arithmetic  3.9 us (3%)
  local copies, waits for them, and re-layouts  3.13 us (2%)
    ppermute x27, waiting for transfers between devices, flip(): return lax.ppermute(value, AXES, pairs)  61 us
    ppermute x27, starting transfers between devices, flip(): return lax.ppermute(value, AXES, pairs)  50 us
    dot_general x6, matrix products, dot(): jnp.einsum(spec, a, b, precision=HIGH, preferred_element_type=jnp.float32)  14.8 us
  transfers between devices with their start and end apart: 27, of which 23 were waited for; matrix products, arithmetic and copies ran while one was open for 5% of the time, Pallas kernels for 0%

profile of v2, /device:TPU:1, one launch (start us, length us, event | category | flops | bytes accessed | tf_op | source)
XLA Modules:
  0.0 133.3 jit_solution(2491847303571247236)
XLA Ops:
  0.0 0.8 constant_dynamic-slice_fusion
  0.8 1.4 %collective-permute-start = (f32[64,64]{1,0:T(8,128)S(1)}, f32[64,64]{1,0:T(8,128)S(1)}, u32[]{:S(2)}, u32[]{:S(2)}) collective-permute-start(f32[64,64]{1,0:T(8,128)S(1)} %get-tuple-element.42), channel_id=1, source_target_pairs={{0,8},{2,10},{4,12},{6,14},{8,0},{10,2},{12,4},{14,6},{16,24},{18,... | collective-permute-start | bytes 49160 | tf_op jit(solution)/shard_map/ppermute | solution.py:26
  2.2 0.9 collective-permute-done
  3.1 3.9 %collective-permute-start.1 = (f32[2,32,128]{2,1,0:T(8,128)S(1)}, f32[2,32,128]{2,1,0:T(8,128)S(1)}, u32[]{:S(2)}, u32[]{:S(2)}) collective-permute-start(f32[2,32,128]{2,1,0:T(8,128)S(1)} %pad_maximum_fusion.21), channel_id=1, source_target_pairs={{0,32},{2,34},{4,36},{6,38},{8,104},{10,106},{12,108},{14,110},{16... | collective-permute-start | bytes 98312 | tf_op jit(solution)/shard_map/ppermute | solution.py:26
  7.0 1.3 collective-permute-done.1
  8.4 2.8 %collective-permute-start.2 = (f32[2,32,256]{2,1,0:T(8,128)S(1)}, f32[2,32,256]{2,1,0:T(8,128)S(1)}, u32[]{:S(2)}, u32[]{:S(2)}) collective-permute-start(f32[2,32,256]{2,1,0:T(8,128)S(1)} %pad_maximum_fusion.19), channel_id=1, source_target_pairs={{0,2},{2,0},{4,6},{6,4},{8,14},{10,12},{12,10},{14,8},{16,18},{18,... | collective-permute-start | bytes 196616 | tf_op jit(solution)/shard_map/ppermute | solution.py:26
  11.2 1.2 collective-permute-start.3
  13.0 4.7 %collective-permute-done.4 = f32[64,512]{1,0:T(8,128)S(1)} collective-permute-done((f32[64,512]{1,0:T(8,128)}, f32[64,512]{1,0:T(8,128)S(1)}, u32[]{:S(2)}, u32[]{:S(2)}) %collective-permute-start.4) | collective-permute-done | bytes 131104 | tf_op jit(solution)/shard_map/ppermute | solution.py:26
  17.7 0.9 pad_maximum_fusion.15
  18.6 1.0 pad_maximum_fusion.12
  19.6 0.6 collective-permute-start.5
  20.2 3.8 %collective-permute-start.8 = (f32[128,1024]{1,0:T(8,128)S(1)}, f32[128,1024]{1,0:T(8,128)S(1)}, u32[]{:S(2)}, u32[]{:S(2)}) collective-permute-start(f32[128,1024]{1,0:T(8,128)S(1)} %pad_maximum_fusion.12), channel_id=1, source_target_pairs={{0,32},{2,34},{4,36},{6,38},{8,104},{10,106},{12,108},{14,110},{16... | collective-permute-start | bytes 1572872 | tf_op jit(solution)/shard_map/ppermute | solution.py:26
  24.3 2.8 %collective-permute-start.9 = (f32[128,512]{1,0:T(8,128)S(1)}, f32[128,512]{1,0:T(8,128)S(1)}, u32[]{:S(2)}, u32[]{:S(2)}) collective-permute-start(f32[128,512]{1,0:T(8,128)S(1)} %pad_maximum_fusion.15), channel_id=1, source_target_pairs={{0,1},{2,3},{4,5},{6,7},{8,9},{10,11},{12,13},{14,15},{16,17},{18,... | collective-permute-start | bytes 786440 | tf_op jit(solution)/shard_map/ppermute | solution.py:26
  27.1 0.5 collective-permute-start.6
  27.6 2.2 %collective-permute-done.7 = f32[64,512]{1,0:T(8,128)S(1)} collective-permute-done((f32[64,512]{1,0:T(8,128)S(1)}, f32[64,512]{1,0:T(8,128)S(1)}, u32[]{:S(2)}, u32[]{:S(2)}) %collective-permute-start.7) | collective-permute-done | bytes 131104 | tf_op jit(solution)/shard_map/ppermute | solution.py:26
  29.9 1.3 %collective-permute-done.6 = f32[64,512]{1,0:T(8,128)S(1)} collective-permute-done((f32[64,512]{1,0:T(8,128)S(1)}, f32[64,512]{1,0:T(8,128)S(1)}, u32[]{:S(2)}, u32[]{:S(2)}) %collective-permute-start.6) | collective-permute-done | bytes 131104 | tf_op jit(solution)/shard_map/ppermute | solution.py:26
  31.6 2.8 %collective-permute-start.10 = (f32[256,512]{1,0:T(8,128)S(1)}, f32[256,512]{1,0:T(8,128)S(1)}, u32[]{:S(2)}, u32[]{:S(2)}) collective-permute-start(f32[256,512]{1,0:T(8,128)S(1)} %fusion.16), channel_id=1, source_target_pairs={{0,1},{2,3},{4,5},{6,7},{8,9},{10,11},{12,13},{14,15},{16,17},{18,... | collective-permute-start | bytes 1572872 | tf_op jit(solution)/shard_map/ppermute | solution.py:26
  34.4 1.8 %collective-permute-start.11 = (f32[256,1024]{1,0:T(8,128)S(1)}, f32[256,1024]{1,0:T(8,128)S(1)}, u32[]{:S(2)}, u32[]{:S(2)}) collective-permute-start(f32[256,1024]{1,0:T(8,128)S(1)} %pad_maximum_fusion.2), channel_id=1, source_target_pairs={{0,96},{2,98},{4,100},{6,102},{8,40},{10,42},{12,44},{14,46},{16,1... | collective-permute-start | bytes 3145736 | tf_op jit(solution)/shard_map/ppermute | solution.py:26
  36.2 1.2 collective-permute-start.12
  37.4 4.5 %collective-permute-done.10 = f32[256,512]{1,0:T(8,128)S(1)} collective-permute-done((f32[256,512]{1,0:T(8,128)S(1)}, f32[256,512]{1,0:T(8,128)S(1)}, u32[]{:S(2)}, u32[]{:S(2)}) %collective-permute-start.10) | collective-permute-done | bytes 524320 | tf_op jit(solution)/shard_map/ppermute | solution.py:26
  42.0 2.5 %collective-permute-done.12 = f32[256,512]{1,0:T(8,128)S(1)} collective-permute-done((f32[256,512]{1,0:T(8,128)S(1)}, f32[256,512]{1,0:T(8,128)S(1)}, u32[]{:S(2)}, u32[]{:S(2)}) %collective-permute-start.12) | collective-permute-done | bytes 524320 | tf_op jit(solution)/shard_map/ppermute | solution.py:26
  44.6 4.1 %collective-permute-done.11 = f32[256,1024]{1,0:T(8,128)S(1)} collective-permute-done((f32[256,1024]{1,0:T(8,128)S(1)}, f32[256,1024]{1,0:T(8,128)S(1)}, u32[]{:S(2)}, u32[]{:S(2)}) %collective-permute-start.11) | collective-permute-done | bytes 1048608 | tf_op jit(solution)/shard_map/ppermute | solution.py:26
  48.8 8.3 %collective-permute-start.15 = (f32[512,1024]{1,0:T(8,128)S(1)}, f32[512,1024]{1,0:T(8,128)S(1)}, u32[]{:S(2)}, u32[]{:S(2)}) collective-permute-start(f32[512,1024]{1,0:T(8,128)S(1)} %pad_maximum_fusion.1), channel_id=1, source_target_pairs={{0,8},{2,10},{4,12},{6,14},{8,0},{10,2},{12,4},{14,6},{16,24},{18,... | collective-permute-start | bytes 6291464 | tf_op jit(solution)/shard_map/ppermute | solution.py:26
  57.4 3.6 %collective-permute-done.15 = f32[512,1024]{1,0:T(8,128)S(1)} collective-permute-done((f32[512,1024]{1,0:T(8,128)S(1)}, f32[512,1024]{1,0:T(8,128)S(1)}, u32[]{:S(2)}, u32[]{:S(2)}) %collective-permute-start.15) | collective-permute-done | bytes 2097184 | tf_op jit(solution)/shard_map/ppermute | solution.py:26
  61.4 0.6 copy.17
  62.0 3.5 %collective-permute-done.13 = f32[256,512]{1,0:T(8,128)S(1)} collective-permute-done((f32[256,512]{1,0:T(8,128)S(1)}, f32[256,512]{1,0:T(8,128)S(1)}, u32[]{:S(2)}, u32[]{:S(2)}) %collective-permute-start.13) | collective-permute-done | bytes 524320 | tf_op jit(solution)/shard_map/ppermute | solution.py:26
  65.5 3.6 %fusion = f32[512,1024]{1,0:T(8,128)S(1)} fusion(f32[1024,1024]{1,0:T(8,128)S(1)} %bitcast.68, f32[128,1024]{1,0:T(8,128)S(1)} %collective-permute-done.14, f32[128,1024]{1,0:T(8,128)S(1)} %maximum_maximum_fusion, f32[256,512]{1,0:T(8,128)S(1)} %collective-permute-done.13, f32[256,512]{1,0:T(8,128)S(1)} %pad_maximum_fusion.11), kind=kOutput, calls=%fused_computation.2 | convolution fusion | flops 3222798336 | bytes 8388608 | tf_op jit(solution)/shard_map/vc,cn->vn/dot_general | solution.py:51
  69.1 3.0 %collective-permute-start.16 = (f32[512,1024]{1,0:T(8,128)S(1)}, f32[512,1024]{1,0:T(8,128)S(1)}, u32[]{:S(2)}, u32[]{:S(2)}) collective-permute-start(f32[512,1024]{1,0:T(8,128)S(1)} %fusion), channel_id=1, source_target_pairs={{0,8},{2,10},{4,12},{6,14},{8,0},{10,2},{12,4},{14,6},{16,24},{18,... | collective-permute-start | bytes 6291464 | tf_op jit(solution)/shard_map/ppermute | solution.py:26
  72.2 3.6 %collective-permute-done.16 = f32[512,1024]{1,0:T(8,128)S(1)} collective-permute-done((f32[512,1024]{1,0:T(8,128)S(1)}, f32[512,1024]{1,0:T(8,128)S(1)}, u32[]{:S(2)}, u32[]{:S(2)}) %collective-permute-start.16) | collective-permute-done | bytes 2097184 | tf_op jit(solution)/shard_map/ppermute | solution.py:26
  75.9 2.0 %fusion.14 = f32[512,1024]{1,0:T(8,128)S(1)} fusion(f32[512,1024]{1,0:T(8,128)S(1)} %collective-permute-done.16, f32[256,512]{1,0:T(8,128)S(1)} %bitcast.76, f32[256,512]{1,0:T(8,128)S(1)} %bitcast.74), kind=kOutput, calls=%fused_computation.21 | convolution fusion | flops 1610874880 | bytes 5242880 | tf_op jit(solution)/shard_map/vm,vn->mn/dot_general | solution.py:51
  77.8 1.9 %fusion.10 = f32[512,1024]{1,0:T(8,128)S(1)} fusion(f32[512,1024]{1,0:T(8,128)S(1)} %copy-done, f32[512,1024]{1,0:T(8,128)S(1)} %fusion.14, f32[256,512]{1,0:T(8,128)S(1)} %bitcast.77, f32[256,512]{1,0:T(8,128)S(1)} %bitcast.75), kind=kOutput, calls=%fused_computation.13 | convolution fusion | flops 1611399168 | bytes 7340032 | tf_op jit(solution)/shard_map/vm,mn->vn/dot_general | solution.py:51
  80.3 1.9 %fusion.15 = f32[512,1024]{1,0:T(8,128)S(1)} fusion(f32[512,1024]{1,0:T(8,128)S(1)} %fusion, f32[256,512]{1,0:T(8,128)S(1)} %bitcast.80, f32[256,512]{1,0:T(8,128)S(1)} %bitcast.78), kind=kOutput, calls=%fused_computation.22 | convolution fusion | flops 1610874880 | bytes 5242880 | tf_op jit(solution)/shard_map/vm,vn->mn/dot_general | solution.py:51
  82.2 1.9 %fusion.12 = f32[512,1024]{1,0:T(8,128)S(1)} fusion(f32[512,1024]{1,0:T(8,128)S(1)} %copy-done, f32[512,1024]{1,0:T(8,128)S(1)} %fusion.15, f32[256,512]{1,0:T(8,128)S(1)} %bitcast.81, f32[256,512]{1,0:T(8,128)S(1)} %bitcast.79), kind=kOutput, calls=%fused_computation.15 | convolution fusion | flops 1611399168 | bytes 7340032 | tf_op jit(solution)/shard_map/vm,mn->vn/dot_general | solution.py:51
  84.2 3.5 %fusion.8 = f32[512,1024]{1,0:T(8,128)S(1)} fusion(f32[1024,1024]{1,0:T(8,128)S(1)} %bitcast.69, f32[512,1024]{1,0:T(8,128)S(1)} %fusion.12, f32[512,1024]{1,0:T(8,128)S(1)} %collective-permute-done.17), kind=kOutput, calls=%fused_computation.11 | convolution fusion | flops 3221749760 | bytes 10485760 | tf_op jit(solution)/shard_map/vn,cn->vc/dot_general | solution.py:51
  88.2 8.0 %collective-permute-done.18 = f32[256,512]{1,0:T(8,128)S(1)} collective-permute-done((f32[256,512]{1,0:T(8,128)S(1)}, f32[256,512]{1,0:T(8,128)S(1)}, u32[]{:S(2)}, u32[]{:S(2)}) %collective-permute-start.18) | collective-permute-done | bytes 524320 | tf_op jit(solution)/shard_map/ppermute | solution.py:26
  96.6 1.2 collective-permute-start.21
  97.9 3.7 %collective-permute-done.19 = f32[2,64,512]{2,1,0:T(8,128)S(1)} collective-permute-done((f32[2,64,512]{2,1,0:T(8,128)S(1)}, f32[2,64,512]{2,1,0:T(8,128)S(1)}, u32[]{:S(2)}, u32[]{:S(2)}) %collective-permute-start.19) | collective-permute-done | bytes 262176 | tf_op jit(solution)/shard_map/ppermute | solution.py:26
  102.6 6.2 %collective-permute-done.22 = f32[4,32,512]{2,1,0:T(8,128)S(1)} collective-permute-done((f32[4,32,512]{2,1,0:T(8,128)S(1)}, f32[4,32,512]{2,1,0:T(8,128)S(1)}, u32[]{:S(2)}, u32[]{:S(2)}) %collective-permute-start.22) | collective-permute-done | bytes 262176 | tf_op jit(solution)/shard_map/ppermute | solution.py:26
  109.0 0.8 slice_reduce_fusion
  109.8 2.2 %collective-permute-start.23 = (f32[128,256]{1,0:T(8,128)S(1)}, f32[128,256]{1,0:T(8,128)S(1)}, u32[]{:S(2)}, u32[]{:S(2)}) collective-permute-start(f32[128,256]{1,0:T(8,128)S(1)} %bitcast.98), channel_id=1, source_target_pairs={{0,32},{2,34},{4,36},{6,38},{8,104},{10,106},{12,108},{14,110},{16... | collective-permute-start | bytes 393224 | tf_op jit(solution)/shard_map/ppermute | solution.py:26
  112.2 2.8 %collective-permute-done.23 = f32[128,256]{1,0:T(8,128)S(1)} collective-permute-done((f32[128,256]{1,0:T(8,128)S(1)}, f32[128,256]{1,0:T(8,128)S(1)}, u32[]{:S(2)}, u32[]{:S(2)}) %collective-permute-start.23) | collective-permute-done | bytes 131104 | tf_op jit(solution)/shard_map/ppermute | solution.py:26
  115.0 0.6 collective-permute-start.24
  115.6 4.1 %collective-permute-done.24 = f32[2,32,256]{2,1,0:T(8,128)S(1)} collective-permute-done((f32[2,32,256]{2,1,0:T(8,128)S(1)}, f32[2,32,256]{2,1,0:T(8,128)S(1)}, u32[]{:S(2)}, u32[]{:S(2)}) %collective-permute-start.24) | collective-permute-done | bytes 65568 | tf_op jit(solution)/shard_map/ppermute | solution.py:26
  119.7 0.7 collective-permute-start.25
  120.4 2.2 %collective-permute-done.25 = f32[64,128]{1,0:T(8,128)S(1)} collective-permute-done((f32[64,128]{1,0:T(8,128)S(1)}, f32[64,128]{1,0:T(8,128)S(1)}, u32[]{:S(2)}, u32[]{:S(2)}) %collective-permute-start.25) | collective-permute-done | bytes 32800 | tf_op jit(solution)/shard_map/ppermute | solution.py:26
  122.6 9.2 %collective-permute-start.26 = (f32[64,64]{1,0:T(8,128)S(1)}, f32[64,64]{1,0:T(8,128)S(1)}, u32[]{:S(2)}, u32[]{:S(2)}) collective-permute-start(f32[64,64]{1,0:T(8,128)S(1)} %slice.148), channel_id=1, source_target_pairs={{0,8},{2,10},{4,12},{6,14},{8,0},{10,2},{12,4},{14,6},{16,24},{18,... | collective-permute-start | bytes 49160 | tf_op jit(solution)/shard_map/ppermute | solution.py:26
  131.8 0.9 collective-permute-done.26
  132.7 0.6 pad_maximum_fusion.20
  (66 shorter events, 5.2 us)
Async XLA Ops:
  0.8 2.3 %collective-permute-start = (f32[64,64]{1,0:T(8,128)S(1)}, f32[64,64]{1,0:T(8,128)S(1)}, u32[]{:S(2)}, u32[]{:S(2)}) collective-permute-start(f32[64,64]{1,0:T(8,128)S(1)} %get-tuple-element.42), channel_id=1, source_target_pairs={{0,8},{2,10},{4,12},{6,14},{8,0},{10,2},{12,4},{14,6},{16,24},{18,... | collective-permute-start | bytes 49160 | tf_op jit(solution)/shard_map/ppermute | solution.py:26
  3.1 5.2 %collective-permute-start.1 = (f32[2,32,128]{2,1,0:T(8,128)S(1)}, f32[2,32,128]{2,1,0:T(8,128)S(1)}, u32[]{:S(2)}, u32[]{:S(2)}) collective-permute-start(f32[2,32,128]{2,1,0:T(8,128)S(1)} %pad_maximum_fusion.21), channel_id=1, source_target_pairs={{0,32},{2,34},{4,36},{6,38},{8,104},{10,106},{12,108},{14,110},{16... | collective-permute-start | bytes 98312 | tf_op jit(solution)/shard_map/ppermute | solution.py:26
  8.4 4.5 %collective-permute-start.2 = (f32[2,32,256]{2,1,0:T(8,128)S(1)}, f32[2,32,256]{2,1,0:T(8,128)S(1)}, u32[]{:S(2)}, u32[]{:S(2)}) collective-permute-start(f32[2,32,256]{2,1,0:T(8,128)S(1)} %pad_maximum_fusion.19), channel_id=1, source_target_pairs={{0,2},{2,0},{4,6},{6,4},{8,14},{10,12},{12,10},{14,8},{16,18},{18,... | collective-permute-start | bytes 196616 | tf_op jit(solution)/shard_map/ppermute | solution.py:26
  11.2 7.4 %collective-permute-start.3 = (f32[64,1024]{1,0:T(8,128)}, f32[64,1024]{1,0:T(8,128)S(1)}, u32[]{:S(2)}, u32[]{:S(2)}) collective-permute-start(f32[64,1024]{1,0:T(8,128)} %param.6), channel_id=1, source_target_pairs={{0,16},{2,18},{4,20},{6,22},{8,24},{10,26},{12,28},{14,30},{16,0},... | collective-permute-start | bytes 786440 | tf_op jit(solution)/shard_map/ppermute | solution.py:26
  12.4 5.2 %collective-permute-start.4 = (f32[64,512]{1,0:T(8,128)}, f32[64,512]{1,0:T(8,128)S(1)}, u32[]{:S(2)}, u32[]{:S(2)}) collective-permute-start(f32[64,512]{1,0:T(8,128)} %param.5), channel_id=1, source_target_pairs={{0,2},{2,0},{4,6},{6,4},{8,14},{10,12},{12,10},{14,8},{16,18},{18,... | collective-permute-start | bytes 393224 | tf_op jit(solution)/shard_map/ppermute | solution.py:26
  19.6 4.5 %collective-permute-start.5 = (f32[2,64,256]{2,1,0:T(8,128)S(1)}, f32[2,64,256]{2,1,0:T(8,128)S(1)}, u32[]{:S(2)}, u32[]{:S(2)}) collective-permute-start(f32[2,64,256]{2,1,0:T(8,128)S(1)} %pad_maximum_fusion.18), channel_id=1, source_target_pairs={{0,16},{2,18},{4,20},{6,22},{8,24},{10,26},{12,28},{14,30},{16,0},... | collective-permute-start | bytes 393224 | tf_op jit(solution)/shard_map/ppermute | solution.py:26
  20.2 11.2 %collective-permute-start.8 = (f32[128,1024]{1,0:T(8,128)S(1)}, f32[128,1024]{1,0:T(8,128)S(1)}, u32[]{:S(2)}, u32[]{:S(2)}) collective-permute-start(f32[128,1024]{1,0:T(8,128)S(1)} %pad_maximum_fusion.12), channel_id=1, source_target_pairs={{0,32},{2,34},{4,36},{6,38},{8,104},{10,106},{12,108},{14,110},{16... | collective-permute-start | bytes 1572872 | tf_op jit(solution)/shard_map/ppermute | solution.py:26
  24.2 5.7 %collective-permute-start.7 = (f32[64,512]{1,0:T(8,128)S(1)}, f32[64,512]{1,0:T(8,128)S(1)}, u32[]{:S(2)}, u32[]{:S(2)}) collective-permute-start(f32[64,512]{1,0:T(8,128)S(1)} %get-tuple-element.37), channel_id=1, source_target_pairs={{0,96},{2,98},{4,100},{6,102},{8,40},{10,42},{12,44},{14,46},{16,1... | collective-permute-start | bytes 393224 | tf_op jit(solution)/shard_map/ppermute | solution.py:26
  24.3 7.0 %collective-permute-start.9 = (f32[128,512]{1,0:T(8,128)S(1)}, f32[128,512]{1,0:T(8,128)S(1)}, u32[]{:S(2)}, u32[]{:S(2)}) collective-permute-start(f32[128,512]{1,0:T(8,128)S(1)} %pad_maximum_fusion.15), channel_id=1, source_target_pairs={{0,1},{2,3},{4,5},{6,7},{8,9},{10,11},{12,13},{14,15},{16,17},{18,... | collective-permute-start | bytes 786440 | tf_op jit(solution)/shard_map/ppermute | solution.py:26
  27.1 4.1 %collective-permute-start.6 = (f32[64,512]{1,0:T(8,128)S(1)}, f32[64,512]{1,0:T(8,128)S(1)}, u32[]{:S(2)}, u32[]{:S(2)}) collective-permute-start(f32[64,512]{1,0:T(8,128)S(1)} %get-tuple-element.38), channel_id=1, source_target_pairs={{0,6},{2,4},{4,2},{6,0},{8,10},{10,8},{12,14},{14,12},{16,22},{18,... | collective-permute-start | bytes 393224 | tf_op jit(solution)/shard_map/ppermute | solution.py:26
  31.6 10.4 %collective-permute-start.10 = (f32[256,512]{1,0:T(8,128)S(1)}, f32[256,512]{1,0:T(8,128)S(1)}, u32[]{:S(2)}, u32[]{:S(2)}) collective-permute-start(f32[256,512]{1,0:T(8,128)S(1)} %fusion.16), channel_id=1, source_target_pairs={{0,1},{2,3},{4,5},{6,7},{8,9},{10,11},{12,13},{14,15},{16,17},{18,... | collective-permute-start | bytes 1572872 | tf_op jit(solution)/shard_map/ppermute | solution.py:26
  34.4 14.3 %collective-permute-start.11 = (f32[256,1024]{1,0:T(8,128)S(1)}, f32[256,1024]{1,0:T(8,128)S(1)}, u32[]{:S(2)}, u32[]{:S(2)}) collective-permute-start(f32[256,1024]{1,0:T(8,128)S(1)} %pad_maximum_fusion.2), channel_id=1, source_target_pairs={{0,96},{2,98},{4,100},{6,102},{8,40},{10,42},{12,44},{14,46},{16,1... | collective-permute-start | bytes 3145736 | tf_op jit(solution)/shard_map/ppermute | solution.py:26
  36.2 8.3 %collective-permute-start.12 = (f32[256,512]{1,0:T(8,128)S(1)}, f32[256,512]{1,0:T(8,128)S(1)}, u32[]{:S(2)}, u32[]{:S(2)}) collective-permute-start(f32[256,512]{1,0:T(8,128)S(1)} %pad_maximum_fusion.13), channel_id=1, source_target_pairs={{0,6},{2,4},{4,2},{6,0},{8,10},{10,8},{12,14},{14,12},{16,22},{18,... | collective-permute-start | bytes 1572872 | tf_op jit(solution)/shard_map/ppermute | solution.py:26
  48.8 12.1 %collective-permute-start.15 = (f32[512,1024]{1,0:T(8,128)S(1)}, f32[512,1024]{1,0:T(8,128)S(1)}, u32[]{:S(2)}, u32[]{:S(2)}) collective-permute-start(f32[512,1024]{1,0:T(8,128)S(1)} %pad_maximum_fusion.1), channel_id=1, source_target_pairs={{0,8},{2,10},{4,12},{6,14},{8,0},{10,2},{12,4},{14,6},{16,24},{18,... | collective-permute-start | bytes 6291464 | tf_op jit(solution)/shard_map/ppermute | solution.py:26
  57.2 8.3 %collective-permute-start.13 = (f32[256,512]{1,0:T(8,128)S(1)}, f32[256,512]{1,0:T(8,128)S(1)}, u32[]{:S(2)}, u32[]{:S(2)}) collective-permute-start(f32[256,512]{1,0:T(8,128)S(1)} %pad_maximum_fusion.11), channel_id=1, source_target_pairs={{0,96},{2,98},{4,100},{6,102},{8,40},{10,42},{12,44},{14,46},{16,1... | collective-permute-start | bytes 1572872 | tf_op jit(solution)/shard_map/ppermute | solution.py:26
  57.2 8.3 %collective-permute-start.14 = (f32[128,1024]{1,0:T(8,128)S(1)}, f32[128,1024]{1,0:T(8,128)S(1)}, u32[]{:S(2)}, u32[]{:S(2)}) collective-permute-start(f32[128,1024]{1,0:T(8,128)S(1)} %maximum_maximum_fusion), channel_id=1, source_target_pairs={{0,6},{2,4},{4,2},{6,0},{8,10},{10,8},{12,14},{14,12},{16,22},{18,... | collective-permute-start | bytes 1572872 | tf_op jit(solution)/shard_map/ppermute | solution.py:26
  69.1 6.8 %collective-permute-start.16 = (f32[512,1024]{1,0:T(8,128)S(1)}, f32[512,1024]{1,0:T(8,128)S(1)}, u32[]{:S(2)}, u32[]{:S(2)}) collective-permute-start(f32[512,1024]{1,0:T(8,128)S(1)} %fusion), channel_id=1, source_target_pairs={{0,8},{2,10},{4,12},{6,14},{8,0},{10,2},{12,4},{14,6},{16,24},{18,... | collective-permute-start | bytes 6291464 | tf_op jit(solution)/shard_map/ppermute | solution.py:26
  75.9 2.0 %copy-start = (f32[512,1024]{1,0:T(8,128)S(1)}, f32[512,1024]{1,0:T(8,128)}, u32[]{:S(2)}) copy-start(f32[512,1024]{1,0:T(8,128)} %param.7) | copy-start | bytes 6291460
  79.7 4.4 %collective-permute-start.17 = (f32[512,1024]{1,0:T(8,128)S(1)}, f32[512,1024]{1,0:T(8,128)S(1)}, u32[]{:S(2)}, u32[]{:S(2)}) collective-permute-start(f32[512,1024]{1,0:T(8,128)S(1)} %fusion.10), channel_id=1, source_target_pairs={{0,8},{2,10},{4,12},{6,14},{8,0},{10,2},{12,4},{14,6},{16,24},{18,... | collective-permute-start | bytes 6291464 | tf_op jit(solution)/shard_map/ppermute | solution.py:26
  87.8 8.4 %collective-permute-start.18 = (f32[256,512]{1,0:T(8,128)S(1)}, f32[256,512]{1,0:T(8,128)S(1)}, u32[]{:S(2)}, u32[]{:S(2)}) collective-permute-start(f32[256,512]{1,0:T(8,128)S(1)} %slice.132), channel_id=1, source_target_pairs={{0,96},{2,98},{4,100},{6,102},{8,40},{10,42},{12,44},{14,46},{16,1... | collective-permute-start | bytes 1572872 | tf_op jit(solution)/shard_map/ppermute | solution.py:26
  87.9 8.6 %collective-permute-start.20 = (f32[128,1024]{1,0:T(8,128)S(1)}, f32[128,1024]{1,0:T(8,128)S(1)}, u32[]{:S(2)}, u32[]{:S(2)}) collective-permute-start(f32[128,1024]{1,0:T(8,128)S(1)} %slice.136), channel_id=1, source_target_pairs={{0,6},{2,4},{4,2},{6,0},{8,10},{10,8},{12,14},{14,12},{16,22},{18,... | collective-permute-start | bytes 1572872 | tf_op jit(solution)/shard_map/ppermute | solution.py:26
  96.3 5.3 %collective-permute-start.19 = (f32[2,64,512]{2,1,0:T(8,128)S(1)}, f32[2,64,512]{2,1,0:T(8,128)S(1)}, u32[]{:S(2)}, u32[]{:S(2)}) collective-permute-start(f32[2,64,512]{2,1,0:T(8,128)S(1)} %slice_bitcast_fusion.4), channel_id=1, source_target_pairs={{0,6},{2,4},{4,2},{6,0},{8,10},{10,8},{12,14},{14,12},{16,22},{18,... | collective-permute-start | bytes 786440 | tf_op jit(solution)/shard_map/ppermute | solution.py:26
  96.6 5.3 %collective-permute-start.21 = (f32[128,512]{1,0:T(8,128)S(1)}, f32[128,512]{1,0:T(8,128)S(1)}, u32[]{:S(2)}, u32[]{:S(2)}) collective-permute-start(f32[128,512]{1,0:T(8,128)S(1)} %slice.138), channel_id=1, source_target_pairs={{0,96},{2,98},{4,100},{6,102},{8,40},{10,42},{12,44},{14,46},{16,1... | collective-permute-start | bytes 786440 | tf_op jit(solution)/shard_map/ppermute | solution.py:26
  102.1 6.7 %collective-permute-start.22 = (f32[4,32,512]{2,1,0:T(8,128)S(1)}, f32[4,32,512]{2,1,0:T(8,128)S(1)}, u32[]{:S(2)}, u32[]{:S(2)}) collective-permute-start(f32[4,32,512]{2,1,0:T(8,128)S(1)} %slice_bitcast_fusion.2), channel_id=1, source_target_pairs={{0,2},{2,0},{4,6},{6,4},{8,14},{10,12},{12,10},{14,8},{16,18},{18,... | collective-permute-start | bytes 786440 | tf_op jit(solution)/shard_map/ppermute | solution.py:26
  109.8 5.1 %collective-permute-start.23 = (f32[128,256]{1,0:T(8,128)S(1)}, f32[128,256]{1,0:T(8,128)S(1)}, u32[]{:S(2)}, u32[]{:S(2)}) collective-permute-start(f32[128,256]{1,0:T(8,128)S(1)} %bitcast.98), channel_id=1, source_target_pairs={{0,32},{2,34},{4,36},{6,38},{8,104},{10,106},{12,108},{14,110},{16... | collective-permute-start | bytes 393224 | tf_op jit(solution)/shard_map/ppermute | solution.py:26
  115.0 4.7 %collective-permute-start.24 = (f32[2,32,256]{2,1,0:T(8,128)S(1)}, f32[2,32,256]{2,1,0:T(8,128)S(1)}, u32[]{:S(2)}, u32[]{:S(2)}) collective-permute-start(f32[2,32,256]{2,1,0:T(8,128)S(1)} %slice.144), channel_id=1, source_target_pairs={{0,1},{2,3},{4,5},{6,7},{8,9},{10,11},{12,13},{14,15},{16,17},{18,... | collective-permute-start | bytes 196616 | tf_op jit(solution)/shard_map/ppermute | solution.py:26
  119.7 2.8 %collective-permute-start.25 = (f32[64,128]{1,0:T(8,128)S(1)}, f32[64,128]{1,0:T(8,128)S(1)}, u32[]{:S(2)}, u32[]{:S(2)}) collective-permute-start(f32[64,128]{1,0:T(8,128)S(1)} %slice.146), channel_id=1, source_target_pairs={{0,16},{2,18},{4,20},{6,22},{8,24},{10,26},{12,28},{14,30},{16,0},... | collective-permute-start | bytes 98312 | tf_op jit(solution)/shard_map/ppermute | solution.py:26
  122.6 10.1 %collective-permute-start.26 = (f32[64,64]{1,0:T(8,128)S(1)}, f32[64,64]{1,0:T(8,128)S(1)}, u32[]{:S(2)}, u32[]{:S(2)}) collective-permute-start(f32[64,64]{1,0:T(8,128)S(1)} %slice.148), channel_id=1, source_target_pairs={{0,8},{2,10},{4,12},{6,14},{8,0},{10,2},{12,4},{14,6},{16,24},{18,... | collective-permute-start | bytes 49160 | tf_op jit(solution)/shard_map/ppermute | solution.py:26

commit v3 on v2

v3 whole, which is shorter than its diff:
```python
import jax
import jax.numpy as jnp
from jax import lax
from jax.sharding import Mesh, PartitionSpec as P

AXES = ("z", "xl", "core", "y", "xh")
HIGH = lax.Precision.HIGH


def index(z, x, core, y):
    return (((z * 2 + x % 2) * 2 + core) * 4 + y) * 2 + x // 2


def flip(value, per_core):
    pairs = []
    for z in range(4):
        for x in range(4):
            for core in range(2):
                for y in range(4):
                    if per_core == "core":
                        target = index(z, x, 1 - core, y)
                    else:
                        dz, dx, dy = per_core[core]
                        target = index(z ^ dz, x ^ dx, core, y ^ dy)
                    pairs.append((index(z, x, core, y), target))
    return lax.ppermute(value, AXES, pairs)


Z1, Z3, Y1, Y3 = (1, 0, 0), (3, 0, 0), (0, 0, 1), (0, 0, 3)
X1, X2, X3 = (0, 1, 0), (0, 2, 0), (0, 3, 0)
ZA, ZB, YA, YB, XL, XH = (Z1, Z3), (Z3, Z1), (Y1, Y3), (Y3, Y1), (X1, X1), (X2, X2)
XA, XB = (X1, X3), (X3, X1)
XN = (X3, X3)


def grow(value, step, axis):
    return jnp.concatenate([value, flip(value, step)], axis=axis)


def alternate(value, axis, size):
    blocks = [lax.slice_in_dim(value, i, i + size, axis=axis) for i in range(0, value.shape[axis], size)]
    return jnp.concatenate(blocks[::2], axis=axis), jnp.concatenate(blocks[1::2], axis=axis)


def trade(value, step, axis, size):
    kept, sent = alternate(value, axis, size)
    return kept + flip(sent, step)


def dot(spec, a, b):
    return jnp.einsum(spec, a, b, precision=HIGH, preferred_element_type=jnp.float32)


def in_parts(v):
    first = v[:, :, :, :32].transpose(1, 0, 2, 3, 4).reshape(256, -1)
    second = v[:, :, :, 32:].transpose(0, 2, 1, 3, 4).reshape(256, -1)
    return jnp.concatenate([first, second], axis=0)


def square(core, own, near):
    size = own.shape[0]
    got = flip(jnp.concatenate([own, near], axis=0), XB)
    far, both = got[:size], got[size:]
    first = core == 0
    top = jnp.concatenate([own, jnp.where(first, near, far)], axis=1)
    bottom = jnp.concatenate([both, jnp.where(first, far, near)], axis=1)
    return top, bottom


def body(trials, valence, conduction, screened):
    core = lax.axis_index("core")
    mine = lax.dynamic_index_in_dim(trials, core, 0, keepdims=False)
    theirs = lax.dynamic_index_in_dim(trials, 1 - core, 0, keepdims=False)

    c = grow(conduction, XL, 0)
    v = grow(valence, YA, 0)
    t = jnp.concatenate([mine, flip(theirs, "core")], axis=1)
    t = t.reshape(2, 32, 128)
    t = grow(t, ZA, 2)
    t, v = lax.optimization_barrier((t, v))
    v = grow(v, XH, 0)
    t = grow(t, ZB, 2)
    t, c = lax.optimization_barrier((t, c))
    c = grow(c, ZA, 0)
    p, q = t[0], t[1]
    q_near = flip(q, XA)
    p = grow(p, YA, 0)
    p, q, q_near, v, c = lax.optimization_barrier((p, q, q_near, v, c))
    c_near = flip(c, "core")
    c_far = flip(c, ZB)
    q = jnp.concatenate(square(core, q, q_near), axis=0)
    p = grow(p, YB, 0)
    p, q = lax.optimization_barrier((p, q))
    p_near = flip(p, XA)
    q = grow(q, YA, 0)
    p, p_near, q, c_near, c_far = lax.optimization_barrier((p, p_near, q, c_near, c_far))
    v = grow(v, YB, 0)
    c_other = jnp.concatenate([c_near, flip(c_far, "core")], axis=0)
    c = jnp.concatenate([c, c_far], axis=0)
    p = jnp.concatenate(square(core, p, p_near), axis=0)
    q = grow(q, YB, 0)
    p, v = lax.optimization_barrier((p, v))

    c_own = c.reshape(2, 2, 2, 64, 1024).transpose(2, 0, 1, 3, 4)
    c_other = c_other.reshape(2, 2, 2, 64, 1024).transpose(2, 1, 0, 3, 4)
    c_all = jnp.stack([c_own, c_other], axis=3).reshape(1024, 1024)
    v = v.reshape(2, 2, 2, 64, 512)
    v_mine, v_theirs = in_parts(v), in_parts(v.swapaxes(0, 2))

    half_p = dot("vc,cn->vn", p, c_all)
    got_p = flip(half_p, "core")
    half_q = dot("vc,cn->vn", q, c_all)
    got_q = flip(half_q, "core")
    half_mine = jnp.concatenate([half_p, half_q], axis=0)
    half_theirs = jnp.concatenate([got_p, got_q], axis=0)
    pairs_mine = screened * dot("vm,vn->mn", v_mine, half_mine)
    pairs_theirs = screened * dot("vm,vn->mn", v_theirs, half_theirs)
    to_p = flip(dot("vm,mn->vn", v_theirs[:256], pairs_theirs), "core")
    to_q = flip(dot("vm,mn->vn", v_theirs[256:], pairs_theirs), "core")
    sums_p = dot("vm,mn->vn", v_mine[:256], pairs_mine) + to_p
    sums_q = dot("vm,mn->vn", v_mine[256:], pairs_mine) + to_q
    p = dot("vn,cn->vc", sums_p, c_all)
    q = dot("vn,cn->vc", sums_q, c_all)
    p = trade(p, ZB, 1, 256)
    q = trade(q, YB, 0, 128)
    p = trade(p, YB, 0, 64)
    q = trade(q, ZB, 1, 256)
    p_kept, p_sent = alternate(p, 0, 32)
    q_kept, q_sent = alternate(q, 0, 64)
    r = jnp.concatenate([p_kept, q_kept], axis=0) + flip(jnp.concatenate([p_sent, q_sent], axis=0), YA)
    r = trade(r, ZA, 1, 128)
    kept, sent = alternate(r, 0, 32)
    r = kept + flip(jnp.concatenate([sent[:, 128:], sent[:, :128]], axis=1), XN)
    r = trade(r, XL, 1, 128)
    kept = r[:, :64]
    got = flip(r[:, 64:], "core")
    first = core == 0
    return jnp.stack([jnp.where(first, kept, got), jnp.where(first, got, kept)])


def solution(mesh):
    split = Mesh(mesh.devices.reshape(4, 2, 2, 4, 2), AXES)
    row, col = ("z", "xl", "core"), ("y", "xh")
    placed = (P(None, col, row), P(col, row), P(row, col), P(row, col))
    return jax.shard_map(
        body, mesh=split, in_specs=placed, out_specs=P(None, col, row), check_vma=False
    )
```

time: 134 us -> 124 us (0.925)
  waiting for transfers between devices: 61 us -> 51.9 us
  starting transfers between devices: 50 us -> 46.9 us
  matrix products: 14.8 us -> 17 us
  other arithmetic: 3.9 us -> 5.79 us
    ppermute x27 -> x32, waiting for transfers between devices: 61 us -> 51.9 us  [flip(): return lax.ppermute(value, AXES, pairs)]
    ppermute x27 -> x32, starting transfers between devices: 50 us -> 46.9 us  [flip(): return lax.ppermute(value, AXES, pairs)]
    dot_general x6 -> x10, matrix products: 14.8 us -> 17 us  [dot(): jnp.einsum(spec, a, b, precision=HIGH, preferred_element_type=jnp.float32)]
    concatenate x3 -> x13, other arithmetic: 0.11 us -> 1.87 us  [the longest x1 1.4 us: body(): c = jnp.concatenate([c, c_far], axis=0)]
  transfers between devices with their start and end apart: 27 -> 32, of which waited for: 23 -> 21; matrix products, arithmetic and copies ran while one was open for 5% -> 16% of each run, Pallas kernels for 0% -> 0%
where the time goes in v3:
time: 124 us
  waiting for transfers between devices  51.9 us (42%)
  starting transfers between devices  46.9 us (38%)
  matrix products  17 us (14%)
  other arithmetic  5.79 us (5%)
  local copies, waits for them, and re-layouts  2.17 us (2%)
    ppermute x32, waiting for transfers between devices, flip(): return lax.ppermute(value, AXES, pairs)  51.9 us
    ppermute x32, starting transfers between devices, flip(): return lax.ppermute(value, AXES, pairs)  46.9 us
    dot_general x10, matrix products, dot(): jnp.einsum(spec, a, b, precision=HIGH, preferred_element_type=jnp.float32)  17 us
  transfers between devices with their start and end apart: 32, of which 21 were waited for; matrix products, arithmetic and copies ran while one was open for 16% of the time, Pallas kernels for 0%

profile of v3, /device:TPU:1, one launch (start us, length us, event | category | flops | bytes accessed | tf_op | source)
XLA Modules:
  0.0 124.2 jit_solution(13134772670136310881)
XLA Ops:
  0.8 1.4 %collective-permute-start = (f32[64,64]{1,0:T(8,128)S(1)}, f32[64,64]{1,0:T(8,128)S(1)}, u32[]{:S(2)}, u32[]{:S(2)}) collective-permute-start(f32[64,64]{1,0:T(8,128)S(1)} %get-tuple-element.82), channel_id=1, source_target_pairs={{0,8},{2,10},{4,12},{6,14},{8,0},{10,2},{12,4},{14,6},{16,24},{18,... | collective-permute-start | bytes 49160 | tf_op jit(solution)/shard_map/ppermute | solution.py:26
  3.1 3.9 %collective-permute-start.1 = (f32[2,32,128]{2,1,0:T(8,128)S(1)}, f32[2,32,128]{2,1,0:T(8,128)S(1)}, u32[]{:S(2)}, u32[]{:S(2)}) collective-permute-start(f32[2,32,128]{2,1,0:T(8,128)S(1)} %pad_maximum_fusion.22), channel_id=1, source_target_pairs={{0,32},{2,34},{4,36},{6,38},{8,104},{10,106},{12,108},{14,110},{16... | collective-permute-start | bytes 98312 | tf_op jit(solution)/shard_map/ppermute | solution.py:26
  7.0 2.7 %collective-permute-start.2 = (f32[64,512]{1,0:T(8,128)}, f32[64,512]{1,0:T(8,128)S(1)}, u32[]{:S(2)}, u32[]{:S(2)}) collective-permute-start(f32[64,512]{1,0:T(8,128)} %param.5), channel_id=1, source_target_pairs={{0,2},{2,0},{4,6},{6,4},{8,14},{10,12},{12,10},{14,8},{16,18},{18,... | collective-permute-start | bytes 393224 | tf_op jit(solution)/shard_map/ppermute | solution.py:26
  9.7 1.2 collective-permute-start.4
  11.0 1.3 %collective-permute-done.2 = f32[64,512]{1,0:T(8,128)S(1)} collective-permute-done((f32[64,512]{1,0:T(8,128)}, f32[64,512]{1,0:T(8,128)S(1)}, u32[]{:S(2)}, u32[]{:S(2)}) %collective-permute-start.2) | collective-permute-done | bytes 131104 | tf_op jit(solution)/shard_map/ppermute | solution.py:26
  12.3 0.9 pad_maximum_fusion.10
  13.3 2.8 %collective-permute-start.7 = (f32[128,512]{1,0:T(8,128)S(1)}, f32[128,512]{1,0:T(8,128)S(1)}, u32[]{:S(2)}, u32[]{:S(2)}) collective-permute-start(f32[128,512]{1,0:T(8,128)S(1)} %pad_maximum_fusion.10), channel_id=1, source_target_pairs={{0,1},{2,3},{4,5},{6,7},{8,9},{10,11},{12,13},{14,15},{16,17},{18,... | collective-permute-start | bytes 786440 | tf_op jit(solution)/shard_map/ppermute | solution.py:26
  16.7 1.0 pad_maximum_fusion.5
  17.7 1.7 %collective-permute-start.8 = (f32[128,1024]{1,0:T(8,128)S(1)}, f32[128,1024]{1,0:T(8,128)S(1)}, u32[]{:S(2)}, u32[]{:S(2)}) collective-permute-start(f32[128,1024]{1,0:T(8,128)S(1)} %pad_maximum_fusion.5), channel_id=1, source_target_pairs={{0,32},{2,34},{4,36},{6,38},{8,104},{10,106},{12,108},{14,110},{16... | collective-permute-start | bytes 1572872 | tf_op jit(solution)/shard_map/ppermute | solution.py:26
  19.4 1.2 collective-permute-start.5
  20.6 2.5 %collective-permute-start.6 = (f32[32,512]{1,0:T(8,128)S(1)}, f32[32,512]{1,0:T(8,128)S(1)}, u32[]{:S(2)}, u32[]{:S(2)}) collective-permute-start(f32[32,512]{1,0:T(8,128)S(1)} %get-tuple-element.28), channel_id=1, source_target_pairs={{0,16},{2,18},{4,20},{6,22},{8,25},{10,27},{12,29},{14,31},{16,0},... | collective-permute-start | bytes 196616 | tf_op jit(solution)/shard_map/ppermute | solution.py:26
  24.0 3.1 %collective-permute-done.8 = f32[128,1024]{1,0:T(8,128)S(1)} collective-permute-done((f32[128,1024]{1,0:T(8,128)S(1)}, f32[128,1024]{1,0:T(8,128)S(1)}, u32[]{:S(2)}, u32[]{:S(2)}) %collective-permute-start.8) | collective-permute-done | bytes 524320 | tf_op jit(solution)/shard_map/ppermute | solution.py:26
  27.3 2.9 %collective-permute-start.13 = (f32[256,1024]{1,0:T(8,128)S(1)}, f32[256,1024]{1,0:T(8,128)S(1)}, u32[]{:S(2)}, u32[]{:S(2)}) collective-permute-start(f32[256,1024]{1,0:T(8,128)S(1)} %pad_maximum_fusion.3), channel_id=1, source_target_pairs={{0,8},{2,10},{4,12},{6,14},{8,0},{10,2},{12,4},{14,6},{16,24},{18,... | collective-permute-start | bytes 3145736 | tf_op jit(solution)/shard_map/ppermute | solution.py:26
  30.2 1.3 %collective-permute-start.10 = (f32[64,512]{1,0:T(8,128)S(1)}, f32[64,512]{1,0:T(8,128)S(1)}, u32[]{:S(2)}, u32[]{:S(2)}) collective-permute-start(f32[64,512]{1,0:T(8,128)S(1)} %pad_maximum_fusion.17), channel_id=1, source_target_pairs={{0,17},{2,19},{4,21},{6,23},{8,24},{10,26},{12,28},{14,30},{16,1},... | collective-permute-start | bytes 393224 | tf_op jit(solution)/shard_map/ppermute | solution.py:26
  31.5 1.3 %collective-permute-start.9 = (f32[64,512]{1,0:T(8,128)S(1)}, f32[64,512]{1,0:T(8,128)S(1)}, u32[]{:S(2)}, u32[]{:S(2)}) collective-permute-start(f32[64,512]{1,0:T(8,128)S(1)} %pad_maximum_fusion.16), channel_id=1, source_target_pairs={{0,6},{2,4},{4,2},{6,0},{8,10},{10,8},{12,14},{14,12},{16,22},{18,... | collective-permute-start | bytes 393224 | tf_op jit(solution)/shard_map/ppermute | solution.py:26
  32.8 1.7 %collective-permute-done.10 = f32[64,512]{1,0:T(8,128)S(1)} collective-permute-done((f32[64,512]{1,0:T(8,128)S(1)}, f32[64,512]{1,0:T(8,128)S(1)}, u32[]{:S(2)}, u32[]{:S(2)}) %collective-permute-start.10) | collective-permute-done | bytes 131104 | tf_op jit(solution)/shard_map/ppermute | solution.py:26
  34.5 1.2 collective-permute-done.9
  35.7 2.8 %collective-permute-start.12 = (f32[64,1024]{1,0:T(8,128)S(1)}, f32[64,1024]{1,0:T(8,128)S(1)}, u32[]{:S(2)}, u32[]{:S(2)}) collective-permute-start(f32[64,1024]{1,0:T(8,128)S(1)} %maximum_maximum_fusion.1), channel_id=1, source_target_pairs={{0,2},{2,0},{4,6},{6,4},{8,14},{10,12},{12,10},{14,8},{16,18},{18,... | collective-permute-start | bytes 786440 | tf_op jit(solution)/shard_map/ppermute | solution.py:26
  38.5 1.8 %collective-permute-start.11 = (f32[128,512]{1,0:T(8,128)S(1)}, f32[128,512]{1,0:T(8,128)S(1)}, u32[]{:S(2)}, u32[]{:S(2)}) collective-permute-start(f32[128,512]{1,0:T(8,128)S(1)} %pad_maximum_fusion.11), channel_id=1, source_target_pairs={{0,16},{2,18},{4,20},{6,22},{8,25},{10,27},{12,29},{14,31},{16,0},... | collective-permute-start | bytes 786440 | tf_op jit(solution)/shard_map/ppermute | solution.py:26
  40.4 2.3 %collective-permute-done.12 = f32[64,1024]{1,0:T(8,128)S(1)} collective-permute-done((f32[64,1024]{1,0:T(8,128)S(1)}, f32[64,1024]{1,0:T(8,128)S(1)}, u32[]{:S(2)}, u32[]{:S(2)}) %collective-permute-start.12) | collective-permute-done | bytes 262176 | tf_op jit(solution)/shard_map/ppermute | solution.py:26
  42.7 2.5 %collective-permute-done.11 = f32[128,512]{1,0:T(8,128)S(1)} collective-permute-done((f32[128,512]{1,0:T(8,128)S(1)}, f32[128,512]{1,0:T(8,128)S(1)}, u32[]{:S(2)}, u32[]{:S(2)}) %collective-permute-start.11) | collective-permute-done | bytes 262176 | tf_op jit(solution)/shard_map/ppermute | solution.py:26
  45.3 2.9 %collective-permute-start.17 = (f32[256,1024]{1,0:T(8,128)}, f32[256,1024]{1,0:T(8,128)S(1)}, u32[]{:S(2)}, u32[]{:S(2)}) collective-permute-start(f32[256,1024]{1,0:T(8,128)} %collective-permute-done.14), channel_id=1, source_target_pairs={{0,8},{2,10},{4,12},{6,14},{8,0},{10,2},{12,4},{14,6},{16,24},{18,... | collective-permute-start | bytes 3145736 | tf_op jit(solution)/shard_map/ppermute | solution.py:26
  48.3 2.3 %collective-permute-done.16 = f32[256,512]{1,0:T(8,128)S(1)} collective-permute-done((f32[256,512]{1,0:T(8,128)S(1)}, f32[256,512]{1,0:T(8,128)S(1)}, u32[]{:S(2)}, u32[]{:S(2)}) %collective-permute-start.16) | collective-permute-done | bytes 524320 | tf_op jit(solution)/shard_map/ppermute | solution.py:26
  50.8 1.4 %pad_maximum_fusion.1 = f32[512,1024]{1,0:T(8,128)S(1)} fusion(f32[256,1024]{1,0:T(8,128)} %collective-permute-done.14, f32[256,1024]{1,0:T(8,128)S(1)} %pad_maximum_fusion.3), kind=kLoop, calls=%fused_computation.1 | loop fusion | flops 524288 | bytes 4194304 | tf_op jit(solution)/shard_map/concatenate | solution.py:99
  52.3 4.3 %collective-permute-done.15 = f32[256,512]{1,0:T(8,128)S(1)} collective-permute-done((f32[256,512]{1,0:T(8,128)S(1)}, f32[256,512]{1,0:T(8,128)S(1)}, u32[]{:S(2)}, u32[]{:S(2)}) %collective-permute-start.15) | collective-permute-done | bytes 524320 | tf_op jit(solution)/shard_map/ppermute | solution.py:26
  58.3 2.1 %fusion.36 = f32[256,1024]{1,0:T(8,128)S(1)} fusion(f32[256,1024]{1,0:T(8,128)S(1)} %maximum_maximum_fusion, f32[1024,1024]{1,0:T(8,128)S(1)} %bitcast.54), kind=kOutput, calls=%fused_computation.84 | convolution fusion | flops 1610612736 | bytes 6291456 | tf_op jit(solution)/shard_map/vc,cn->vn/dot_general | solution.py:51
  60.3 2.2 %collective-permute-start.19 = (f32[256,1024]{1,0:T(8,128)S(1)}, f32[256,1024]{1,0:T(8,128)S(1)}, u32[]{:S(2)}, u32[]{:S(2)}) collective-permute-start(f32[256,1024]{1,0:T(8,128)S(1)} %fusion.36), channel_id=1, source_target_pairs={{0,8},{2,10},{4,12},{6,14},{8,0},{10,2},{12,4},{14,6},{16,24},{18,... | collective-permute-start | bytes 3145736 | tf_op jit(solution)/shard_map/ppermute | solution.py:26
  62.5 2.1 %fusion.17 = f32[256,1024]{1,0:T(8,128)S(1)} fusion(f32[1024,1024]{1,0:T(8,128)S(1)} %bitcast.55, f32[128,1024]{1,0:T(8,128)S(1)} %collective-permute-done.18, f32[128,1024]{1,0:T(8,128)S(1)} %pad_maximum_fusion.7), kind=kOutput, calls=%fused_computation.22 | convolution fusion | flops 1610874880 | bytes 6291456 | tf_op jit(solution)/shard_map/vc,cn->vn/dot_general | solution.py:51
  65.0 2.4 %collective-permute-done.20 = f32[256,1024]{1,0:T(8,128)S(1)} collective-permute-done((f32[256,1024]{1,0:T(8,128)S(1)}, f32[256,1024]{1,0:T(8,128)S(1)}, u32[]{:S(2)}, u32[]{:S(2)}) %collective-permute-start.20) | collective-permute-done | bytes 1048608 | tf_op jit(solution)/shard_map/ppermute | solution.py:26
  67.5 2.0 %fusion.8 = f32[512,1024]{1,0:T(8,128)S(1)} fusion(f32[512,1024]{1,0:T(8,128)S(1)} %copy-done, f32[256,1024]{1,0:T(8,128)S(1)} %collective-permute-done.20, f32[256,1024]{1,0:T(8,128)S(1)} %collective-permute-done.19, f32[256,512]{1,0:T(8,128)S(1)} %bitcast.65, f32[256,512]{1,0:T(8,128)S(1)} %bitcast.69), kind=kOutput, calls=%fused_computation.12 | convolution fusion | flops 1611923456 | bytes 7340032 | tf_op jit(solution)/shard_map/vm,vn->mn/dot_general | solution.py:51
  69.5 1.2 fusion.37
  71.1 2.0 %fusion.11 = f32[512,1024]{1,0:T(8,128)S(1)} fusion(f32[512,1024]{1,0:T(8,128)S(1)} %copy-done, f32[256,1024]{1,0:T(8,128)S(1)} %fusion.17, f32[256,1024]{1,0:T(8,128)S(1)} %fusion.36, f32[256,512]{1,0:T(8,128)S(1)} %bitcast.63, f32[256,512]{1,0:T(8,128)S(1)} %bitcast.67), kind=kOutput, calls=%fused_computation.13 | convolution fusion | flops 1611923456 | bytes 7340032 | tf_op jit(solution)/shard_map/vm,vn->mn/dot_general | solution.py:51
  73.1 1.2 fusion.39
  74.7 1.2 convolution_add_fusion.1
  75.9 2.0 %fusion.38 = f32[256,1024]{1,0:T(8,128)S(1)} fusion(f32[256,1024]{1,0:T(8,128)S(1)} %convolution_add_fusion.1, f32[1024,1024]{1,0:T(8,128)S(1)} %bitcast.56), kind=kOutput, calls=%fused_computation.86 | convolution fusion | flops 1610612736 | bytes 6291456 | tf_op jit(solution)/shard_map/vn,cn->vc/dot_general | solution.py:51
  78.9 1.2 convolution_add_fusion
  80.2 2.0 %fusion.40 = f32[256,1024]{1,0:T(8,128)S(1)} fusion(f32[256,1024]{1,0:T(8,128)S(1)} %convolution_add_fusion, f32[1024,1024]{1,0:T(8,128)S(1)} %bitcast.57), kind=kOutput, calls=%fused_computation.88 | convolution fusion | flops 1610612736 | bytes 6291456 | tf_op jit(solution)/shard_map/vn,cn->vc/dot_general | solution.py:51
  82.3 4.4 %collective-permute-done.22 = f32[256,512]{1,0:T(8,128)S(1)} collective-permute-done((f32[256,512]{1,0:T(8,128)S(1)}, f32[256,512]{1,0:T(8,128)S(1)}, u32[]{:S(2)}, u32[]{:S(2)}) %collective-permute-start.22) | collective-permute-done | bytes 524320 | tf_op jit(solution)/shard_map/ppermute | solution.py:26
  87.1 3.5 %collective-permute-done.25 = f32[128,1024]{1,0:T(8,128)S(1)} collective-permute-done((f32[128,1024]{1,0:T(8,128)S(1)}, f32[128,1024]{1,0:T(8,128)S(1)}, u32[]{:S(2)}, u32[]{:S(2)}) %collective-permute-start.25) | collective-permute-done | bytes 524320 | tf_op jit(solution)/shard_map/ppermute | solution.py:26
  90.8 1.1 collective-permute-start.26
  91.8 1.3 %collective-permute-done.23 = f32[128,512]{1,0:T(8,128)S(1)} collective-permute-done((f32[128,512]{1,0:T(8,128)S(1)}, f32[128,512]{1,0:T(8,128)S(1)}, u32[]{:S(2)}, u32[]{:S(2)}) %collective-permute-start.23) | collective-permute-done | bytes 262176 | tf_op jit(solution)/shard_map/ppermute | solution.py:26
  93.2 3.2 %collective-permute-done.26 = f32[128,512]{1,0:T(8,128)S(1)} collective-permute-done((f32[128,512]{1,0:T(8,128)S(1)}, f32[128,512]{1,0:T(8,128)S(1)}, u32[]{:S(2)}, u32[]{:S(2)}) %collective-permute-start.26) | collective-permute-done | bytes 262176 | tf_op jit(solution)/shard_map/ppermute | solution.py:26
  96.5 2.9 %collective-permute-start.27 = (f32[128,512]{1,0:T(8,128)S(1)}, f32[128,512]{1,0:T(8,128)S(1)}, u32[]{:S(2)}, u32[]{:S(2)}) collective-permute-start(f32[128,512]{1,0:T(8,128)S(1)} %pad_maximum_fusion.14), channel_id=1, source_target_pairs={{0,2},{2,0},{4,6},{6,4},{8,14},{10,12},{12,10},{14,8},{16,18},{18,... | collective-permute-start | bytes 786440 | tf_op jit(solution)/shard_map/ppermute | solution.py:26
  99.4 3.8 %collective-permute-done.27 = f32[128,512]{1,0:T(8,128)S(1)} collective-permute-done((f32[128,512]{1,0:T(8,128)S(1)}, f32[128,512]{1,0:T(8,128)S(1)}, u32[]{:S(2)}, u32[]{:S(2)}) %collective-permute-start.27) | collective-permute-done | bytes 262176 | tf_op jit(solution)/shard_map/ppermute | solution.py:26
  103.9 4.5 %collective-permute-done.28 = f32[128,256]{1,0:T(8,128)S(1)} collective-permute-done((f32[128,256]{1,0:T(8,128)S(1)}, f32[128,256]{1,0:T(8,128)S(1)}, u32[]{:S(2)}, u32[]{:S(2)}) %collective-permute-start.28) | collective-permute-done | bytes 131104 | tf_op jit(solution)/shard_map/ppermute | solution.py:26
  108.7 4.1 %collective-permute-done.29 = f32[64,256]{1,0:T(8,128)S(1)} collective-permute-done((f32[64,256]{1,0:T(8,128)S(1)}, f32[64,256]{1,0:T(8,128)S(1)}, u32[]{:S(2)}, u32[]{:S(2)}) %collective-permute-start.29) | collective-permute-done | bytes 65568 | tf_op jit(solution)/shard_map/ppermute | solution.py:26
  112.9 2.8 %collective-permute-done.30 = f32[64,128]{1,0:T(8,128)S(1)} collective-permute-done((f32[64,128]{1,0:T(8,128)S(1)}, f32[64,128]{1,0:T(8,128)S(1)}, u32[]{:S(2)}, u32[]{:S(2)}) %collective-permute-start.30) | collective-permute-done | bytes 32800 | tf_op jit(solution)/shard_map/ppermute | solution.py:26
  115.8 6.9 %collective-permute-start.31 = (f32[64,64]{1,0:T(8,128)S(1)}, f32[64,64]{1,0:T(8,128)S(1)}, u32[]{:S(2)}, u32[]{:S(2)}) collective-permute-start(f32[64,64]{1,0:T(8,128)S(1)} %slice.217), channel_id=1, source_target_pairs={{0,8},{2,10},{4,12},{6,14},{8,0},{10,2},{12,4},{14,6},{16,24},{18,... | collective-permute-start | bytes 49160 | tf_op jit(solution)/shard_map/ppermute | solution.py:26
  (85 shorter events, 11.3 us)
Async XLA Ops:
  0.8 2.3 %collective-permute-start = (f32[64,64]{1,0:T(8,128)S(1)}, f32[64,64]{1,0:T(8,128)S(1)}, u32[]{:S(2)}, u32[]{:S(2)}) collective-permute-start(f32[64,64]{1,0:T(8,128)S(1)} %get-tuple-element.82), channel_id=1, source_target_pairs={{0,8},{2,10},{4,12},{6,14},{8,0},{10,2},{12,4},{14,6},{16,24},{18,... | collective-permute-start | bytes 49160 | tf_op jit(solution)/shard_map/ppermute | solution.py:26
  3.1 7.8 %collective-permute-start.1 = (f32[2,32,128]{2,1,0:T(8,128)S(1)}, f32[2,32,128]{2,1,0:T(8,128)S(1)}, u32[]{:S(2)}, u32[]{:S(2)}) collective-permute-start(f32[2,32,128]{2,1,0:T(8,128)S(1)} %pad_maximum_fusion.22), channel_id=1, source_target_pairs={{0,32},{2,34},{4,36},{6,38},{8,104},{10,106},{12,108},{14,110},{16... | collective-permute-start | bytes 98312 | tf_op jit(solution)/shard_map/ppermute | solution.py:26
  7.0 5.3 %collective-permute-start.2 = (f32[64,512]{1,0:T(8,128)}, f32[64,512]{1,0:T(8,128)S(1)}, u32[]{:S(2)}, u32[]{:S(2)}) collective-permute-start(f32[64,512]{1,0:T(8,128)} %param.5), channel_id=1, source_target_pairs={{0,2},{2,0},{4,6},{6,4},{8,14},{10,12},{12,10},{14,8},{16,18},{18,... | collective-permute-start | bytes 393224 | tf_op jit(solution)/shard_map/ppermute | solution.py:26
  9.7 7.0 %collective-permute-start.4 = (f32[64,1024]{1,0:T(8,128)}, f32[64,1024]{1,0:T(8,128)S(1)}, u32[]{:S(2)}, u32[]{:S(2)}) collective-permute-start(f32[64,1024]{1,0:T(8,128)} %param.6), channel_id=1, source_target_pairs={{0,16},{2,18},{4,20},{6,22},{8,24},{10,26},{12,28},{14,30},{16,0},... | collective-permute-start | bytes 786440 | tf_op jit(solution)/shard_map/ppermute | solution.py:26
  13.2 3.5 %collective-permute-start.3 = (f32[2,32,256]{2,1,0:T(8,128)S(1)}, f32[2,32,256]{2,1,0:T(8,128)S(1)}, u32[]{:S(2)}, u32[]{:S(2)}) collective-permute-start(f32[2,32,256]{2,1,0:T(8,128)S(1)} %pad_maximum_fusion.20), channel_id=1, source_target_pairs={{0,96},{2,98},{4,100},{6,102},{8,40},{10,42},{12,44},{14,46},{16,1... | collective-permute-start | bytes 196616 | tf_op jit(solution)/shard_map/ppermute | solution.py:26
  13.3 10.6 %collective-permute-start.7 = (f32[128,512]{1,0:T(8,128)S(1)}, f32[128,512]{1,0:T(8,128)S(1)}, u32[]{:S(2)}, u32[]{:S(2)}) collective-permute-start(f32[128,512]{1,0:T(8,128)S(1)} %pad_maximum_fusion.10), channel_id=1, source_target_pairs={{0,1},{2,3},{4,5},{6,7},{8,9},{10,11},{12,13},{14,15},{16,17},{18,... | collective-permute-start | bytes 786440 | tf_op jit(solution)/shard_map/ppermute | solution.py:26
  17.7 9.3 %collective-permute-start.8 = (f32[128,1024]{1,0:T(8,128)S(1)}, f32[128,1024]{1,0:T(8,128)S(1)}, u32[]{:S(2)}, u32[]{:S(2)}) collective-permute-start(f32[128,1024]{1,0:T(8,128)S(1)} %pad_maximum_fusion.5), channel_id=1, source_target_pairs={{0,32},{2,34},{4,36},{6,38},{8,104},{10,106},{12,108},{14,110},{16... | collective-permute-start | bytes 1572872 | tf_op jit(solution)/shard_map/ppermute | solution.py:26
  19.4 4.5 %collective-permute-start.5 = (f32[32,512]{1,0:T(8,128)S(1)}, f32[32,512]{1,0:T(8,128)S(1)}, u32[]{:S(2)}, u32[]{:S(2)}) collective-permute-start(f32[32,512]{1,0:T(8,128)S(1)} %get-tuple-element.78), channel_id=1, source_target_pairs={{0,2},{2,0},{4,6},{6,4},{8,14},{10,12},{12,10},{14,8},{16,18},{18,... | collective-permute-start | bytes 196616 | tf_op jit(solution)/shard_map/ppermute | solution.py:26
  20.6 6.6 %collective-permute-start.6 = (f32[32,512]{1,0:T(8,128)S(1)}, f32[32,512]{1,0:T(8,128)S(1)}, u32[]{:S(2)}, u32[]{:S(2)}) collective-permute-start(f32[32,512]{1,0:T(8,128)S(1)} %get-tuple-element.28), channel_id=1, source_target_pairs={{0,16},{2,18},{4,20},{6,22},{8,25},{10,27},{12,29},{14,31},{16,0},... | collective-permute-start | bytes 196616 | tf_op jit(solution)/shard_map/ppermute | solution.py:26
  27.2 18.1 %collective-permute-start.14 = (f32[256,1024]{1,0:T(8,128)S(1)}, f32[256,1024]{1,0:T(8,128)}, u32[]{:S(2)}, u32[]{:S(2)}) collective-permute-start(f32[256,1024]{1,0:T(8,128)S(1)} %pad_maximum_fusion.3), channel_id=1, source_target_pairs={{0,96},{2,98},{4,100},{6,102},{8,40},{10,42},{12,44},{14,46},{16,1... | collective-permute-start | bytes 3145736 | tf_op jit(solution)/shard_map/ppermute | solution.py:26
  27.3 18.0 %collective-permute-start.13 = (f32[256,1024]{1,0:T(8,128)S(1)}, f32[256,1024]{1,0:T(8,128)S(1)}, u32[]{:S(2)}, u32[]{:S(2)}) collective-permute-start(f32[256,1024]{1,0:T(8,128)S(1)} %pad_maximum_fusion.3), channel_id=1, source_target_pairs={{0,8},{2,10},{4,12},{6,14},{8,0},{10,2},{12,4},{14,6},{16,24},{18,... | collective-permute-start | bytes 3145736 | tf_op jit(solution)/shard_map/ppermute | solution.py:26
  30.2 4.3 %collective-permute-start.10 = (f32[64,512]{1,0:T(8,128)S(1)}, f32[64,512]{1,0:T(8,128)S(1)}, u32[]{:S(2)}, u32[]{:S(2)}) collective-permute-start(f32[64,512]{1,0:T(8,128)S(1)} %pad_maximum_fusion.17), channel_id=1, source_target_pairs={{0,17},{2,19},{4,21},{6,23},{8,24},{10,26},{12,28},{14,30},{16,1},... | collective-permute-start | bytes 393224 | tf_op jit(solution)/shard_map/ppermute | solution.py:26
  31.5 4.2 %collective-permute-start.9 = (f32[64,512]{1,0:T(8,128)S(1)}, f32[64,512]{1,0:T(8,128)S(1)}, u32[]{:S(2)}, u32[]{:S(2)}) collective-permute-start(f32[64,512]{1,0:T(8,128)S(1)} %pad_maximum_fusion.16), channel_id=1, source_target_pairs={{0,6},{2,4},{4,2},{6,0},{8,10},{10,8},{12,14},{14,12},{16,22},{18,... | collective-permute-start | bytes 393224 | tf_op jit(solution)/shard_map/ppermute | solution.py:26
  35.7 7.0 %collective-permute-start.12 = (f32[64,1024]{1,0:T(8,128)S(1)}, f32[64,1024]{1,0:T(8,128)S(1)}, u32[]{:S(2)}, u32[]{:S(2)}) collective-permute-start(f32[64,1024]{1,0:T(8,128)S(1)} %maximum_maximum_fusion.1), channel_id=1, source_target_pairs={{0,2},{2,0},{4,6},{6,4},{8,14},{10,12},{12,10},{14,8},{16,18},{18,... | collective-permute-start | bytes 786440 | tf_op jit(solution)/shard_map/ppermute | solution.py:26
  38.5 6.7 %collective-permute-start.11 = (f32[128,512]{1,0:T(8,128)S(1)}, f32[128,512]{1,0:T(8,128)S(1)}, u32[]{:S(2)}, u32[]{:S(2)}) collective-permute-start(f32[128,512]{1,0:T(8,128)S(1)} %pad_maximum_fusion.11), channel_id=1, source_target_pairs={{0,16},{2,18},{4,20},{6,22},{8,25},{10,27},{12,29},{14,31},{16,0},... | collective-permute-start | bytes 786440 | tf_op jit(solution)/shard_map/ppermute | solution.py:26
  40.4 10.3 %collective-permute-start.16 = (f32[256,512]{1,0:T(8,128)S(1)}, f32[256,512]{1,0:T(8,128)S(1)}, u32[]{:S(2)}, u32[]{:S(2)}) collective-permute-start(f32[256,512]{1,0:T(8,128)S(1)} %pad_maximum_fusion.6), channel_id=1, source_target_pairs={{0,6},{2,4},{4,2},{6,0},{8,10},{10,8},{12,14},{14,12},{16,22},{18,... | collective-permute-start | bytes 1572872 | tf_op jit(solution)/shard_map/ppermute | solution.py:26
  45.3 11.5 %collective-permute-start.17 = (f32[256,1024]{1,0:T(8,128)}, f32[256,1024]{1,0:T(8,128)S(1)}, u32[]{:S(2)}, u32[]{:S(2)}) collective-permute-start(f32[256,1024]{1,0:T(8,128)} %collective-permute-done.14), channel_id=1, source_target_pairs={{0,8},{2,10},{4,12},{6,14},{8,0},{10,2},{12,4},{14,6},{16,24},{18,... | collective-permute-start | bytes 3145736 | tf_op jit(solution)/shard_map/ppermute | solution.py:26
  48.2 8.4 %collective-permute-start.15 = (f32[256,512]{1,0:T(8,128)S(1)}, f32[256,512]{1,0:T(8,128)S(1)}, u32[]{:S(2)}, u32[]{:S(2)}) collective-permute-start(f32[256,512]{1,0:T(8,128)S(1)} %pad_maximum_fusion.8), channel_id=1, source_target_pairs={{0,17},{2,19},{4,21},{6,23},{8,24},{10,26},{12,28},{14,30},{16,1},... | collective-permute-start | bytes 1572872 | tf_op jit(solution)/shard_map/ppermute | solution.py:26
  50.7 11.8 %collective-permute-start.18 = (f32[128,1024]{1,0:T(8,128)S(1)}, f32[128,1024]{1,0:T(8,128)S(1)}, u32[]{:S(2)}, u32[]{:S(2)}) collective-permute-start(f32[128,1024]{1,0:T(8,128)S(1)} %pad_maximum_fusion.7), channel_id=1, source_target_pairs={{0,6},{2,4},{4,2},{6,0},{8,10},{10,8},{12,14},{14,12},{16,22},{18,... | collective-permute-start | bytes 1572872 | tf_op jit(solution)/shard_map/ppermute | solution.py:26
  60.3 4.7 %collective-permute-start.19 = (f32[256,1024]{1,0:T(8,128)S(1)}, f32[256,1024]{1,0:T(8,128)S(1)}, u32[]{:S(2)}, u32[]{:S(2)}) collective-permute-start(f32[256,1024]{1,0:T(8,128)S(1)} %fusion.36), channel_id=1, source_target_pairs={{0,8},{2,10},{4,12},{6,14},{8,0},{10,2},{12,4},{14,6},{16,24},{18,... | collective-permute-start | bytes 3145736 | tf_op jit(solution)/shard_map/ppermute | solution.py:26
  64.6 2.9 %collective-permute-start.20 = (f32[256,1024]{1,0:T(8,128)S(1)}, f32[256,1024]{1,0:T(8,128)S(1)}, u32[]{:S(2)}, u32[]{:S(2)}) collective-permute-start(f32[256,1024]{1,0:T(8,128)S(1)} %fusion.17), channel_id=1, source_target_pairs={{0,8},{2,10},{4,12},{6,14},{8,0},{10,2},{12,4},{14,6},{16,24},{18,... | collective-permute-start | bytes 3145736 | tf_op jit(solution)/shard_map/ppermute | solution.py:26
  64.8 2.6 %copy-start = (f32[512,1024]{1,0:T(8,128)S(1)}, f32[512,1024]{1,0:T(8,128)}, u32[]{:S(2)}) copy-start(f32[512,1024]{1,0:T(8,128)} %param.7) | copy-start | bytes 6291460
  70.7 4.0 %collective-permute-start.21 = (f32[256,1024]{1,0:T(8,128)S(1)}, f32[256,1024]{1,0:T(8,128)S(1)}, u32[]{:S(2)}, u32[]{:S(2)}) collective-permute-start(f32[256,1024]{1,0:T(8,128)S(1)} %fusion.37), channel_id=1, source_target_pairs={{0,8},{2,10},{4,12},{6,14},{8,0},{10,2},{12,4},{14,6},{16,24},{18,... | collective-permute-start | bytes 3145736 | tf_op jit(solution)/shard_map/ppermute | solution.py:26
  74.3 4.7 %collective-permute-start.24 = (f32[256,1024]{1,0:T(8,128)S(1)}, f32[256,1024]{1,0:T(8,128)S(1)}, u32[]{:S(2)}, u32[]{:S(2)}) collective-permute-start(f32[256,1024]{1,0:T(8,128)S(1)} %fusion.39), channel_id=1, source_target_pairs={{0,8},{2,10},{4,12},{6,14},{8,0},{10,2},{12,4},{14,6},{16,24},{18,... | collective-permute-start | bytes 3145736 | tf_op jit(solution)/shard_map/ppermute | solution.py:26
  78.1 8.6 %collective-permute-start.22 = (f32[256,512]{1,0:T(8,128)S(1)}, f32[256,512]{1,0:T(8,128)S(1)}, u32[]{:S(2)}, u32[]{:S(2)}) collective-permute-start(f32[256,512]{1,0:T(8,128)S(1)} %pad_maximum_fusion.9), channel_id=1, source_target_pairs={{0,96},{2,98},{4,100},{6,102},{8,40},{10,42},{12,44},{14,46},{16,1... | collective-permute-start | bytes 1572872 | tf_op jit(solution)/shard_map/ppermute | solution.py:26
  82.2 8.4 %collective-permute-start.25 = (f32[128,1024]{1,0:T(8,128)S(1)}, f32[128,1024]{1,0:T(8,128)S(1)}, u32[]{:S(2)}, u32[]{:S(2)}) collective-permute-start(f32[128,1024]{1,0:T(8,128)S(1)} %slice.195), channel_id=1, source_target_pairs={{0,6},{2,4},{4,2},{6,0},{8,10},{10,8},{12,14},{14,12},{16,22},{18,... | collective-permute-start | bytes 1572872 | tf_op jit(solution)/shard_map/ppermute | solution.py:26
  86.9 6.3 %collective-permute-start.23 = (f32[128,512]{1,0:T(8,128)S(1)}, f32[128,512]{1,0:T(8,128)S(1)}, u32[]{:S(2)}, u32[]{:S(2)}) collective-permute-start(f32[128,512]{1,0:T(8,128)S(1)} %pad_maximum_fusion.12), channel_id=1, source_target_pairs={{0,6},{2,4},{4,2},{6,0},{8,10},{10,8},{12,14},{14,12},{16,22},{18,... | collective-permute-start | bytes 786440 | tf_op jit(solution)/shard_map/ppermute | solution.py:26
  90.8 5.6 %collective-permute-start.26 = (f32[128,512]{1,0:T(8,128)S(1)}, f32[128,512]{1,0:T(8,128)S(1)}, u32[]{:S(2)}, u32[]{:S(2)}) collective-permute-start(f32[128,512]{1,0:T(8,128)S(1)} %pad_maximum_fusion.13), channel_id=1, source_target_pairs={{0,96},{2,98},{4,100},{6,102},{8,40},{10,42},{12,44},{14,46},{16,1... | collective-permute-start | bytes 786440 | tf_op jit(solution)/shard_map/ppermute | solution.py:26
  96.5 6.7 %collective-permute-start.27 = (f32[128,512]{1,0:T(8,128)S(1)}, f32[128,512]{1,0:T(8,128)S(1)}, u32[]{:S(2)}, u32[]{:S(2)}) collective-permute-start(f32[128,512]{1,0:T(8,128)S(1)} %pad_maximum_fusion.14), channel_id=1, source_target_pairs={{0,2},{2,0},{4,6},{6,4},{8,14},{10,12},{12,10},{14,8},{16,18},{18,... | collective-permute-start | bytes 786440 | tf_op jit(solution)/shard_map/ppermute | solution.py:26
  103.2 5.1 %collective-permute-start.28 = (f32[128,256]{1,0:T(8,128)S(1)}, f32[128,256]{1,0:T(8,128)S(1)}, u32[]{:S(2)}, u32[]{:S(2)}) collective-permute-start(f32[128,256]{1,0:T(8,128)S(1)} %pad_maximum_fusion.18), channel_id=1, source_target_pairs={{0,32},{2,34},{4,36},{6,38},{8,104},{10,106},{12,108},{14,110},{16... | collective-permute-start | bytes 393224 | tf_op jit(solution)/shard_map/ppermute | solution.py:26
  108.4 4.4 %collective-permute-start.29 = (f32[64,256]{1,0:T(8,128)S(1)}, f32[64,256]{1,0:T(8,128)S(1)}, u32[]{:S(2)}, u32[]{:S(2)}) collective-permute-start(f32[64,256]{1,0:T(8,128)S(1)} %fusion.24), channel_id=1, source_target_pairs={{0,17},{2,19},{4,21},{6,23},{8,25},{10,27},{12,29},{14,31},{16,1},... | collective-permute-start | bytes 196616 | tf_op jit(solution)/shard_map/ppermute | solution.py:26
  112.9 2.8 %collective-permute-start.30 = (f32[64,128]{1,0:T(8,128)S(1)}, f32[64,128]{1,0:T(8,128)S(1)}, u32[]{:S(2)}, u32[]{:S(2)}) collective-permute-start(f32[64,128]{1,0:T(8,128)S(1)} %slice.215), channel_id=1, source_target_pairs={{0,16},{2,18},{4,20},{6,22},{8,24},{10,26},{12,28},{14,30},{16,0},... | collective-permute-start | bytes 98312 | tf_op jit(solution)/shard_map/ppermute | solution.py:26
  115.8 7.7 %collective-permute-start.31 = (f32[64,64]{1,0:T(8,128)S(1)}, f32[64,64]{1,0:T(8,128)S(1)}, u32[]{:S(2)}, u32[]{:S(2)}) collective-permute-start(f32[64,64]{1,0:T(8,128)S(1)} %slice.217), channel_id=1, source_target_pairs={{0,8},{2,10},{4,12},{6,14},{8,0},{10,2},{12,4},{14,6},{16,24},{18,... | collective-permute-start | bytes 49160 | tf_op jit(solution)/shard_map/ppermute | solution.py:26

commit v4 on v3

--- a/solution.py
+++ b/solution.py
@@ -107,20 +107,16 @@
     v = v.reshape(2, 2, 2, 64, 512)
     v_mine, v_theirs = in_parts(v), in_parts(v.swapaxes(0, 2))
 
-    half_p = dot("vc,cn->vn", p, c_all)
-    got_p = flip(half_p, "core")
-    half_q = dot("vc,cn->vn", q, c_all)
-    got_q = flip(half_q, "core")
-    half_mine = jnp.concatenate([half_p, half_q], axis=0)
-    half_theirs = jnp.concatenate([got_p, got_q], axis=0)
+    half_mine = dot("vc,cn->vn", jnp.concatenate([p, q], axis=0), c_all)
+    half_theirs = flip(half_mine, "core")
     pairs_mine = screened * dot("vm,vn->mn", v_mine, half_mine)
+    sums = dot("vm,mn->vn", v_mine, pairs_mine)
+    sums, half_theirs = lax.optimization_barrier((sums, half_theirs))
     pairs_theirs = screened * dot("vm,vn->mn", v_theirs, half_theirs)
     to_p = flip(dot("vm,mn->vn", v_theirs[:256], pairs_theirs), "core")
     to_q = flip(dot("vm,mn->vn", v_theirs[256:], pairs_theirs), "core")
-    sums_p = dot("vm,mn->vn", v_mine[:256], pairs_mine) + to_p
-    sums_q = dot("vm,mn->vn", v_mine[256:], pairs_mine) + to_q
-    p = dot("vn,cn->vc", sums_p, c_all)
-    q = dot("vn,cn->vc", sums_q, c_all)
+    p = dot("vn,cn->vc", sums[:256] + to_p, c_all)
+    q = dot("vn,cn->vc", sums[256:] + to_q, c_all)
     p = trade(p, ZB, 1, 256)
     q = trade(q, YB, 0, 128)
     p = trade(p, YB, 0, 64)

time: 124 us -> 122 us (0.984)
  waiting for transfers between devices: 51.9 us -> 49.1 us
  starting transfers between devices: 46.9 us -> 48.5 us
  matrix products: 17 us -> 15.7 us
    ppermute x32 -> x31, waiting for transfers between devices: 51.9 us -> 49.1 us  [flip(): return lax.ppermute(value, AXES, pairs)]
    ppermute x32 -> x31, starting transfers between devices: 46.9 us -> 48.5 us  [flip(): return lax.ppermute(value, AXES, pairs)]
    dot_general x10 -> x8, matrix products: 17 us -> 15.7 us  [dot(): jnp.einsum(spec, a, b, precision=HIGH, preferred_element_type=jnp.float32)]
  transfers between devices with their start and end apart: 32 -> 31, of which waited for: 21 -> 22; matrix products, arithmetic and copies ran while one was open for 16% -> 13% of each run, Pallas kernels for 0% -> 0%
where the time goes in v4:
time: 122 us
  waiting for transfers between devices  49.1 us (40%)
  starting transfers between devices  48.5 us (40%)
  matrix products  15.7 us (13%)
  other arithmetic  5.79 us (5%)
  local copies, waits for them, and re-layouts  2.21 us (2%)
    ppermute x31, waiting for transfers between devices, flip(): return lax.ppermute(value, AXES, pairs)  49.1 us
    ppermute x31, starting transfers between devices, flip(): return lax.ppermute(value, AXES, pairs)  48.5 us
    dot_general x8, matrix products, dot(): jnp.einsum(spec, a, b, precision=HIGH, preferred_element_type=jnp.float32)  15.7 us
  transfers between devices with their start and end apart: 31, of which 22 were waited for; matrix products, arithmetic and copies ran while one was open for 13% of the time, Pallas kernels for 0%

profile of v4, /device:TPU:1, one launch (start us, length us, event | category | flops | bytes accessed | tf_op | source)
XLA Modules:
  0.0 121.8 jit_solution(6400539028917363268)
XLA Ops:
  0.8 1.4 %collective-permute-start = (f32[64,64]{1,0:T(8,128)S(1)}, f32[64,64]{1,0:T(8,128)S(1)}, u32[]{:S(2)}, u32[]{:S(2)}) collective-permute-start(f32[64,64]{1,0:T(8,128)S(1)} %get-tuple-element.86), channel_id=1, source_target_pairs={{0,8},{2,10},{4,12},{6,14},{8,0},{10,2},{12,4},{14,6},{16,24},{18,... | collective-permute-start | bytes 49160 | tf_op jit(solution)/shard_map/ppermute | solution.py:26
  2.2 0.9 collective-permute-done
  3.1 3.9 %collective-permute-start.1 = (f32[2,32,128]{2,1,0:T(8,128)S(1)}, f32[2,32,128]{2,1,0:T(8,128)S(1)}, u32[]{:S(2)}, u32[]{:S(2)}) collective-permute-start(f32[2,32,128]{2,1,0:T(8,128)S(1)} %pad_maximum_fusion.25), channel_id=1, source_target_pairs={{0,32},{2,34},{4,36},{6,38},{8,104},{10,106},{12,108},{14,110},{16... | collective-permute-start | bytes 98312 | tf_op jit(solution)/shard_map/ppermute | solution.py:26
  7.0 2.7 %collective-permute-start.2 = (f32[64,512]{1,0:T(8,128)}, f32[64,512]{1,0:T(8,128)S(1)}, u32[]{:S(2)}, u32[]{:S(2)}) collective-permute-start(f32[64,512]{1,0:T(8,128)} %param.5), channel_id=1, source_target_pairs={{0,2},{2,0},{4,6},{6,4},{8,14},{10,12},{12,10},{14,8},{16,18},{18,... | collective-permute-start | bytes 393224 | tf_op jit(solution)/shard_map/ppermute | solution.py:26
  9.7 1.2 collective-permute-start.4
  11.0 1.3 %collective-permute-done.2 = f32[64,512]{1,0:T(8,128)S(1)} collective-permute-done((f32[64,512]{1,0:T(8,128)}, f32[64,512]{1,0:T(8,128)S(1)}, u32[]{:S(2)}, u32[]{:S(2)}) %collective-permute-start.2) | collective-permute-done | bytes 131104 | tf_op jit(solution)/shard_map/ppermute | solution.py:26
  12.3 0.9 pad_maximum_fusion.13
  13.3 2.8 %collective-permute-start.7 = (f32[128,512]{1,0:T(8,128)S(1)}, f32[128,512]{1,0:T(8,128)S(1)}, u32[]{:S(2)}, u32[]{:S(2)}) collective-permute-start(f32[128,512]{1,0:T(8,128)S(1)} %pad_maximum_fusion.13), channel_id=1, source_target_pairs={{0,1},{2,3},{4,5},{6,7},{8,9},{10,11},{12,13},{14,15},{16,17},{18,... | collective-permute-start | bytes 786440 | tf_op jit(solution)/shard_map/ppermute | solution.py:26
  16.7 1.0 pad_maximum_fusion.8
  17.7 1.7 %collective-permute-start.8 = (f32[128,1024]{1,0:T(8,128)S(1)}, f32[128,1024]{1,0:T(8,128)S(1)}, u32[]{:S(2)}, u32[]{:S(2)}) collective-permute-start(f32[128,1024]{1,0:T(8,128)S(1)} %pad_maximum_fusion.8), channel_id=1, source_target_pairs={{0,32},{2,34},{4,36},{6,38},{8,104},{10,106},{12,108},{14,110},{16... | collective-permute-start | bytes 1572872 | tf_op jit(solution)/shard_map/ppermute | solution.py:26
  19.4 1.2 collective-permute-start.5
  20.6 2.5 %collective-permute-start.6 = (f32[32,512]{1,0:T(8,128)S(1)}, f32[32,512]{1,0:T(8,128)S(1)}, u32[]{:S(2)}, u32[]{:S(2)}) collective-permute-start(f32[32,512]{1,0:T(8,128)S(1)} %get-tuple-element.30), channel_id=1, source_target_pairs={{0,16},{2,18},{4,20},{6,22},{8,25},{10,27},{12,29},{14,31},{16,0},... | collective-permute-start | bytes 196616 | tf_op jit(solution)/shard_map/ppermute | solution.py:26
  24.0 3.1 %collective-permute-done.8 = f32[128,1024]{1,0:T(8,128)S(1)} collective-permute-done((f32[128,1024]{1,0:T(8,128)S(1)}, f32[128,1024]{1,0:T(8,128)S(1)}, u32[]{:S(2)}, u32[]{:S(2)}) %collective-permute-start.8) | collective-permute-done | bytes 524320 | tf_op jit(solution)/shard_map/ppermute | solution.py:26
  27.3 2.9 %collective-permute-start.13 = (f32[256,1024]{1,0:T(8,128)S(1)}, f32[256,1024]{1,0:T(8,128)S(1)}, u32[]{:S(2)}, u32[]{:S(2)}) collective-permute-start(f32[256,1024]{1,0:T(8,128)S(1)} %pad_maximum_fusion.3), channel_id=1, source_target_pairs={{0,8},{2,10},{4,12},{6,14},{8,0},{10,2},{12,4},{14,6},{16,24},{18,... | collective-permute-start | bytes 3145736 | tf_op jit(solution)/shard_map/ppermute | solution.py:26
  30.2 1.3 %collective-permute-start.10 = (f32[64,512]{1,0:T(8,128)S(1)}, f32[64,512]{1,0:T(8,128)S(1)}, u32[]{:S(2)}, u32[]{:S(2)}) collective-permute-start(f32[64,512]{1,0:T(8,128)S(1)} %pad_maximum_fusion.20), channel_id=1, source_target_pairs={{0,17},{2,19},{4,21},{6,23},{8,24},{10,26},{12,28},{14,30},{16,1},... | collective-permute-start | bytes 393224 | tf_op jit(solution)/shard_map/ppermute | solution.py:26
  31.5 1.3 %collective-permute-start.9 = (f32[64,512]{1,0:T(8,128)S(1)}, f32[64,512]{1,0:T(8,128)S(1)}, u32[]{:S(2)}, u32[]{:S(2)}) collective-permute-start(f32[64,512]{1,0:T(8,128)S(1)} %pad_maximum_fusion.19), channel_id=1, source_target_pairs={{0,6},{2,4},{4,2},{6,0},{8,10},{10,8},{12,14},{14,12},{16,22},{18,... | collective-permute-start | bytes 393224 | tf_op jit(solution)/shard_map/ppermute | solution.py:26
  32.8 1.7 %collective-permute-done.10 = f32[64,512]{1,0:T(8,128)S(1)} collective-permute-done((f32[64,512]{1,0:T(8,128)S(1)}, f32[64,512]{1,0:T(8,128)S(1)}, u32[]{:S(2)}, u32[]{:S(2)}) %collective-permute-start.10) | collective-permute-done | bytes 131104 | tf_op jit(solution)/shard_map/ppermute | solution.py:26
  34.5 1.2 collective-permute-done.9
  35.7 2.8 %collective-permute-start.12 = (f32[64,1024]{1,0:T(8,128)S(1)}, f32[64,1024]{1,0:T(8,128)S(1)}, u32[]{:S(2)}, u32[]{:S(2)}) collective-permute-start(f32[64,1024]{1,0:T(8,128)S(1)} %maximum_maximum_fusion.1), channel_id=1, source_target_pairs={{0,2},{2,0},{4,6},{6,4},{8,14},{10,12},{12,10},{14,8},{16,18},{18,... | collective-permute-start | bytes 786440 | tf_op jit(solution)/shard_map/ppermute | solution.py:26
  38.5 1.8 %collective-permute-start.11 = (f32[128,512]{1,0:T(8,128)S(1)}, f32[128,512]{1,0:T(8,128)S(1)}, u32[]{:S(2)}, u32[]{:S(2)}) collective-permute-start(f32[128,512]{1,0:T(8,128)S(1)} %pad_maximum_fusion.14), channel_id=1, source_target_pairs={{0,16},{2,18},{4,20},{6,22},{8,25},{10,27},{12,29},{14,31},{16,0},... | collective-permute-start | bytes 786440 | tf_op jit(solution)/shard_map/ppermute | solution.py:26
  40.4 2.3 %collective-permute-done.12 = f32[64,1024]{1,0:T(8,128)S(1)} collective-permute-done((f32[64,1024]{1,0:T(8,128)S(1)}, f32[64,1024]{1,0:T(8,128)S(1)}, u32[]{:S(2)}, u32[]{:S(2)}) %collective-permute-start.12) | collective-permute-done | bytes 262176 | tf_op jit(solution)/shard_map/ppermute | solution.py:26
  42.7 2.5 %collective-permute-done.11 = f32[128,512]{1,0:T(8,128)S(1)} collective-permute-done((f32[128,512]{1,0:T(8,128)S(1)}, f32[128,512]{1,0:T(8,128)S(1)}, u32[]{:S(2)}, u32[]{:S(2)}) %collective-permute-start.11) | collective-permute-done | bytes 262176 | tf_op jit(solution)/shard_map/ppermute | solution.py:26
  45.3 2.9 %collective-permute-start.18 = (f32[256,1024]{1,0:T(8,128)}, f32[256,1024]{1,0:T(8,128)S(1)}, u32[]{:S(2)}, u32[]{:S(2)}) collective-permute-start(f32[256,1024]{1,0:T(8,128)} %collective-permute-done.14), channel_id=1, source_target_pairs={{0,8},{2,10},{4,12},{6,14},{8,0},{10,2},{12,4},{14,6},{16,24},{18,... | collective-permute-start | bytes 3145736 | tf_op jit(solution)/shard_map/ppermute | solution.py:26
  48.3 2.3 %collective-permute-done.16 = f32[256,512]{1,0:T(8,128)S(1)} collective-permute-done((f32[256,512]{1,0:T(8,128)S(1)}, f32[256,512]{1,0:T(8,128)S(1)}, u32[]{:S(2)}, u32[]{:S(2)}) %collective-permute-start.16) | collective-permute-done | bytes 524320 | tf_op jit(solution)/shard_map/ppermute | solution.py:26
  50.8 1.4 %pad_maximum_fusion.1 = f32[512,1024]{1,0:T(8,128)S(1)} fusion(f32[256,1024]{1,0:T(8,128)} %collective-permute-done.14, f32[256,1024]{1,0:T(8,128)S(1)} %pad_maximum_fusion.3), kind=kLoop, calls=%fused_computation.7 | loop fusion | flops 524288 | bytes 4194304 | tf_op jit(solution)/shard_map/concatenate | solution.py:99
  52.3 4.3 %collective-permute-done.15 = f32[256,512]{1,0:T(8,128)S(1)} collective-permute-done((f32[256,512]{1,0:T(8,128)S(1)}, f32[256,512]{1,0:T(8,128)S(1)}, u32[]{:S(2)}, u32[]{:S(2)}) %collective-permute-start.15) | collective-permute-done | bytes 524320 | tf_op jit(solution)/shard_map/ppermute | solution.py:26
  59.1 3.5 %fusion = f32[512,1024]{1,0:T(8,128)S(1)} fusion(f32[1024,1024]{1,0:T(8,128)S(1)} %bitcast.48, f32[128,1024]{1,0:T(8,128)S(1)} %collective-permute-done.17, f32[128,1024]{1,0:T(8,128)S(1)} %pad_maximum_fusion.10, f32[256,1024]{1,0:T(8,128)S(1)} %maximum_maximum_fusion), kind=kOutput, calls=%fused_computation.1 | convolution fusion | flops 3222274048 | bytes 8388608 | tf_op jit(solution)/shard_map/vc,cn->vn/dot_general | solution.py:51
  62.6 2.0 %collective-permute-start.19 = (f32[512,1024]{1,0:T(8,128)S(1)}, f32[512,1024]{1,0:T(8,128)S(1)}, u32[]{:S(2)}, u32[]{:S(2)}) collective-permute-start(f32[512,1024]{1,0:T(8,128)S(1)} %fusion), channel_id=1, source_target_pairs={{0,8},{2,10},{4,12},{6,14},{8,0},{10,2},{12,4},{14,6},{16,24},{18,... | collective-permute-start | bytes 6291464 | tf_op jit(solution)/shard_map/ppermute | solution.py:26
  65.0 1.9 %fusion.17 = f32[512,1024]{1,0:T(8,128)S(1)} fusion(f32[512,1024]{1,0:T(8,128)S(1)} %fusion, f32[256,512]{1,0:T(8,128)S(1)} %bitcast.62, f32[256,512]{1,0:T(8,128)S(1)} %bitcast.60), kind=kOutput, calls=%fused_computation.26 | convolution fusion | flops 1610874880 | bytes 5242880 | tf_op jit(solution)/shard_map/vm,vn->mn/dot_general | solution.py:51
  67.0 1.9 %fusion.6 = f32[512,1024]{1,0:T(8,128)S(1)} fusion(f32[512,1024]{1,0:T(8,128)S(1)} %copy-done, f32[512,1024]{1,0:T(8,128)S(1)} %fusion.17, f32[256,512]{1,0:T(8,128)S(1)} %bitcast.63, f32[256,512]{1,0:T(8,128)S(1)} %bitcast.61), kind=kOutput, calls=%fused_computation.10 | convolution fusion | flops 1611399168 | bytes 7340032 | tf_op jit(solution)/shard_map/vm,mn->vn/dot_general | solution.py:51
  68.9 1.9 %convolution_multiply_fusion = f32[512,1024]{1,0:T(8,128)S(1)} fusion(f32[512,1024]{1,0:T(8,128)S(1)} %copy-done, f32[512,1024]{1,0:T(8,128)S(1)} %collective-permute-done.19, f32[256,512]{1,0:T(8,128)S(1)} %bitcast.56, f32[256,512]{1,0:T(8,128)S(1)} %bitcast.58), kind=kOutput, calls=%fused_computation.12 | convolution fusion | flops 1611399168 | bytes 7340032 | tf_op jit(solution)/shard_map/vm,vn->mn/dot_general | solution.py:51
  70.8 1.2 fusion.31
  72.1 1.2 fusion.32
  73.8 0.9 collective-permute-done.20
  74.7 2.0 %fusion.14 = f32[256,1024]{1,0:T(8,128)S(1)} fusion(f32[1024,1024]{1,0:T(8,128)S(1)} %bitcast.49, f32[256,1024]{1,0:T(8,128)S(1)} %collective-permute-done.20, f32[512,1024]{1,0:T(8,128)S(1)} %fusion.6), kind=kOutput, calls=%fused_computation.23 | convolution fusion | flops 1610874880 | bytes 7340032 | tf_op jit(solution)/shard_map/vn,cn->vc/dot_general | solution.py:51
  77.2 2.0 %fusion.11 = f32[256,1024]{1,0:T(8,128)S(1)} fusion(f32[1024,1024]{1,0:T(8,128)S(1)} %bitcast.50, f32[256,1024]{1,0:T(8,128)S(1)} %collective-permute-done.23, f32[512,1024]{1,0:T(8,128)S(1)} %fusion.6), kind=kOutput, calls=%fused_computation.20 | convolution fusion | flops 1610874880 | bytes 7340032 | tf_op jit(solution)/shard_map/vn,cn->vc/dot_general | solution.py:51
  79.4 6.1 %collective-permute-done.21 = f32[256,512]{1,0:T(8,128)S(1)} collective-permute-done((f32[256,512]{1,0:T(8,128)S(1)}, f32[256,512]{1,0:T(8,128)S(1)}, u32[]{:S(2)}, u32[]{:S(2)}) %collective-permute-start.21) | collective-permute-done | bytes 524320 | tf_op jit(solution)/shard_map/ppermute | solution.py:26
  85.8 2.0 %collective-permute-done.24 = f32[128,1024]{1,0:T(8,128)S(1)} collective-permute-done((f32[128,1024]{1,0:T(8,128)S(1)}, f32[128,1024]{1,0:T(8,128)S(1)}, u32[]{:S(2)}, u32[]{:S(2)}) %collective-permute-start.24) | collective-permute-done | bytes 524320 | tf_op jit(solution)/shard_map/ppermute | solution.py:26
  87.9 1.5 %collective-permute-start.25 = (f32[128,512]{1,0:T(8,128)S(1)}, f32[128,512]{1,0:T(8,128)S(1)}, u32[]{:S(2)}, u32[]{:S(2)}) collective-permute-start(f32[128,512]{1,0:T(8,128)S(1)} %pad_maximum_fusion.16), channel_id=1, source_target_pairs={{0,96},{2,98},{4,100},{6,102},{8,40},{10,42},{12,44},{14,46},{16,1... | collective-permute-start | bytes 786440 | tf_op jit(solution)/shard_map/ppermute | solution.py:26
  89.4 1.6 %collective-permute-done.22 = f32[128,512]{1,0:T(8,128)S(1)} collective-permute-done((f32[128,512]{1,0:T(8,128)S(1)}, f32[128,512]{1,0:T(8,128)S(1)}, u32[]{:S(2)}, u32[]{:S(2)}) %collective-permute-start.22) | collective-permute-done | bytes 262176 | tf_op jit(solution)/shard_map/ppermute | solution.py:26
  91.0 2.4 %collective-permute-done.25 = f32[128,512]{1,0:T(8,128)S(1)} collective-permute-done((f32[128,512]{1,0:T(8,128)S(1)}, f32[128,512]{1,0:T(8,128)S(1)}, u32[]{:S(2)}, u32[]{:S(2)}) %collective-permute-start.25) | collective-permute-done | bytes 262176 | tf_op jit(solution)/shard_map/ppermute | solution.py:26
  93.6 2.9 %collective-permute-start.26 = (f32[128,512]{1,0:T(8,128)S(1)}, f32[128,512]{1,0:T(8,128)S(1)}, u32[]{:S(2)}, u32[]{:S(2)}) collective-permute-start(f32[128,512]{1,0:T(8,128)S(1)} %pad_maximum_fusion.17), channel_id=1, source_target_pairs={{0,2},{2,0},{4,6},{6,4},{8,14},{10,12},{12,10},{14,8},{16,18},{18,... | collective-permute-start | bytes 786440 | tf_op jit(solution)/shard_map/ppermute | solution.py:26
  96.5 3.8 %collective-permute-done.26 = f32[128,512]{1,0:T(8,128)S(1)} collective-permute-done((f32[128,512]{1,0:T(8,128)S(1)}, f32[128,512]{1,0:T(8,128)S(1)}, u32[]{:S(2)}, u32[]{:S(2)}) %collective-permute-start.26) | collective-permute-done | bytes 262176 | tf_op jit(solution)/shard_map/ppermute | solution.py:26
  100.9 4.5 %collective-permute-done.27 = f32[128,256]{1,0:T(8,128)S(1)} collective-permute-done((f32[128,256]{1,0:T(8,128)S(1)}, f32[128,256]{1,0:T(8,128)S(1)}, u32[]{:S(2)}, u32[]{:S(2)}) %collective-permute-start.27) | collective-permute-done | bytes 131104 | tf_op jit(solution)/shard_map/ppermute | solution.py:26
  105.5 1.5 %collective-permute-start.28 = (f32[64,256]{1,0:T(8,128)S(1)}, f32[64,256]{1,0:T(8,128)S(1)}, u32[]{:S(2)}, u32[]{:S(2)}) collective-permute-start(f32[64,256]{1,0:T(8,128)S(1)} %fusion.18), channel_id=1, source_target_pairs={{0,17},{2,19},{4,21},{6,23},{8,25},{10,27},{12,29},{14,31},{16,1},... | collective-permute-start | bytes 196616 | tf_op jit(solution)/shard_map/ppermute | solution.py:26
  107.0 2.9 %collective-permute-done.28 = f32[64,256]{1,0:T(8,128)S(1)} collective-permute-done((f32[64,256]{1,0:T(8,128)S(1)}, f32[64,256]{1,0:T(8,128)S(1)}, u32[]{:S(2)}, u32[]{:S(2)}) %collective-permute-start.28) | collective-permute-done | bytes 65568 | tf_op jit(solution)/shard_map/ppermute | solution.py:26
  110.5 2.3 %collective-permute-done.29 = f32[64,128]{1,0:T(8,128)S(1)} collective-permute-done((f32[64,128]{1,0:T(8,128)S(1)}, f32[64,128]{1,0:T(8,128)S(1)}, u32[]{:S(2)}, u32[]{:S(2)}) %collective-permute-start.29) | collective-permute-done | bytes 32800 | tf_op jit(solution)/shard_map/ppermute | solution.py:26
  112.9 7.4 %collective-permute-start.30 = (f32[64,64]{1,0:T(8,128)S(1)}, f32[64,64]{1,0:T(8,128)S(1)}, u32[]{:S(2)}, u32[]{:S(2)}) collective-permute-start(f32[64,64]{1,0:T(8,128)S(1)} %slice.225), channel_id=1, source_target_pairs={{0,8},{2,10},{4,12},{6,14},{8,0},{10,2},{12,4},{14,6},{16,24},{18,... | collective-permute-start | bytes 49160 | tf_op jit(solution)/shard_map/ppermute | solution.py:26
  (81 shorter events, 10.5 us)
Async XLA Ops:
  0.8 2.3 %collective-permute-start = (f32[64,64]{1,0:T(8,128)S(1)}, f32[64,64]{1,0:T(8,128)S(1)}, u32[]{:S(2)}, u32[]{:S(2)}) collective-permute-start(f32[64,64]{1,0:T(8,128)S(1)} %get-tuple-element.86), channel_id=1, source_target_pairs={{0,8},{2,10},{4,12},{6,14},{8,0},{10,2},{12,4},{14,6},{16,24},{18,... | collective-permute-start | bytes 49160 | tf_op jit(solution)/shard_map/ppermute | solution.py:26
  3.1 7.8 %collective-permute-start.1 = (f32[2,32,128]{2,1,0:T(8,128)S(1)}, f32[2,32,128]{2,1,0:T(8,128)S(1)}, u32[]{:S(2)}, u32[]{:S(2)}) collective-permute-start(f32[2,32,128]{2,1,0:T(8,128)S(1)} %pad_maximum_fusion.25), channel_id=1, source_target_pairs={{0,32},{2,34},{4,36},{6,38},{8,104},{10,106},{12,108},{14,110},{16... | collective-permute-start | bytes 98312 | tf_op jit(solution)/shard_map/ppermute | solution.py:26
  7.0 5.3 %collective-permute-start.2 = (f32[64,512]{1,0:T(8,128)}, f32[64,512]{1,0:T(8,128)S(1)}, u32[]{:S(2)}, u32[]{:S(2)}) collective-permute-start(f32[64,512]{1,0:T(8,128)} %param.5), channel_id=1, source_target_pairs={{0,2},{2,0},{4,6},{6,4},{8,14},{10,12},{12,10},{14,8},{16,18},{18,... | collective-permute-start | bytes 393224 | tf_op jit(solution)/shard_map/ppermute | solution.py:26
  9.7 7.0 %collective-permute-start.4 = (f32[64,1024]{1,0:T(8,128)}, f32[64,1024]{1,0:T(8,128)S(1)}, u32[]{:S(2)}, u32[]{:S(2)}) collective-permute-start(f32[64,1024]{1,0:T(8,128)} %param.6), channel_id=1, source_target_pairs={{0,16},{2,18},{4,20},{6,22},{8,24},{10,26},{12,28},{14,30},{16,0},... | collective-permute-start | bytes 786440 | tf_op jit(solution)/shard_map/ppermute | solution.py:26
  13.2 3.5 %collective-permute-start.3 = (f32[2,32,256]{2,1,0:T(8,128)S(1)}, f32[2,32,256]{2,1,0:T(8,128)S(1)}, u32[]{:S(2)}, u32[]{:S(2)}) collective-permute-start(f32[2,32,256]{2,1,0:T(8,128)S(1)} %pad_maximum_fusion.23), channel_id=1, source_target_pairs={{0,96},{2,98},{4,100},{6,102},{8,40},{10,42},{12,44},{14,46},{16,1... | collective-permute-start | bytes 196616 | tf_op jit(solution)/shard_map/ppermute | solution.py:26
  13.3 10.6 %collective-permute-start.7 = (f32[128,512]{1,0:T(8,128)S(1)}, f32[128,512]{1,0:T(8,128)S(1)}, u32[]{:S(2)}, u32[]{:S(2)}) collective-permute-start(f32[128,512]{1,0:T(8,128)S(1)} %pad_maximum_fusion.13), channel_id=1, source_target_pairs={{0,1},{2,3},{4,5},{6,7},{8,9},{10,11},{12,13},{14,15},{16,17},{18,... | collective-permute-start | bytes 786440 | tf_op jit(solution)/shard_map/ppermute | solution.py:26
  17.7 9.3 %collective-permute-start.8 = (f32[128,1024]{1,0:T(8,128)S(1)}, f32[128,1024]{1,0:T(8,128)S(1)}, u32[]{:S(2)}, u32[]{:S(2)}) collective-permute-start(f32[128,1024]{1,0:T(8,128)S(1)} %pad_maximum_fusion.8), channel_id=1, source_target_pairs={{0,32},{2,34},{4,36},{6,38},{8,104},{10,106},{12,108},{14,110},{16... | collective-permute-start | bytes 1572872 | tf_op jit(solution)/shard_map/ppermute | solution.py:26
  19.4 4.5 %collective-permute-start.5 = (f32[32,512]{1,0:T(8,128)S(1)}, f32[32,512]{1,0:T(8,128)S(1)}, u32[]{:S(2)}, u32[]{:S(2)}) collective-permute-start(f32[32,512]{1,0:T(8,128)S(1)} %get-tuple-element.82), channel_id=1, source_target_pairs={{0,2},{2,0},{4,6},{6,4},{8,14},{10,12},{12,10},{14,8},{16,18},{18,... | collective-permute-start | bytes 196616 | tf_op jit(solution)/shard_map/ppermute | solution.py:26
  20.6 6.6 %collective-permute-start.6 = (f32[32,512]{1,0:T(8,128)S(1)}, f32[32,512]{1,0:T(8,128)S(1)}, u32[]{:S(2)}, u32[]{:S(2)}) collective-permute-start(f32[32,512]{1,0:T(8,128)S(1)} %get-tuple-element.30), channel_id=1, source_target_pairs={{0,16},{2,18},{4,20},{6,22},{8,25},{10,27},{12,29},{14,31},{16,0},... | collective-permute-start | bytes 196616 | tf_op jit(solution)/shard_map/ppermute | solution.py:26
  27.2 18.1 %collective-permute-start.14 = (f32[256,1024]{1,0:T(8,128)S(1)}, f32[256,1024]{1,0:T(8,128)}, u32[]{:S(2)}, u32[]{:S(2)}) collective-permute-start(f32[256,1024]{1,0:T(8,128)S(1)} %pad_maximum_fusion.3), channel_id=1, source_target_pairs={{0,96},{2,98},{4,100},{6,102},{8,40},{10,42},{12,44},{14,46},{16,1... | collective-permute-start | bytes 3145736 | tf_op jit(solution)/shard_map/ppermute | solution.py:26
  27.3 18.0 %collective-permute-start.13 = (f32[256,1024]{1,0:T(8,128)S(1)}, f32[256,1024]{1,0:T(8,128)S(1)}, u32[]{:S(2)}, u32[]{:S(2)}) collective-permute-start(f32[256,1024]{1,0:T(8,128)S(1)} %pad_maximum_fusion.3), channel_id=1, source_target_pairs={{0,8},{2,10},{4,12},{6,14},{8,0},{10,2},{12,4},{14,6},{16,24},{18,... | collective-permute-start | bytes 3145736 | tf_op jit(solution)/shard_map/ppermute | solution.py:26
  30.2 4.3 %collective-permute-start.10 = (f32[64,512]{1,0:T(8,128)S(1)}, f32[64,512]{1,0:T(8,128)S(1)}, u32[]{:S(2)}, u32[]{:S(2)}) collective-permute-start(f32[64,512]{1,0:T(8,128)S(1)} %pad_maximum_fusion.20), channel_id=1, source_target_pairs={{0,17},{2,19},{4,21},{6,23},{8,24},{10,26},{12,28},{14,30},{16,1},... | collective-permute-start | bytes 393224 | tf_op jit(solution)/shard_map/ppermute | solution.py:26
  31.5 4.2 %collective-permute-start.9 = (f32[64,512]{1,0:T(8,128)S(1)}, f32[64,512]{1,0:T(8,128)S(1)}, u32[]{:S(2)}, u32[]{:S(2)}) collective-permute-start(f32[64,512]{1,0:T(8,128)S(1)} %pad_maximum_fusion.19), channel_id=1, source_target_pairs={{0,6},{2,4},{4,2},{6,0},{8,10},{10,8},{12,14},{14,12},{16,22},{18,... | collective-permute-start | bytes 393224 | tf_op jit(solution)/shard_map/ppermute | solution.py:26
  35.7 7.0 %collective-permute-start.12 = (f32[64,1024]{1,0:T(8,128)S(1)}, f32[64,1024]{1,0:T(8,128)S(1)}, u32[]{:S(2)}, u32[]{:S(2)}) collective-permute-start(f32[64,1024]{1,0:T(8,128)S(1)} %maximum_maximum_fusion.1), channel_id=1, source_target_pairs={{0,2},{2,0},{4,6},{6,4},{8,14},{10,12},{12,10},{14,8},{16,18},{18,... | collective-permute-start | bytes 786440 | tf_op jit(solution)/shard_map/ppermute | solution.py:26
  38.5 6.7 %collective-permute-start.11 = (f32[128,512]{1,0:T(8,128)S(1)}, f32[128,512]{1,0:T(8,128)S(1)}, u32[]{:S(2)}, u32[]{:S(2)}) collective-permute-start(f32[128,512]{1,0:T(8,128)S(1)} %pad_maximum_fusion.14), channel_id=1, source_target_pairs={{0,16},{2,18},{4,20},{6,22},{8,25},{10,27},{12,29},{14,31},{16,0},... | collective-permute-start | bytes 786440 | tf_op jit(solution)/shard_map/ppermute | solution.py:26
  40.4 10.3 %collective-permute-start.16 = (f32[256,512]{1,0:T(8,128)S(1)}, f32[256,512]{1,0:T(8,128)S(1)}, u32[]{:S(2)}, u32[]{:S(2)}) collective-permute-start(f32[256,512]{1,0:T(8,128)S(1)} %pad_maximum_fusion.9), channel_id=1, source_target_pairs={{0,6},{2,4},{4,2},{6,0},{8,10},{10,8},{12,14},{14,12},{16,22},{18,... | collective-permute-start | bytes 1572872 | tf_op jit(solution)/shard_map/ppermute | solution.py:26
  45.3 11.5 %collective-permute-start.18 = (f32[256,1024]{1,0:T(8,128)}, f32[256,1024]{1,0:T(8,128)S(1)}, u32[]{:S(2)}, u32[]{:S(2)}) collective-permute-start(f32[256,1024]{1,0:T(8,128)} %collective-permute-done.14), channel_id=1, source_target_pairs={{0,8},{2,10},{4,12},{6,14},{8,0},{10,2},{12,4},{14,6},{16,24},{18,... | collective-permute-start | bytes 3145736 | tf_op jit(solution)/shard_map/ppermute | solution.py:26
  48.2 8.4 %collective-permute-start.15 = (f32[256,512]{1,0:T(8,128)S(1)}, f32[256,512]{1,0:T(8,128)S(1)}, u32[]{:S(2)}, u32[]{:S(2)}) collective-permute-start(f32[256,512]{1,0:T(8,128)S(1)} %pad_maximum_fusion.11), channel_id=1, source_target_pairs={{0,17},{2,19},{4,21},{6,23},{8,24},{10,26},{12,28},{14,30},{16,1},... | collective-permute-start | bytes 1572872 | tf_op jit(solution)/shard_map/ppermute | solution.py:26
  50.7 8.4 %collective-permute-start.17 = (f32[128,1024]{1,0:T(8,128)S(1)}, f32[128,1024]{1,0:T(8,128)S(1)}, u32[]{:S(2)}, u32[]{:S(2)}) collective-permute-start(f32[128,1024]{1,0:T(8,128)S(1)} %pad_maximum_fusion.10), channel_id=1, source_target_pairs={{0,6},{2,4},{4,2},{6,0},{8,10},{10,8},{12,14},{14,12},{16,22},{18,... | collective-permute-start | bytes 1572872 | tf_op jit(solution)/shard_map/ppermute | solution.py:26
  62.6 6.2 %collective-permute-start.19 = (f32[512,1024]{1,0:T(8,128)S(1)}, f32[512,1024]{1,0:T(8,128)S(1)}, u32[]{:S(2)}, u32[]{:S(2)}) collective-permute-start(f32[512,1024]{1,0:T(8,128)S(1)} %fusion), channel_id=1, source_target_pairs={{0,8},{2,10},{4,12},{6,14},{8,0},{10,2},{12,4},{14,6},{16,24},{18,... | collective-permute-start | bytes 6291464 | tf_op jit(solution)/shard_map/ppermute | solution.py:26
  65.0 1.9 %copy-start = (f32[512,1024]{1,0:T(8,128)S(1)}, f32[512,1024]{1,0:T(8,128)}, u32[]{:S(2)}) copy-start(f32[512,1024]{1,0:T(8,128)} %param.7) | copy-start | bytes 6291460
  72.0 2.7 %collective-permute-start.20 = (f32[256,1024]{1,0:T(8,128)S(1)}, f32[256,1024]{1,0:T(8,128)S(1)}, u32[]{:S(2)}, u32[]{:S(2)}) collective-permute-start(f32[256,1024]{1,0:T(8,128)S(1)} %fusion.31), channel_id=1, source_target_pairs={{0,8},{2,10},{4,12},{6,14},{8,0},{10,2},{12,4},{14,6},{16,24},{18,... | collective-permute-start | bytes 3145736 | tf_op jit(solution)/shard_map/ppermute | solution.py:26
  73.3 4.0 %collective-permute-start.23 = (f32[256,1024]{1,0:T(8,128)S(1)}, f32[256,1024]{1,0:T(8,128)S(1)}, u32[]{:S(2)}, u32[]{:S(2)}) collective-permute-start(f32[256,1024]{1,0:T(8,128)S(1)} %fusion.32), channel_id=1, source_target_pairs={{0,8},{2,10},{4,12},{6,14},{8,0},{10,2},{12,4},{14,6},{16,24},{18,... | collective-permute-start | bytes 3145736 | tf_op jit(solution)/shard_map/ppermute | solution.py:26
  76.9 8.6 %collective-permute-start.21 = (f32[256,512]{1,0:T(8,128)S(1)}, f32[256,512]{1,0:T(8,128)S(1)}, u32[]{:S(2)}, u32[]{:S(2)}) collective-permute-start(f32[256,512]{1,0:T(8,128)S(1)} %pad_maximum_fusion.12), channel_id=1, source_target_pairs={{0,96},{2,98},{4,100},{6,102},{8,40},{10,42},{12,44},{14,46},{16,1... | collective-permute-start | bytes 1572872 | tf_op jit(solution)/shard_map/ppermute | solution.py:26
  79.3 8.4 %collective-permute-start.24 = (f32[128,1024]{1,0:T(8,128)S(1)}, f32[128,1024]{1,0:T(8,128)S(1)}, u32[]{:S(2)}, u32[]{:S(2)}) collective-permute-start(f32[128,1024]{1,0:T(8,128)S(1)} %slice.203), channel_id=1, source_target_pairs={{0,6},{2,4},{4,2},{6,0},{8,10},{10,8},{12,14},{14,12},{16,22},{18,... | collective-permute-start | bytes 1572872 | tf_op jit(solution)/shard_map/ppermute | solution.py:26
  85.7 5.3 %collective-permute-start.22 = (f32[128,512]{1,0:T(8,128)S(1)}, f32[128,512]{1,0:T(8,128)S(1)}, u32[]{:S(2)}, u32[]{:S(2)}) collective-permute-start(f32[128,512]{1,0:T(8,128)S(1)} %pad_maximum_fusion.15), channel_id=1, source_target_pairs={{0,6},{2,4},{4,2},{6,0},{8,10},{10,8},{12,14},{14,12},{16,22},{18,... | collective-permute-start | bytes 786440 | tf_op jit(solution)/shard_map/ppermute | solution.py:26
  87.9 5.6 %collective-permute-start.25 = (f32[128,512]{1,0:T(8,128)S(1)}, f32[128,512]{1,0:T(8,128)S(1)}, u32[]{:S(2)}, u32[]{:S(2)}) collective-permute-start(f32[128,512]{1,0:T(8,128)S(1)} %pad_maximum_fusion.16), channel_id=1, source_target_pairs={{0,96},{2,98},{4,100},{6,102},{8,40},{10,42},{12,44},{14,46},{16,1... | collective-permute-start | bytes 786440 | tf_op jit(solution)/shard_map/ppermute | solution.py:26
  93.6 6.7 %collective-permute-start.26 = (f32[128,512]{1,0:T(8,128)S(1)}, f32[128,512]{1,0:T(8,128)S(1)}, u32[]{:S(2)}, u32[]{:S(2)}) collective-permute-start(f32[128,512]{1,0:T(8,128)S(1)} %pad_maximum_fusion.17), channel_id=1, source_target_pairs={{0,2},{2,0},{4,6},{6,4},{8,14},{10,12},{12,10},{14,8},{16,18},{18,... | collective-permute-start | bytes 786440 | tf_op jit(solution)/shard_map/ppermute | solution.py:26
  100.3 5.1 %collective-permute-start.27 = (f32[128,256]{1,0:T(8,128)S(1)}, f32[128,256]{1,0:T(8,128)S(1)}, u32[]{:S(2)}, u32[]{:S(2)}) collective-permute-start(f32[128,256]{1,0:T(8,128)S(1)} %pad_maximum_fusion.21), channel_id=1, source_target_pairs={{0,32},{2,34},{4,36},{6,38},{8,104},{10,106},{12,108},{14,110},{16... | collective-permute-start | bytes 393224 | tf_op jit(solution)/shard_map/ppermute | solution.py:26
  105.5 4.4 %collective-permute-start.28 = (f32[64,256]{1,0:T(8,128)S(1)}, f32[64,256]{1,0:T(8,128)S(1)}, u32[]{:S(2)}, u32[]{:S(2)}) collective-permute-start(f32[64,256]{1,0:T(8,128)S(1)} %fusion.18), channel_id=1, source_target_pairs={{0,17},{2,19},{4,21},{6,23},{8,25},{10,27},{12,29},{14,31},{16,1},... | collective-permute-start | bytes 196616 | tf_op jit(solution)/shard_map/ppermute | solution.py:26
  109.9 2.8 %collective-permute-start.29 = (f32[64,128]{1,0:T(8,128)S(1)}, f32[64,128]{1,0:T(8,128)S(1)}, u32[]{:S(2)}, u32[]{:S(2)}) collective-permute-start(f32[64,128]{1,0:T(8,128)S(1)} %slice.223), channel_id=1, source_target_pairs={{0,16},{2,18},{4,20},{6,22},{8,24},{10,26},{12,28},{14,30},{16,0},... | collective-permute-start | bytes 98312 | tf_op jit(solution)/shard_map/ppermute | solution.py:26
  112.9 8.3 %collective-permute-start.30 = (f32[64,64]{1,0:T(8,128)S(1)}, f32[64,64]{1,0:T(8,128)S(1)}, u32[]{:S(2)}, u32[]{:S(2)}) collective-permute-start(f32[64,64]{1,0:T(8,128)S(1)} %slice.225), channel_id=1, source_target_pairs={{0,8},{2,10},{4,12},{6,14},{8,0},{10,2},{12,4},{14,6},{16,24},{18,... | collective-permute-start | bytes 49160 | tf_op jit(solution)/shard_map/ppermute | solution.py:26

commit v5 on v4

--- a/solution.py
+++ b/solution.py
@@ -30,7 +30,6 @@
 X1, X2, X3 = (0, 1, 0), (0, 2, 0), (0, 3, 0)
 ZA, ZB, YA, YB, XL, XH = (Z1, Z3), (Z3, Z1), (Y1, Y3), (Y3, Y1), (X1, X1), (X2, X2)
 XA, XB = (X1, X3), (X3, X1)
-XN = (X3, X3)
 
 
 def grow(value, step, axis):
@@ -125,8 +124,7 @@
     q_kept, q_sent = alternate(q, 0, 64)
     r = jnp.concatenate([p_kept, q_kept], axis=0) + flip(jnp.concatenate([p_sent, q_sent], axis=0), YA)
     r = trade(r, ZA, 1, 128)
-    kept, sent = alternate(r, 0, 32)
-    r = kept + flip(jnp.concatenate([sent[:, 128:], sent[:, :128]], axis=1), XN)
+    r = trade(r, XH, 0, 32)
     r = trade(r, XL, 1, 128)
     kept = r[:, :64]
     got = flip(r[:, 64:], "core")

time: 122 us -> 122 us (level)
  starting transfers between devices: 48.5 us -> 50 us
    ppermute x31, starting transfers between devices: 48.5 us -> 50 us  [flip(): return lax.ppermute(value, AXES, pairs)]
    ppermute x31, waiting for transfers between devices: 49.1 us -> 47.9 us  [flip(): return lax.ppermute(value, AXES, pairs)]
  transfers between devices with their start and end apart: 31 -> 31, of which waited for: 22 -> 22; matrix products, arithmetic and copies ran while one was open for 13% -> 12% of each run, Pallas kernels for 0% -> 0%
where the time goes in v5:
time: 122 us
  starting transfers between devices  50 us (41%)
  waiting for transfers between devices  47.9 us (39%)
  matrix products  15.7 us (13%)
  other arithmetic  5.78 us (5%)
  local copies, waits for them, and re-layouts  2.21 us (2%)
    ppermute x31, starting transfers between devices, flip(): return lax.ppermute(value, AXES, pairs)  50 us
    ppermute x31, waiting for transfers between devices, flip(): return lax.ppermute(value, AXES, pairs)  47.9 us
    dot_general x8, matrix products, dot(): jnp.einsum(spec, a, b, precision=HIGH, preferred_element_type=jnp.float32)  15.7 us
  transfers between devices with their start and end apart: 31, of which 22 were waited for; matrix products, arithmetic and copies ran while one was open for 12% of the time, Pallas kernels for 0%

profile of v5, /device:TPU:1, one launch (start us, length us, event | category | flops | bytes accessed | tf_op | source)
XLA Modules:
  0.0 122.1 jit_solution(13059066428291094066)
XLA Ops:
  0.8 1.4 %collective-permute-start = (f32[64,64]{1,0:T(8,128)S(1)}, f32[64,64]{1,0:T(8,128)S(1)}, u32[]{:S(2)}, u32[]{:S(2)}) collective-permute-start(f32[64,64]{1,0:T(8,128)S(1)} %get-tuple-element.86), channel_id=1, source_target_pairs={{0,8},{2,10},{4,12},{6,14},{8,0},{10,2},{12,4},{14,6},{16,24},{18,... | collective-permute-start | bytes 49160 | tf_op jit(solution)/shard_map/ppermute | solution.py:26
  3.1 3.9 %collective-permute-start.1 = (f32[2,32,128]{2,1,0:T(8,128)S(1)}, f32[2,32,128]{2,1,0:T(8,128)S(1)}, u32[]{:S(2)}, u32[]{:S(2)}) collective-permute-start(f32[2,32,128]{2,1,0:T(8,128)S(1)} %pad_maximum_fusion.25), channel_id=1, source_target_pairs={{0,32},{2,34},{4,36},{6,38},{8,104},{10,106},{12,108},{14,110},{16... | collective-permute-start | bytes 98312 | tf_op jit(solution)/shard_map/ppermute | solution.py:26
  7.0 2.7 %collective-permute-start.2 = (f32[64,512]{1,0:T(8,128)}, f32[64,512]{1,0:T(8,128)S(1)}, u32[]{:S(2)}, u32[]{:S(2)}) collective-permute-start(f32[64,512]{1,0:T(8,128)} %param.5), channel_id=1, source_target_pairs={{0,2},{2,0},{4,6},{6,4},{8,14},{10,12},{12,10},{14,8},{16,18},{18,... | collective-permute-start | bytes 393224 | tf_op jit(solution)/shard_map/ppermute | solution.py:26
  9.7 1.2 collective-permute-start.4
  11.0 1.3 %collective-permute-done.2 = f32[64,512]{1,0:T(8,128)S(1)} collective-permute-done((f32[64,512]{1,0:T(8,128)}, f32[64,512]{1,0:T(8,128)S(1)}, u32[]{:S(2)}, u32[]{:S(2)}) %collective-permute-start.2) | collective-permute-done | bytes 131104 | tf_op jit(solution)/shard_map/ppermute | solution.py:26
  12.3 0.9 pad_maximum_fusion.13
  13.3 2.8 %collective-permute-start.7 = (f32[128,512]{1,0:T(8,128)S(1)}, f32[128,512]{1,0:T(8,128)S(1)}, u32[]{:S(2)}, u32[]{:S(2)}) collective-permute-start(f32[128,512]{1,0:T(8,128)S(1)} %pad_maximum_fusion.13), channel_id=1, source_target_pairs={{0,1},{2,3},{4,5},{6,7},{8,9},{10,11},{12,13},{14,15},{16,17},{18,... | collective-permute-start | bytes 786440 | tf_op jit(solution)/shard_map/ppermute | solution.py:26
  16.7 1.0 pad_maximum_fusion.8
  17.7 1.7 %collective-permute-start.8 = (f32[128,1024]{1,0:T(8,128)S(1)}, f32[128,1024]{1,0:T(8,128)S(1)}, u32[]{:S(2)}, u32[]{:S(2)}) collective-permute-start(f32[128,1024]{1,0:T(8,128)S(1)} %pad_maximum_fusion.8), channel_id=1, source_target_pairs={{0,32},{2,34},{4,36},{6,38},{8,104},{10,106},{12,108},{14,110},{16... | collective-permute-start | bytes 1572872 | tf_op jit(solution)/shard_map/ppermute | solution.py:26
  19.4 1.2 collective-permute-start.5
  20.6 2.5 %collective-permute-start.6 = (f32[32,512]{1,0:T(8,128)S(1)}, f32[32,512]{1,0:T(8,128)S(1)}, u32[]{:S(2)}, u32[]{:S(2)}) collective-permute-start(f32[32,512]{1,0:T(8,128)S(1)} %get-tuple-element.30), channel_id=1, source_target_pairs={{0,16},{2,18},{4,20},{6,22},{8,25},{10,27},{12,29},{14,31},{16,0},... | collective-permute-start | bytes 196616 | tf_op jit(solution)/shard_map/ppermute | solution.py:26
  24.0 3.1 %collective-permute-done.8 = f32[128,1024]{1,0:T(8,128)S(1)} collective-permute-done((f32[128,1024]{1,0:T(8,128)S(1)}, f32[128,1024]{1,0:T(8,128)S(1)}, u32[]{:S(2)}, u32[]{:S(2)}) %collective-permute-start.8) | collective-permute-done | bytes 524320 | tf_op jit(solution)/shard_map/ppermute | solution.py:26
  27.3 2.9 %collective-permute-start.13 = (f32[256,1024]{1,0:T(8,128)S(1)}, f32[256,1024]{1,0:T(8,128)S(1)}, u32[]{:S(2)}, u32[]{:S(2)}) collective-permute-start(f32[256,1024]{1,0:T(8,128)S(1)} %pad_maximum_fusion.3), channel_id=1, source_target_pairs={{0,8},{2,10},{4,12},{6,14},{8,0},{10,2},{12,4},{14,6},{16,24},{18,... | collective-permute-start | bytes 3145736 | tf_op jit(solution)/shard_map/ppermute | solution.py:26
  30.2 1.3 %collective-permute-start.10 = (f32[64,512]{1,0:T(8,128)S(1)}, f32[64,512]{1,0:T(8,128)S(1)}, u32[]{:S(2)}, u32[]{:S(2)}) collective-permute-start(f32[64,512]{1,0:T(8,128)S(1)} %pad_maximum_fusion.20), channel_id=1, source_target_pairs={{0,17},{2,19},{4,21},{6,23},{8,24},{10,26},{12,28},{14,30},{16,1},... | collective-permute-start | bytes 393224 | tf_op jit(solution)/shard_map/ppermute | solution.py:26
  31.5 1.3 %collective-permute-start.9 = (f32[64,512]{1,0:T(8,128)S(1)}, f32[64,512]{1,0:T(8,128)S(1)}, u32[]{:S(2)}, u32[]{:S(2)}) collective-permute-start(f32[64,512]{1,0:T(8,128)S(1)} %pad_maximum_fusion.19), channel_id=1, source_target_pairs={{0,6},{2,4},{4,2},{6,0},{8,10},{10,8},{12,14},{14,12},{16,22},{18,... | collective-permute-start | bytes 393224 | tf_op jit(solution)/shard_map/ppermute | solution.py:26
  32.8 1.7 %collective-permute-done.10 = f32[64,512]{1,0:T(8,128)S(1)} collective-permute-done((f32[64,512]{1,0:T(8,128)S(1)}, f32[64,512]{1,0:T(8,128)S(1)}, u32[]{:S(2)}, u32[]{:S(2)}) %collective-permute-start.10) | collective-permute-done | bytes 131104 | tf_op jit(solution)/shard_map/ppermute | solution.py:26
  34.5 1.2 collective-permute-done.9
  35.7 2.8 %collective-permute-start.12 = (f32[64,1024]{1,0:T(8,128)S(1)}, f32[64,1024]{1,0:T(8,128)S(1)}, u32[]{:S(2)}, u32[]{:S(2)}) collective-permute-start(f32[64,1024]{1,0:T(8,128)S(1)} %maximum_maximum_fusion.1), channel_id=1, source_target_pairs={{0,2},{2,0},{4,6},{6,4},{8,14},{10,12},{12,10},{14,8},{16,18},{18,... | collective-permute-start | bytes 786440 | tf_op jit(solution)/shard_map/ppermute | solution.py:26
  38.5 1.8 %collective-permute-start.11 = (f32[128,512]{1,0:T(8,128)S(1)}, f32[128,512]{1,0:T(8,128)S(1)}, u32[]{:S(2)}, u32[]{:S(2)}) collective-permute-start(f32[128,512]{1,0:T(8,128)S(1)} %pad_maximum_fusion.14), channel_id=1, source_target_pairs={{0,16},{2,18},{4,20},{6,22},{8,25},{10,27},{12,29},{14,31},{16,0},... | collective-permute-start | bytes 786440 | tf_op jit(solution)/shard_map/ppermute | solution.py:26
  40.4 2.3 %collective-permute-done.12 = f32[64,1024]{1,0:T(8,128)S(1)} collective-permute-done((f32[64,1024]{1,0:T(8,128)S(1)}, f32[64,1024]{1,0:T(8,128)S(1)}, u32[]{:S(2)}, u32[]{:S(2)}) %collective-permute-start.12) | collective-permute-done | bytes 262176 | tf_op jit(solution)/shard_map/ppermute | solution.py:26
  42.7 2.5 %collective-permute-done.11 = f32[128,512]{1,0:T(8,128)S(1)} collective-permute-done((f32[128,512]{1,0:T(8,128)S(1)}, f32[128,512]{1,0:T(8,128)S(1)}, u32[]{:S(2)}, u32[]{:S(2)}) %collective-permute-start.11) | collective-permute-done | bytes 262176 | tf_op jit(solution)/shard_map/ppermute | solution.py:26
  45.3 2.9 %collective-permute-start.18 = (f32[256,1024]{1,0:T(8,128)}, f32[256,1024]{1,0:T(8,128)S(1)}, u32[]{:S(2)}, u32[]{:S(2)}) collective-permute-start(f32[256,1024]{1,0:T(8,128)} %collective-permute-done.14), channel_id=1, source_target_pairs={{0,8},{2,10},{4,12},{6,14},{8,0},{10,2},{12,4},{14,6},{16,24},{18,... | collective-permute-start | bytes 3145736 | tf_op jit(solution)/shard_map/ppermute | solution.py:26
  48.3 2.3 %collective-permute-done.16 = f32[256,512]{1,0:T(8,128)S(1)} collective-permute-done((f32[256,512]{1,0:T(8,128)S(1)}, f32[256,512]{1,0:T(8,128)S(1)}, u32[]{:S(2)}, u32[]{:S(2)}) %collective-permute-start.16) | collective-permute-done | bytes 524320 | tf_op jit(solution)/shard_map/ppermute | solution.py:26
  50.8 1.4 %pad_maximum_fusion.1 = f32[512,1024]{1,0:T(8,128)S(1)} fusion(f32[256,1024]{1,0:T(8,128)} %collective-permute-done.14, f32[256,1024]{1,0:T(8,128)S(1)} %pad_maximum_fusion.3), kind=kLoop, calls=%fused_computation.7 | loop fusion | flops 524288 | bytes 4194304 | tf_op jit(solution)/shard_map/concatenate | solution.py:98
  52.3 4.3 %collective-permute-done.15 = f32[256,512]{1,0:T(8,128)S(1)} collective-permute-done((f32[256,512]{1,0:T(8,128)S(1)}, f32[256,512]{1,0:T(8,128)S(1)}, u32[]{:S(2)}, u32[]{:S(2)}) %collective-permute-start.15) | collective-permute-done | bytes 524320 | tf_op jit(solution)/shard_map/ppermute | solution.py:26
  59.1 3.5 %fusion = f32[512,1024]{1,0:T(8,128)S(1)} fusion(f32[1024,1024]{1,0:T(8,128)S(1)} %bitcast.48, f32[128,1024]{1,0:T(8,128)S(1)} %collective-permute-done.17, f32[128,1024]{1,0:T(8,128)S(1)} %pad_maximum_fusion.10, f32[256,1024]{1,0:T(8,128)S(1)} %maximum_maximum_fusion), kind=kOutput, calls=%fused_computation.1 | convolution fusion | flops 3222274048 | bytes 8388608 | tf_op jit(solution)/shard_map/vc,cn->vn/dot_general | solution.py:50
  62.6 2.0 %collective-permute-start.19 = (f32[512,1024]{1,0:T(8,128)S(1)}, f32[512,1024]{1,0:T(8,128)S(1)}, u32[]{:S(2)}, u32[]{:S(2)}) collective-permute-start(f32[512,1024]{1,0:T(8,128)S(1)} %fusion), channel_id=1, source_target_pairs={{0,8},{2,10},{4,12},{6,14},{8,0},{10,2},{12,4},{14,6},{16,24},{18,... | collective-permute-start | bytes 6291464 | tf_op jit(solution)/shard_map/ppermute | solution.py:26
  65.0 1.9 %fusion.17 = f32[512,1024]{1,0:T(8,128)S(1)} fusion(f32[512,1024]{1,0:T(8,128)S(1)} %fusion, f32[256,512]{1,0:T(8,128)S(1)} %bitcast.62, f32[256,512]{1,0:T(8,128)S(1)} %bitcast.60), kind=kOutput, calls=%fused_computation.26 | convolution fusion | flops 1610874880 | bytes 5242880 | tf_op jit(solution)/shard_map/vm,vn->mn/dot_general | solution.py:50
  67.0 1.9 %fusion.6 = f32[512,1024]{1,0:T(8,128)S(1)} fusion(f32[512,1024]{1,0:T(8,128)S(1)} %copy-done, f32[512,1024]{1,0:T(8,128)S(1)} %fusion.17, f32[256,512]{1,0:T(8,128)S(1)} %bitcast.63, f32[256,512]{1,0:T(8,128)S(1)} %bitcast.61), kind=kOutput, calls=%fused_computation.10 | convolution fusion | flops 1611399168 | bytes 7340032 | tf_op jit(solution)/shard_map/vm,mn->vn/dot_general | solution.py:50
  68.9 1.9 %convolution_multiply_fusion = f32[512,1024]{1,0:T(8,128)S(1)} fusion(f32[512,1024]{1,0:T(8,128)S(1)} %copy-done, f32[512,1024]{1,0:T(8,128)S(1)} %collective-permute-done.19, f32[256,512]{1,0:T(8,128)S(1)} %bitcast.56, f32[256,512]{1,0:T(8,128)S(1)} %bitcast.58), kind=kOutput, calls=%fused_computation.12 | convolution fusion | flops 1611399168 | bytes 7340032 | tf_op jit(solution)/shard_map/vm,vn->mn/dot_general | solution.py:50
  70.8 1.2 fusion.29
  72.1 1.2 fusion.30
  73.8 0.9 collective-permute-done.20
  74.7 2.0 %fusion.14 = f32[256,1024]{1,0:T(8,128)S(1)} fusion(f32[1024,1024]{1,0:T(8,128)S(1)} %bitcast.49, f32[256,1024]{1,0:T(8,128)S(1)} %collective-permute-done.20, f32[512,1024]{1,0:T(8,128)S(1)} %fusion.6), kind=kOutput, calls=%fused_computation.23 | convolution fusion | flops 1610874880 | bytes 7340032 | tf_op jit(solution)/shard_map/vn,cn->vc/dot_general | solution.py:50
  77.2 2.0 %fusion.11 = f32[256,1024]{1,0:T(8,128)S(1)} fusion(f32[1024,1024]{1,0:T(8,128)S(1)} %bitcast.50, f32[256,1024]{1,0:T(8,128)S(1)} %collective-permute-done.23, f32[512,1024]{1,0:T(8,128)S(1)} %fusion.6), kind=kOutput, calls=%fused_computation.20 | convolution fusion | flops 1610874880 | bytes 7340032 | tf_op jit(solution)/shard_map/vn,cn->vc/dot_general | solution.py:50
  79.4 6.1 %collective-permute-done.21 = f32[256,512]{1,0:T(8,128)S(1)} collective-permute-done((f32[256,512]{1,0:T(8,128)S(1)}, f32[256,512]{1,0:T(8,128)S(1)}, u32[]{:S(2)}, u32[]{:S(2)}) %collective-permute-start.21) | collective-permute-done | bytes 524320 | tf_op jit(solution)/shard_map/ppermute | solution.py:26
  85.8 2.0 %collective-permute-done.24 = f32[128,1024]{1,0:T(8,128)S(1)} collective-permute-done((f32[128,1024]{1,0:T(8,128)S(1)}, f32[128,1024]{1,0:T(8,128)S(1)}, u32[]{:S(2)}, u32[]{:S(2)}) %collective-permute-start.24) | collective-permute-done | bytes 524320 | tf_op jit(solution)/shard_map/ppermute | solution.py:26
  87.9 1.5 %collective-permute-start.25 = (f32[128,512]{1,0:T(8,128)S(1)}, f32[128,512]{1,0:T(8,128)S(1)}, u32[]{:S(2)}, u32[]{:S(2)}) collective-permute-start(f32[128,512]{1,0:T(8,128)S(1)} %pad_maximum_fusion.16), channel_id=1, source_target_pairs={{0,96},{2,98},{4,100},{6,102},{8,40},{10,42},{12,44},{14,46},{16,1... | collective-permute-start | bytes 786440 | tf_op jit(solution)/shard_map/ppermute | solution.py:26
  89.4 1.6 %collective-permute-done.22 = f32[128,512]{1,0:T(8,128)S(1)} collective-permute-done((f32[128,512]{1,0:T(8,128)S(1)}, f32[128,512]{1,0:T(8,128)S(1)}, u32[]{:S(2)}, u32[]{:S(2)}) %collective-permute-start.22) | collective-permute-done | bytes 262176 | tf_op jit(solution)/shard_map/ppermute | solution.py:26
  91.0 2.4 %collective-permute-done.25 = f32[128,512]{1,0:T(8,128)S(1)} collective-permute-done((f32[128,512]{1,0:T(8,128)S(1)}, f32[128,512]{1,0:T(8,128)S(1)}, u32[]{:S(2)}, u32[]{:S(2)}) %collective-permute-start.25) | collective-permute-done | bytes 262176 | tf_op jit(solution)/shard_map/ppermute | solution.py:26
  93.6 2.9 %collective-permute-start.26 = (f32[128,512]{1,0:T(8,128)S(1)}, f32[128,512]{1,0:T(8,128)S(1)}, u32[]{:S(2)}, u32[]{:S(2)}) collective-permute-start(f32[128,512]{1,0:T(8,128)S(1)} %pad_maximum_fusion.17), channel_id=1, source_target_pairs={{0,2},{2,0},{4,6},{6,4},{8,14},{10,12},{12,10},{14,8},{16,18},{18,... | collective-permute-start | bytes 786440 | tf_op jit(solution)/shard_map/ppermute | solution.py:26
  96.5 3.8 %collective-permute-done.26 = f32[128,512]{1,0:T(8,128)S(1)} collective-permute-done((f32[128,512]{1,0:T(8,128)S(1)}, f32[128,512]{1,0:T(8,128)S(1)}, u32[]{:S(2)}, u32[]{:S(2)}) %collective-permute-start.26) | collective-permute-done | bytes 262176 | tf_op jit(solution)/shard_map/ppermute | solution.py:26
  100.9 4.5 %collective-permute-done.27 = f32[128,256]{1,0:T(8,128)S(1)} collective-permute-done((f32[128,256]{1,0:T(8,128)S(1)}, f32[128,256]{1,0:T(8,128)S(1)}, u32[]{:S(2)}, u32[]{:S(2)}) %collective-permute-start.27) | collective-permute-done | bytes 131104 | tf_op jit(solution)/shard_map/ppermute | solution.py:26
  105.5 2.2 %collective-permute-start.28 = (f32[64,256]{1,0:T(8,128)S(1)}, f32[64,256]{1,0:T(8,128)S(1)}, u32[]{:S(2)}, u32[]{:S(2)}) collective-permute-start(f32[64,256]{1,0:T(8,128)S(1)} %pad_maximum_fusion.23), channel_id=1, source_target_pairs={{0,1},{2,3},{4,5},{6,7},{8,9},{10,11},{12,13},{14,15},{16,17},{18,... | collective-permute-start | bytes 196616 | tf_op jit(solution)/shard_map/ppermute | solution.py:26
  107.6 2.5 %collective-permute-done.28 = f32[64,256]{1,0:T(8,128)S(1)} collective-permute-done((f32[64,256]{1,0:T(8,128)S(1)}, f32[64,256]{1,0:T(8,128)S(1)}, u32[]{:S(2)}, u32[]{:S(2)}) %collective-permute-start.28) | collective-permute-done | bytes 65568 | tf_op jit(solution)/shard_map/ppermute | solution.py:26
  110.2 1.4 %collective-permute-start.29 = (f32[64,128]{1,0:T(8,128)S(1)}, f32[64,128]{1,0:T(8,128)S(1)}, u32[]{:S(2)}, u32[]{:S(2)}) collective-permute-start(f32[64,128]{1,0:T(8,128)S(1)} %slice.213), channel_id=1, source_target_pairs={{0,16},{2,18},{4,20},{6,22},{8,24},{10,26},{12,28},{14,30},{16,0},... | collective-permute-start | bytes 98312 | tf_op jit(solution)/shard_map/ppermute | solution.py:26
  111.7 1.4 %collective-permute-done.29 = f32[64,128]{1,0:T(8,128)S(1)} collective-permute-done((f32[64,128]{1,0:T(8,128)S(1)}, f32[64,128]{1,0:T(8,128)S(1)}, u32[]{:S(2)}, u32[]{:S(2)}) %collective-permute-start.29) | collective-permute-done | bytes 32800 | tf_op jit(solution)/shard_map/ppermute | solution.py:26
  113.1 7.4 %collective-permute-start.30 = (f32[64,64]{1,0:T(8,128)S(1)}, f32[64,64]{1,0:T(8,128)S(1)}, u32[]{:S(2)}, u32[]{:S(2)}) collective-permute-start(f32[64,64]{1,0:T(8,128)S(1)} %slice.215), channel_id=1, source_target_pairs={{0,8},{2,10},{4,12},{6,14},{8,0},{10,2},{12,4},{14,6},{16,24},{18,... | collective-permute-start | bytes 49160 | tf_op jit(solution)/shard_map/ppermute | solution.py:26
  (80 shorter events, 10.9 us)
Async XLA Ops:
  0.8 2.3 %collective-permute-start = (f32[64,64]{1,0:T(8,128)S(1)}, f32[64,64]{1,0:T(8,128)S(1)}, u32[]{:S(2)}, u32[]{:S(2)}) collective-permute-start(f32[64,64]{1,0:T(8,128)S(1)} %get-tuple-element.86), channel_id=1, source_target_pairs={{0,8},{2,10},{4,12},{6,14},{8,0},{10,2},{12,4},{14,6},{16,24},{18,... | collective-permute-start | bytes 49160 | tf_op jit(solution)/shard_map/ppermute | solution.py:26
  3.1 7.8 %collective-permute-start.1 = (f32[2,32,128]{2,1,0:T(8,128)S(1)}, f32[2,32,128]{2,1,0:T(8,128)S(1)}, u32[]{:S(2)}, u32[]{:S(2)}) collective-permute-start(f32[2,32,128]{2,1,0:T(8,128)S(1)} %pad_maximum_fusion.25), channel_id=1, source_target_pairs={{0,32},{2,34},{4,36},{6,38},{8,104},{10,106},{12,108},{14,110},{16... | collective-permute-start | bytes 98312 | tf_op jit(solution)/shard_map/ppermute | solution.py:26
  7.0 5.3 %collective-permute-start.2 = (f32[64,512]{1,0:T(8,128)}, f32[64,512]{1,0:T(8,128)S(1)}, u32[]{:S(2)}, u32[]{:S(2)}) collective-permute-start(f32[64,512]{1,0:T(8,128)} %param.5), channel_id=1, source_target_pairs={{0,2},{2,0},{4,6},{6,4},{8,14},{10,12},{12,10},{14,8},{16,18},{18,... | collective-permute-start | bytes 393224 | tf_op jit(solution)/shard_map/ppermute | solution.py:26
  9.7 7.0 %collective-permute-start.4 = (f32[64,1024]{1,0:T(8,128)}, f32[64,1024]{1,0:T(8,128)S(1)}, u32[]{:S(2)}, u32[]{:S(2)}) collective-permute-start(f32[64,1024]{1,0:T(8,128)} %param.6), channel_id=1, source_target_pairs={{0,16},{2,18},{4,20},{6,22},{8,24},{10,26},{12,28},{14,30},{16,0},... | collective-permute-start | bytes 786440 | tf_op jit(solution)/shard_map/ppermute | solution.py:26
  13.2 3.5 %collective-permute-start.3 = (f32[2,32,256]{2,1,0:T(8,128)S(1)}, f32[2,32,256]{2,1,0:T(8,128)S(1)}, u32[]{:S(2)}, u32[]{:S(2)}) collective-permute-start(f32[2,32,256]{2,1,0:T(8,128)S(1)} %pad_maximum_fusion.22), channel_id=1, source_target_pairs={{0,96},{2,98},{4,100},{6,102},{8,40},{10,42},{12,44},{14,46},{16,1... | collective-permute-start | bytes 196616 | tf_op jit(solution)/shard_map/ppermute | solution.py:26
  13.3 10.6 %collective-permute-start.7 = (f32[128,512]{1,0:T(8,128)S(1)}, f32[128,512]{1,0:T(8,128)S(1)}, u32[]{:S(2)}, u32[]{:S(2)}) collective-permute-start(f32[128,512]{1,0:T(8,128)S(1)} %pad_maximum_fusion.13), channel_id=1, source_target_pairs={{0,1},{2,3},{4,5},{6,7},{8,9},{10,11},{12,13},{14,15},{16,17},{18,... | collective-permute-start | bytes 786440 | tf_op jit(solution)/shard_map/ppermute | solution.py:26
  17.7 9.3 %collective-permute-start.8 = (f32[128,1024]{1,0:T(8,128)S(1)}, f32[128,1024]{1,0:T(8,128)S(1)}, u32[]{:S(2)}, u32[]{:S(2)}) collective-permute-start(f32[128,1024]{1,0:T(8,128)S(1)} %pad_maximum_fusion.8), channel_id=1, source_target_pairs={{0,32},{2,34},{4,36},{6,38},{8,104},{10,106},{12,108},{14,110},{16... | collective-permute-start | bytes 1572872 | tf_op jit(solution)/shard_map/ppermute | solution.py:26
  19.4 4.5 %collective-permute-start.5 = (f32[32,512]{1,0:T(8,128)S(1)}, f32[32,512]{1,0:T(8,128)S(1)}, u32[]{:S(2)}, u32[]{:S(2)}) collective-permute-start(f32[32,512]{1,0:T(8,128)S(1)} %get-tuple-element.82), channel_id=1, source_target_pairs={{0,2},{2,0},{4,6},{6,4},{8,14},{10,12},{12,10},{14,8},{16,18},{18,... | collective-permute-start | bytes 196616 | tf_op jit(solution)/shard_map/ppermute | solution.py:26
  20.6 6.6 %collective-permute-start.6 = (f32[32,512]{1,0:T(8,128)S(1)}, f32[32,512]{1,0:T(8,128)S(1)}, u32[]{:S(2)}, u32[]{:S(2)}) collective-permute-start(f32[32,512]{1,0:T(8,128)S(1)} %get-tuple-element.30), channel_id=1, source_target_pairs={{0,16},{2,18},{4,20},{6,22},{8,25},{10,27},{12,29},{14,31},{16,0},... | collective-permute-start | bytes 196616 | tf_op jit(solution)/shard_map/ppermute | solution.py:26
  27.2 18.1 %collective-permute-start.14 = (f32[256,1024]{1,0:T(8,128)S(1)}, f32[256,1024]{1,0:T(8,128)}, u32[]{:S(2)}, u32[]{:S(2)}) collective-permute-start(f32[256,1024]{1,0:T(8,128)S(1)} %pad_maximum_fusion.3), channel_id=1, source_target_pairs={{0,96},{2,98},{4,100},{6,102},{8,40},{10,42},{12,44},{14,46},{16,1... | collective-permute-start | bytes 3145736 | tf_op jit(solution)/shard_map/ppermute | solution.py:26
  27.3 18.0 %collective-permute-start.13 = (f32[256,1024]{1,0:T(8,128)S(1)}, f32[256,1024]{1,0:T(8,128)S(1)}, u32[]{:S(2)}, u32[]{:S(2)}) collective-permute-start(f32[256,1024]{1,0:T(8,128)S(1)} %pad_maximum_fusion.3), channel_id=1, source_target_pairs={{0,8},{2,10},{4,12},{6,14},{8,0},{10,2},{12,4},{14,6},{16,24},{18,... | collective-permute-start | bytes 3145736 | tf_op jit(solution)/shard_map/ppermute | solution.py:26
  30.2 4.3 %collective-permute-start.10 = (f32[64,512]{1,0:T(8,128)S(1)}, f32[64,512]{1,0:T(8,128)S(1)}, u32[]{:S(2)}, u32[]{:S(2)}) collective-permute-start(f32[64,512]{1,0:T(8,128)S(1)} %pad_maximum_fusion.20), channel_id=1, source_target_pairs={{0,17},{2,19},{4,21},{6,23},{8,24},{10,26},{12,28},{14,30},{16,1},... | collective-permute-start | bytes 393224 | tf_op jit(solution)/shard_map/ppermute | solution.py:26
  31.5 4.2 %collective-permute-start.9 = (f32[64,512]{1,0:T(8,128)S(1)}, f32[64,512]{1,0:T(8,128)S(1)}, u32[]{:S(2)}, u32[]{:S(2)}) collective-permute-start(f32[64,512]{1,0:T(8,128)S(1)} %pad_maximum_fusion.19), channel_id=1, source_target_pairs={{0,6},{2,4},{4,2},{6,0},{8,10},{10,8},{12,14},{14,12},{16,22},{18,... | collective-permute-start | bytes 393224 | tf_op jit(solution)/shard_map/ppermute | solution.py:26
  35.7 7.0 %collective-permute-start.12 = (f32[64,1024]{1,0:T(8,128)S(1)}, f32[64,1024]{1,0:T(8,128)S(1)}, u32[]{:S(2)}, u32[]{:S(2)}) collective-permute-start(f32[64,1024]{1,0:T(8,128)S(1)} %maximum_maximum_fusion.1), channel_id=1, source_target_pairs={{0,2},{2,0},{4,6},{6,4},{8,14},{10,12},{12,10},{14,8},{16,18},{18,... | collective-permute-start | bytes 786440 | tf_op jit(solution)/shard_map/ppermute | solution.py:26
  38.5 6.7 %collective-permute-start.11 = (f32[128,512]{1,0:T(8,128)S(1)}, f32[128,512]{1,0:T(8,128)S(1)}, u32[]{:S(2)}, u32[]{:S(2)}) collective-permute-start(f32[128,512]{1,0:T(8,128)S(1)} %pad_maximum_fusion.14), channel_id=1, source_target_pairs={{0,16},{2,18},{4,20},{6,22},{8,25},{10,27},{12,29},{14,31},{16,0},... | collective-permute-start | bytes 786440 | tf_op jit(solution)/shard_map/ppermute | solution.py:26
  40.4 10.3 %collective-permute-start.16 = (f32[256,512]{1,0:T(8,128)S(1)}, f32[256,512]{1,0:T(8,128)S(1)}, u32[]{:S(2)}, u32[]{:S(2)}) collective-permute-start(f32[256,512]{1,0:T(8,128)S(1)} %pad_maximum_fusion.9), channel_id=1, source_target_pairs={{0,6},{2,4},{4,2},{6,0},{8,10},{10,8},{12,14},{14,12},{16,22},{18,... | collective-permute-start | bytes 1572872 | tf_op jit(solution)/shard_map/ppermute | solution.py:26
  45.3 11.5 %collective-permute-start.18 = (f32[256,1024]{1,0:T(8,128)}, f32[256,1024]{1,0:T(8,128)S(1)}, u32[]{:S(2)}, u32[]{:S(2)}) collective-permute-start(f32[256,1024]{1,0:T(8,128)} %collective-permute-done.14), channel_id=1, source_target_pairs={{0,8},{2,10},{4,12},{6,14},{8,0},{10,2},{12,4},{14,6},{16,24},{18,... | collective-permute-start | bytes 3145736 | tf_op jit(solution)/shard_map/ppermute | solution.py:26
  48.2 8.4 %collective-permute-start.15 = (f32[256,512]{1,0:T(8,128)S(1)}, f32[256,512]{1,0:T(8,128)S(1)}, u32[]{:S(2)}, u32[]{:S(2)}) collective-permute-start(f32[256,512]{1,0:T(8,128)S(1)} %pad_maximum_fusion.11), channel_id=1, source_target_pairs={{0,17},{2,19},{4,21},{6,23},{8,24},{10,26},{12,28},{14,30},{16,1},... | collective-permute-start | bytes 1572872 | tf_op jit(solution)/shard_map/ppermute | solution.py:26
  50.7 8.4 %collective-permute-start.17 = (f32[128,1024]{1,0:T(8,128)S(1)}, f32[128,1024]{1,0:T(8,128)S(1)}, u32[]{:S(2)}, u32[]{:S(2)}) collective-permute-start(f32[128,1024]{1,0:T(8,128)S(1)} %pad_maximum_fusion.10), channel_id=1, source_target_pairs={{0,6},{2,4},{4,2},{6,0},{8,10},{10,8},{12,14},{14,12},{16,22},{18,... | collective-permute-start | bytes 1572872 | tf_op jit(solution)/shard_map/ppermute | solution.py:26
  62.6 6.2 %collective-permute-start.19 = (f32[512,1024]{1,0:T(8,128)S(1)}, f32[512,1024]{1,0:T(8,128)S(1)}, u32[]{:S(2)}, u32[]{:S(2)}) collective-permute-start(f32[512,1024]{1,0:T(8,128)S(1)} %fusion), channel_id=1, source_target_pairs={{0,8},{2,10},{4,12},{6,14},{8,0},{10,2},{12,4},{14,6},{16,24},{18,... | collective-permute-start | bytes 6291464 | tf_op jit(solution)/shard_map/ppermute | solution.py:26
  65.0 1.9 %copy-start = (f32[512,1024]{1,0:T(8,128)S(1)}, f32[512,1024]{1,0:T(8,128)}, u32[]{:S(2)}) copy-start(f32[512,1024]{1,0:T(8,128)} %param.7) | copy-start | bytes 6291460
  72.0 2.7 %collective-permute-start.20 = (f32[256,1024]{1,0:T(8,128)S(1)}, f32[256,1024]{1,0:T(8,128)S(1)}, u32[]{:S(2)}, u32[]{:S(2)}) collective-permute-start(f32[256,1024]{1,0:T(8,128)S(1)} %fusion.29), channel_id=1, source_target_pairs={{0,8},{2,10},{4,12},{6,14},{8,0},{10,2},{12,4},{14,6},{16,24},{18,... | collective-permute-start | bytes 3145736 | tf_op jit(solution)/shard_map/ppermute | solution.py:26
  73.3 4.0 %collective-permute-start.23 = (f32[256,1024]{1,0:T(8,128)S(1)}, f32[256,1024]{1,0:T(8,128)S(1)}, u32[]{:S(2)}, u32[]{:S(2)}) collective-permute-start(f32[256,1024]{1,0:T(8,128)S(1)} %fusion.30), channel_id=1, source_target_pairs={{0,8},{2,10},{4,12},{6,14},{8,0},{10,2},{12,4},{14,6},{16,24},{18,... | collective-permute-start | bytes 3145736 | tf_op jit(solution)/shard_map/ppermute | solution.py:26
  76.9 8.6 %collective-permute-start.21 = (f32[256,512]{1,0:T(8,128)S(1)}, f32[256,512]{1,0:T(8,128)S(1)}, u32[]{:S(2)}, u32[]{:S(2)}) collective-permute-start(f32[256,512]{1,0:T(8,128)S(1)} %pad_maximum_fusion.12), channel_id=1, source_target_pairs={{0,96},{2,98},{4,100},{6,102},{8,40},{10,42},{12,44},{14,46},{16,1... | collective-permute-start | bytes 1572872 | tf_op jit(solution)/shard_map/ppermute | solution.py:26
  79.3 8.4 %collective-permute-start.24 = (f32[128,1024]{1,0:T(8,128)S(1)}, f32[128,1024]{1,0:T(8,128)S(1)}, u32[]{:S(2)}, u32[]{:S(2)}) collective-permute-start(f32[128,1024]{1,0:T(8,128)S(1)} %slice.195), channel_id=1, source_target_pairs={{0,6},{2,4},{4,2},{6,0},{8,10},{10,8},{12,14},{14,12},{16,22},{18,... | collective-permute-start | bytes 1572872 | tf_op jit(solution)/shard_map/ppermute | solution.py:26
  85.7 5.3 %collective-permute-start.22 = (f32[128,512]{1,0:T(8,128)S(1)}, f32[128,512]{1,0:T(8,128)S(1)}, u32[]{:S(2)}, u32[]{:S(2)}) collective-permute-start(f32[128,512]{1,0:T(8,128)S(1)} %pad_maximum_fusion.15), channel_id=1, source_target_pairs={{0,6},{2,4},{4,2},{6,0},{8,10},{10,8},{12,14},{14,12},{16,22},{18,... | collective-permute-start | bytes 786440 | tf_op jit(solution)/shard_map/ppermute | solution.py:26
  87.9 5.6 %collective-permute-start.25 = (f32[128,512]{1,0:T(8,128)S(1)}, f32[128,512]{1,0:T(8,128)S(1)}, u32[]{:S(2)}, u32[]{:S(2)}) collective-permute-start(f32[128,512]{1,0:T(8,128)S(1)} %pad_maximum_fusion.16), channel_id=1, source_target_pairs={{0,96},{2,98},{4,100},{6,102},{8,40},{10,42},{12,44},{14,46},{16,1... | collective-permute-start | bytes 786440 | tf_op jit(solution)/shard_map/ppermute | solution.py:26
  93.6 6.7 %collective-permute-start.26 = (f32[128,512]{1,0:T(8,128)S(1)}, f32[128,512]{1,0:T(8,128)S(1)}, u32[]{:S(2)}, u32[]{:S(2)}) collective-permute-start(f32[128,512]{1,0:T(8,128)S(1)} %pad_maximum_fusion.17), channel_id=1, source_target_pairs={{0,2},{2,0},{4,6},{6,4},{8,14},{10,12},{12,10},{14,8},{16,18},{18,... | collective-permute-start | bytes 786440 | tf_op jit(solution)/shard_map/ppermute | solution.py:26
  100.3 5.1 %collective-permute-start.27 = (f32[128,256]{1,0:T(8,128)S(1)}, f32[128,256]{1,0:T(8,128)S(1)}, u32[]{:S(2)}, u32[]{:S(2)}) collective-permute-start(f32[128,256]{1,0:T(8,128)S(1)} %pad_maximum_fusion.21), channel_id=1, source_target_pairs={{0,32},{2,34},{4,36},{6,38},{8,104},{10,106},{12,108},{14,110},{16... | collective-permute-start | bytes 393224 | tf_op jit(solution)/shard_map/ppermute | solution.py:26
  105.5 4.7 %collective-permute-start.28 = (f32[64,256]{1,0:T(8,128)S(1)}, f32[64,256]{1,0:T(8,128)S(1)}, u32[]{:S(2)}, u32[]{:S(2)}) collective-permute-start(f32[64,256]{1,0:T(8,128)S(1)} %pad_maximum_fusion.23), channel_id=1, source_target_pairs={{0,1},{2,3},{4,5},{6,7},{8,9},{10,11},{12,13},{14,15},{16,17},{18,... | collective-permute-start | bytes 196616 | tf_op jit(solution)/shard_map/ppermute | solution.py:26
  110.2 2.8 %collective-permute-start.29 = (f32[64,128]{1,0:T(8,128)S(1)}, f32[64,128]{1,0:T(8,128)S(1)}, u32[]{:S(2)}, u32[]{:S(2)}) collective-permute-start(f32[64,128]{1,0:T(8,128)S(1)} %slice.213), channel_id=1, source_target_pairs={{0,16},{2,18},{4,20},{6,22},{8,24},{10,26},{12,28},{14,30},{16,0},... | collective-permute-start | bytes 98312 | tf_op jit(solution)/shard_map/ppermute | solution.py:26
  113.1 8.3 %collective-permute-start.30 = (f32[64,64]{1,0:T(8,128)S(1)}, f32[64,64]{1,0:T(8,128)S(1)}, u32[]{:S(2)}, u32[]{:S(2)}) collective-permute-start(f32[64,64]{1,0:T(8,128)S(1)} %slice.215), channel_id=1, source_target_pairs={{0,8},{2,10},{4,12},{6,14},{8,0},{10,2},{12,4},{14,6},{16,24},{18,... | collective-permute-start | bytes 49160 | tf_op jit(solution)/shard_map/ppermute | solution.py:26
